TPU v7x, 512 devices: a whole 4x4x16 slice. The times are simulated.
512 devices in a mesh: dp: 16 (over y, z_hi, core), frame: 32 (over z_lo, x).
Axes of the slice: x: 4, y: 4, z: 16 (z_hi: 2, z_lo: 8; z = z_hi * 8 + z_lo), core: 2. Of those that a mesh axis runs over, the one named last changes fastest.
Arguments:
- video: bfloat16 [16, 32, 24, 64, 320], P('dp', 'frame'), may hold values from -18 to 18
- frame_emb: float32 [16, 32, 320], P('dp', 'frame'), may hold values from -12 to 12
- norm1_gain: float32 [320], replicated, may hold values from 0.1 to 1.9
- norm1_shift: float32 [320], replicated, may hold values from -3 to 3
- norm2_gain: float32 [320], replicated, may hold values from 0.1 to 1.9
- norm2_shift: float32 [320], replicated, may hold values from -3 to 3
- spatial_weight: bfloat16 [3, 960, 320], P(None, 'frame', 'dp'), may hold values from -0.109375 to 0.109375
- temporal_weight: bfloat16 [3, 320, 320], P(None, 'frame', 'dp'), may hold values from -0.1875 to 0.1875
- temporal_bias: float32 [320], replicated, may hold values from -3 to 3
Outputs:
- block_out: bfloat16 [16, 32, 24, 64, 320], P('dp', 'frame')
All inputs are finite; a program needn't handle non-finite values.
Results may differ from a plain program's by a relative error of at most 0.0055.
Values may be sent and summed in bfloat16 or wider, within the bound.
No kernel may reach another device: no remote copies, remote signals or barrier semaphores. Data moves between devices by JAX's collectives and lax.ppermute only.
A program may use at most 64 MiB of HBM per device.

v0:
```python
import jax
import jax.numpy as jnp
from jax import lax
from jax.sharding import PartitionSpec as P

GROUPS = 32


epsilon = 1e-05


def spatial_conv(activated, spatial_weight):
    frames, height, breadth, channels = activated.shape
    padded = jnp.pad(activated, ((0, 0), (1, 1), (1, 1), (0, 0)))
    summed = jnp.zeros((frames * height * breadth, channels), jnp.float32)
    for row_tap in range(3):
        columns = jnp.concatenate(
            [
                padded[:, row_tap : row_tap + height, col_tap : col_tap + breadth, :]
                for col_tap in range(3)
            ],
            axis=-1,
        )
        summed = summed + jnp.dot(
            columns.reshape(-1, 3 * channels),
            spatial_weight[row_tap],
            preferred_element_type=jnp.float32,
        )
    return summed


def body(
    video,
    frame_emb,
    norm1_gain,
    norm1_shift,
    norm2_gain,
    norm2_shift,
    spatial_weight,
    temporal_weight,
    temporal_bias,
):
    spatial_rows, temporal_rows = (
        lax.all_gather(spatial_weight, "frame", axis=1, tiled=True),
        lax.all_gather(temporal_weight, "frame", axis=1, tiled=True),
    )
    spatial_full, temporal_full = (
        lax.all_gather(spatial_rows, "dp", axis=2, tiled=True),
        lax.all_gather(temporal_rows, "dp", axis=2, tiled=True),
    )
    one_frame = video[0]
    height, breadth, channels = (video.shape[2], video.shape[3], video.shape[4])
    group_width = channels // GROUPS
    flattened = one_frame.astype(jnp.float32).reshape(height * breadth, GROUPS, group_width)
    average = jnp.mean(flattened, axis=(0, 2))
    variance = jnp.mean(flattened * flattened, axis=(0, 2)) - average * average
    normed = (flattened - average[None, :, None]) * lax.rsqrt(variance + epsilon)[None, :, None]
    normed = normed.reshape(1, height, breadth, channels) * norm1_gain + norm1_shift
    activated = jax.nn.silu(normed).astype(jnp.bfloat16)
    hidden = (spatial_conv(activated, spatial_full) + frame_emb[0]).astype(jnp.bfloat16)
    grouped = hidden.astype(jnp.float32).reshape(-1, GROUPS, group_width)
    moments, squares = lax.psum(
        (jnp.sum(grouped, axis=(0, 2)), jnp.sum(grouped * grouped, axis=(0, 2))), "frame"
    )
    entries = grouped.shape[0] * group_width * lax.axis_size("frame")
    average2 = moments / entries
    variance2 = squares / entries - average2 * average2
    normed2 = (grouped - average2[None, :, None]) * lax.rsqrt(variance2 + epsilon)[None, :, None]
    normed2 = normed2.reshape(-1, channels) * norm2_gain + norm2_shift
    mixed = jax.nn.silu(normed2).astype(jnp.bfloat16)
    pixels_view = lax.all_to_all(mixed[None], "frame", split_axis=1, concat_axis=0, tiled=True)
    frames = pixels_view.shape[0]
    padded = jnp.pad(pixels_view, ((1, 1), (0, 0), (0, 0)))
    temporal_sum = jnp.zeros((pixels_view.shape[0] * pixels_view.shape[1], channels), jnp.float32)
    for offset in range(3):
        temporal_sum = temporal_sum + jnp.dot(
            padded[offset : offset + frames].reshape(-1, channels),
            temporal_full[offset],
            preferred_element_type=jnp.float32,
        )
    temporal_out = (temporal_sum + temporal_bias).astype(jnp.bfloat16).reshape(frames, -1, channels)
    temporal_out = lax.all_to_all(temporal_out, "frame", split_axis=0, concat_axis=1, tiled=True)[0]
    result = hidden.astype(jnp.float32) + temporal_out.astype(jnp.float32)
    return result.astype(jnp.bfloat16).reshape(video.shape)


def solution(mesh):
    placed = (
        P("dp", "frame", None, None, None),
        P("dp", "frame", None),
        P(),
        P(),
        P(),
        P(),
        P(None, "frame", "dp"),
        P(None, "frame", "dp"),
        P(),
    )
    return jax.shard_map(
        body,
        mesh=mesh,
        in_specs=placed,
        out_specs=P("dp", "frame", None, None, None),
        check_vma=False,
    )
```

profile of v0, /device:TPU:1, one launch (start us, length us, event | category | flops | bytes accessed | tf_op | source)
XLA Modules:
  0.0 647.4 jit_solution(13995003885625676265)
XLA Ops:
  7.5 116.9 %all_gather.12 = bf16[3,960,20]{2,0,1:T(4,128)(2,1)S(1)} all-gather(bf16[3,30,20]{2,0,1:T(4,128)(2,1)S(1)} %copy.35), channel_id=1, replica_groups=mesh['dp'=16,'frame'=32] {'frame'}, dimensions={1}, use_global_device_ids=true | all-gather | bytes 118800 | tf_op jit(solution)/shard_map/all_gather | solution.py:44
  124.4 1.7 copy.36
  128.2 5.1 pad_slice_fusion.4
  133.3 1.4 copy.39
  134.7 1.4 copy.40
  136.8 7.1 %pad_maximum_fusion = (bf16[1,24,64,960]{3,2,1,0:T(8,128)(2,1)}, bf16[1,24,64,960]{3,2,1,0:T(8,128)(2,1)}) fusion(bf16[1,24,64,320]{3,2,1,0:T(8,128)(2,1)} %get-tuple-element.18, bf16[1,24,64,320]{3,2,1,0:T(8,128)(2,1)} %get-tuple-element.17, bf16[1,24,64,320]{3,2,1,0:T(8,128)(2,1)} %get-tuple-element.23, bf16[1,24,64,320]{3,2,1,0:T(8,128)(2,1)} %get-tuple-element.22, ...), kind=kLoop, calls=%fused_computation.4 | loop fusion | flops 17694720 | bytes 11796480 | tf_op jit(solution)/shard_map/concatenate | solution.py:17
  143.9 1.8 multiply_convert_fusion.1
  145.6 88.7 %all-gather.2.cloned.1.call-done = bf16[3,960,320]{1,0,2:T(4,128)(2,1)} async-done(((bf16[3,960,20]{1,0,2:T(4,128)(2,1)}), bf16[3,960,320]{1,0,2:T(4,128)(2,1)}) %all-gather.2.cloned.1.call-update) | async-done | bytes 1843216 | tf_op jit(solution)/shard_map/all_gather | solution.py:48
  234.4 7.3 %fusion.45 = (bf16[1,960,320]{1,0,2:T(2,128)(2,1)S(1)}, bf16[1,960,320]{1,0,2:T(2,128)(2,1)S(1)}, bf16[1,960,320]{1,0,2:T(2,128)(2,1)S(1)}) fusion(bf16[3,960,320]{1,0,2:T(4,128)(2,1)} %all-gather.2.cloned.1.call-done), kind=kLoop, calls=%fused_computation.67 | loop fusion | bytes 3686400 | tf_op jit(solution)/shard_map/slice | solution.py:26
  245.4 1.4 convert_reduce_fusion
  247.3 100.4 %all-reduce.2 = (f32[32]{0:T(128)S(1)}, f32[32]{0:T(128)S(1)}) all-reduce(f32[32]{0:T(128)S(1)} %reduce_sum.75, f32[32]{0:T(128)S(1)} %reduce_sum.72), channel_id=1, replica_groups=mesh['dp'=16,'frame'=32] {'frame'}, use_global_device_ids=true, to_apply=%region_9.10 | all-reduce | flops 64 | bytes 512 | tf_op jit(solution)/shard_map/psum | solution.py:62
  349.0 3.5 copy.43
  353.0 8.3 %reduce.9 = bf16[1536,320]{1,0:T(8,128)(2,1)S(1)} reduce(bf16[1536,1,320]{2,1,0:T(2,128)(2,1)S(1)} %bitcast.58, bf16[]{:T(256)} %broadcast.119), dimensions={1}, to_apply=%bitcast.47.reduce_sub_computation | reduce | bytes 1966082
  361.3 2.0 reshape.142
  363.4 3.9 all-to-all-start
  367.3 109.9 %all_gather.14 = bf16[3,320,20]{2,0,1:T(4,128)(2,1)S(1)} all-gather(bf16[3,10,20]{2,0,1:T(4,128)(2,1)S(1)} %copy-done.12), channel_id=1, replica_groups=mesh['dp'=16,'frame'=32] {'frame'}, dimensions={1}, use_global_device_ids=true | all-gather | bytes 39600 | tf_op jit(solution)/shard_map/all_gather | solution.py:45
  477.5 80.2 %all_gather.15 = bf16[3,320,320]{1,0,2:T(4,128)(2,1)S(1)} all-gather(bf16[3,320,20]{1,0,2:T(4,128)(2,1)S(1)} %copy.44), channel_id=1, replica_groups=mesh['dp'=16,'frame'=32] {'dp'}, dimensions={2}, use_global_device_ids=true | all-gather | bytes 652800 | tf_op jit(solution)/shard_map/all_gather | solution.py:49
  558.7 1.4 copy.58
  562.8 2.0 reshape.143
  565.0 4.8 copy.46
  574.2 61.0 %all_to_all.21 = bf16[32,48,320]{2,1,0:T(8,128)(2,1)S(1)} all-to-all(bf16[32,48,320]{2,1,0:T(8,128)(2,1)S(1)} %bitcast.62), channel_id=1, replica_groups=mesh['dp'=16,'frame'=32] {'frame'}, dimensions={0} | all-to-all | bytes 1966080 | tf_op jit(solution)/shard_map/all_to_all | solution.py:82
  635.5 1.9 copy.50
  637.3 1.8 fusion.34
  639.1 1.4 copy.51
  (79 shorter events, 18.4 us)
Async XLA Ops:
  6.5 119.5 %copy-start = (bf16[1,1,24,64,320]{4,3,2,1,0:T(8,128)(2,1)S(1)}, bf16[1,1,24,64,320]{4,3,2,1,0:T(8,128)(2,1)}, u32[]{:S(2)}) copy-start(bf16[1,1,24,64,320]{4,3,2,1,0:T(8,128)(2,1)} %param.9) | copy-start | bytes 2949124
  6.5 120.8 %copy-start.14 = (f32[320]{0:T(512)S(1)}, f32[320]{0:T(512)}, u32[]{:S(2)}) copy-start(f32[320]{0:T(512)} %param.11) | copy-start | bytes 3844
  6.5 120.8 %copy-start.13 = (f32[320]{0:T(512)S(1)}, f32[320]{0:T(512)}, u32[]{:S(2)}) copy-start(f32[320]{0:T(512)} %param.12) | copy-start | bytes 3844
  6.5 227.8 %all-gather.2.cloned.1.call-start = ((), (), s32[]{:S(2)}) async-start(), calls=%async_computation.2 | async-start | bytes 2785280 | tf_op jit(solution)/shard_map/all_gather | solution.py:48
  136.1 0.7 copy-start.18
  145.6 96.1 %copy-start.5 = (bf16[1,24,64,960]{3,2,1,0:T(8,128)(2,1)S(1)}, bf16[1,24,64,960]{3,2,1,0:T(8,128)(2,1)}, u32[]{:S(2)}) copy-start(bf16[1,24,64,960]{3,2,1,0:T(8,128)(2,1)} %get-tuple-element.33) | copy-start | bytes 8847364
  241.7 1.9 copy-start.4
  243.6 1.2 copy-start.6
  243.6 1.5 copy-start.7
  243.6 1.8 copy-start.8
  245.4 102.6 %copy-start.16 = (f32[320]{0:T(512)S(1)}, f32[320]{0:T(512)}, u32[]{:S(2)}) copy-start(f32[320]{0:T(512)} %param.14) | copy-start | bytes 3844
  245.4 102.6 %copy-start.17 = (f32[320]{0:T(512)S(1)}, f32[320]{0:T(512)}, u32[]{:S(2)}) copy-start(f32[320]{0:T(512)} %param.13) | copy-start | bytes 3844
  246.8 101.2 %copy-start.2 = (bf16[1536,320]{0,1:T(8,128)(2,1)}, bf16[1536,320]{0,1:T(8,128)(2,1)S(1)}, u32[]{:S(2)}) copy-start(bf16[1536,320]{0,1:T(8,128)(2,1)S(1)} %get-tuple-element.31) | copy-start | bytes 2949124
  361.3 6.0 copy-start.12
  363.4 199.4 %all-to-all-start = ((bf16[32,2,7680]{2,1,0:T(2,128)(2,1)}), bf16[32,2,7680]{2,1,0:T(2,128)(2,1)S(1)}, u32[]{:S(2)}, u32[]{:S(2)}) async-start(bf16[32,2,7680]{2,1,0:T(2,128)(2,1)} %reshape.142), calls=%async_computation | async-start | bytes 1966080 | tf_op jit(solution)/shard_map/all_to_all | solution.py:71
  569.8 0.9 copy-start.11
  570.0 1.5 copy-start.9
  571.5 1.2 copy-start.1
  571.5 1.2 copy-start.10
  571.5 1.2 copy-start.15
  635.5 1.9 copy-start.3
Sparse Core Ops, SparseCore 0:
  126.2 108.1 all-gather.1
where the time goes:
time: 648 us; the launch traced here: 647 us
  blocking collectives  468 us (72%)
  waiting for transfers between devices  88.8 us (14%)
  local copies, waits for them, and re-layouts  44.6 us (7%)
  other arithmetic  21.9 us (3%)
  between operations  13.7 us (2%)
    all_gather x1, blocking collectives, body(): lax.all_gather(spatial_weight, 'frame', axis=1, tiled=True)  117 us
    all_gather x1, blocking collectives, body(): lax.all_gather(temporal_weight, 'frame', axis=1, tiled=True)  110 us
    psum x1, blocking collectives, body(): lax.psum((jnp.sum(grouped, axis=(0, 2)), jnp.sum(grouped * grouped, axis=...  100 us
    all_gather x1, waiting for transfers between devices, body(): lax.all_gather(spatial_rows, 'dp', axis=2, tiled=True)  88.7 us
    all_gather x1, blocking collectives, body(): lax.all_gather(temporal_rows, 'dp', axis=2, tiled=True)  80.2 us
    all_to_all x1, blocking collectives, body(): lax.all_to_all(temporal_out, 'frame', split_axis=0, concat_axis=1, tiled=...  61 us
  transfers between devices with their start and end apart: 2, of which 1 were waited for; matrix products, arithmetic and copies ran while one was open for 4% of the time, Pallas kernels for 0%

commit v1 on v0

v1 whole, which is shorter than its diff:
```python
import functools

import jax
import jax.numpy as jnp
import numpy as np
from jax import lax
from jax.experimental import pallas as pl
from jax.experimental.pallas import tpu as pltpu
from jax.sharding import Mesh, PartitionSpec as P

GROUPS = 32
C = 320
CELLS = 1536
COLS = 64
EPS = 1e-5
BF = jnp.bfloat16
F32 = jnp.float32
KPAD = 1024
CPAD = 384
HALF = 192
VMEM = 48 * 1024 * 1024


def _consts():
    act_perm = np.zeros((3, C, KPAD), np.float32)
    for f in range(32):
        zl, x = divmod(f, 4)
        for kk in range(30):
            b, i = divmod(30 * f + kk, C)
            act_perm[b, i, 256 * x + 30 * zl + kk] = 1
    piece_perm = np.zeros((8, 128, KPAD), np.float32)
    for zl in range(8):
        for a in range(3):
            for kk in range(30):
                piece_perm[zl, 30 * a + kk, 256 * a + 30 * zl + kk] = 1
            for kk in range(10):
                piece_perm[zl, 90 + 10 * a + kk, 768 + 80 * a + 10 * zl + kk] = 1
    chan = np.zeros(C, np.int64)
    for i in range(C):
        d, j = divmod(i, 20)
        y, zh, core = d // 4, (d // 2) % 2, d % 2
        chan[i] = HALF * core + 48 * y + 24 * zh + j
    order = np.zeros((C, CPAD), np.float32)
    order[np.arange(C), chan] = 1
    temp_perm = np.zeros((KPAD, 3 * CPAD), np.float32)
    for x in range(4):
        for t in range(3):
            for zl in range(8):
                for kk in range(10):
                    i = 40 * zl + 10 * x + kk
                    temp_perm[256 * x + 80 * t + 10 * zl + kk, CPAD * t + chan[i]] = 1
    same1 = np.kron(np.eye(GROUPS), np.ones((10, 10))).astype(np.float32)
    same2 = order.T @ same1 @ order
    pack_s = np.zeros((3, 30, 128), np.float32)
    pack_t = np.zeros((3, 10, 128), np.float32)
    for a in range(3):
        pack_s[a, np.arange(30), 30 * a + np.arange(30)] = 1
        pack_t[a, np.arange(10), 90 + 10 * a + np.arange(10)] = 1
    return act_perm, piece_perm, order, temp_perm, same1, same2, pack_s, pack_t


ACT_PERM, PIECE_PERM, ORDER, TEMP_PERM, SAME1, SAME2, PACK_S, PACK_T = _consts()


def call(kernel, out_shape, flops=0, scratch=(), smem=0, n=0):
    specs = [pl.BlockSpec(memory_space=pltpu.SMEM)] * smem + [pl.BlockSpec(memory_space=pltpu.VMEM)] * n
    return pl.pallas_call(
        kernel,
        out_shape=out_shape,
        in_specs=specs,
        out_specs=jax.tree.map(lambda _: pl.BlockSpec(memory_space=pltpu.VMEM), out_shape),
        scratch_shapes=list(scratch),
        compiler_params=pltpu.CompilerParams(vmem_limit_bytes=VMEM),
        cost_estimate=pl.CostEstimate(flops=flops, bytes_accessed=4_000_000, transcendentals=0),
    )


def exact(a, b):
    return jnp.dot(a, b, precision=lax.Precision.HIGHEST, preferred_element_type=F32)


def nt(a, b):
    return lax.dot_general(a, b, (((1,), (1,)), ((), ())), preferred_element_type=F32)


def silu(v):
    half = 0.5 * v
    return half + half * jnp.tanh(half)


def pack_kernel(sw, tw, ps, pt, out):
    total = jnp.zeros((20, 128), F32)
    for a in range(3):
        total += lax.dot_general(sw[a], ps[a], (((0,), (0,)), ((), ())), preferred_element_type=F32)
        total += lax.dot_general(tw[a], pt[a], (((0,), (0,)), ((), ())), preferred_element_type=F32)
    piece = jnp.concatenate([total, jnp.zeros((4, 128), F32)], axis=0).astype(BF)
    for n in range(16):
        out[n] = piece


def line_kernel(pieces, perm, out):
    total = jnp.zeros((48, KPAD), F32)
    for zl in range(8):
        both = jnp.concatenate([pieces[zl].astype(F32), pieces[8 + zl].astype(F32)], axis=0)
        total += jnp.dot(both.astype(BF), perm[zl], preferred_element_type=F32)
    block = total.astype(BF)
    for n in range(16):
        out[n] = block


def act_kernel(video, gain, shift, same, perm, out):
    chunk = 256

    def sums(i, carry):
        s, q = carry
        v = video[pl.ds(pl.multiple_of(i * chunk, chunk), chunk), :].astype(F32).reshape(chunk // 8, 8, C)
        return s + jnp.sum(v, axis=0), q + jnp.sum(v * v, axis=0)

    zero = jnp.zeros((8, C), F32)
    s, q = lax.fori_loop(0, CELLS // chunk, sums, (zero, zero))
    count = CELLS * C // GROUPS
    mean = jnp.sum(exact(s, same[...]), axis=0, keepdims=True) / count
    square = jnp.sum(exact(q, same[...]), axis=0, keepdims=True) / count
    scale = lax.rsqrt(square - mean * mean + EPS) * gain[...]
    offset = shift[...] - mean * scale
    column = lax.rem(lax.broadcasted_iota(jnp.int32, (chunk, C), 0), COLS)
    out[pl.ds(0, COLS), :] = jnp.zeros((COLS, KPAD), BF)
    out[pl.ds(CELLS + COLS, COLS), :] = jnp.zeros((COLS, KPAD), BF)

    def rows(i, carry):
        v = video[pl.ds(pl.multiple_of(i * chunk, chunk), chunk), :].astype(F32)
        v = silu(v * scale + offset).astype(BF).astype(F32)
        before = jnp.where(column == 0, 0.0, pltpu.roll(v, 1, 0)).astype(BF)
        after = jnp.where(column == COLS - 1, 0.0, pltpu.roll(v, chunk - 1, 0)).astype(BF)
        total = jnp.dot(before, perm[0], preferred_element_type=F32)
        total += jnp.dot(v.astype(BF), perm[1], preferred_element_type=F32)
        total += jnp.dot(after, perm[2], preferred_element_type=F32)
        out[pl.ds(pl.multiple_of(i * chunk + COLS, COLS), chunk), :] = total.astype(BF)
        return carry

    lax.fori_loop(0, CELLS // chunk, rows, 0)


def place_weights(core, own, other, w):
    mine = core * HALF
    theirs = HALF - mine
    for y in range(4):
        for x in range(4):
            for a in range(3):
                lanes = pl.ds(256 * x, 256)
                w[a, pl.ds(pl.multiple_of(mine + 48 * y, 16), 48), lanes] = own[4 * y + x, :, 256 * a : 256 * a + 256]
                w[a, pl.ds(pl.multiple_of(theirs + 48 * y, 16), 48), lanes] = other[4 * y + x, :, 256 * a : 256 * a + 256]


def convolve(cols, w, emb, hidden, stats):
    chunk = 512

    def rows(i, carry):
        s, q = carry
        total = jnp.zeros((chunk, CPAD), F32)
        for a in range(3):
            part = cols[pl.ds(pl.multiple_of(i * chunk + COLS * a, COLS), chunk), :]
            total += nt(part, w[a])
        h = (total + emb).astype(BF)
        hidden[pl.ds(pl.multiple_of(i * chunk, chunk), chunk), :] = h
        if not stats:
            return carry
        h = h.astype(F32).reshape(chunk // 8, 8, CPAD)
        return s + jnp.sum(h, axis=0), q + jnp.sum(h * h, axis=0)

    zero = jnp.zeros((8, CPAD), F32)
    return lax.fori_loop(0, CELLS // chunk, rows, (zero, zero))


def own_kernel(core, cols, own, other, emb, hidden, stats, w):
    place_weights(core[0], own, other, w)
    s, q = convolve(cols, w, emb[...], hidden, True)
    s = jnp.sum(s, axis=0, keepdims=True)
    q = jnp.sum(q, axis=0, keepdims=True)
    rows = [s[:, :128], s[:, 128:256], s[:, 256:], q[:, :128], q[:, 128:256], q[:, 256:], jnp.zeros((2, 128), F32)]
    block = jnp.concatenate(rows, axis=0)
    for n in range(32):
        stats[n] = block


def near_kernel(core, before, after, own, other, emb0, emb2, hidden0, hidden2, w):
    place_weights(core[0], own, other, w)
    convolve(before, w, emb0[...], hidden0, False)
    convolve(after, w, emb2[...], hidden2, False)


def temporal_kernel(core, keep, own, other, perm, order, out, w):
    mine = core[0] * HALF
    theirs = HALF - mine
    for y in range(4):
        for x in range(4):
            lanes = pl.ds(256 * x, 256)
            w[pl.ds(pl.multiple_of(mine + 48 * y, 16), 48), lanes] = own[4 * y + x, :, 768:]
            w[pl.ds(pl.multiple_of(theirs + 48 * y, 16), 48), lanes] = other[4 * y + x, :, 768:]
    for t in range(3):
        part = jnp.dot(w[...], perm[:, CPAD * t : CPAD * t + CPAD], preferred_element_type=F32).astype(BF)
        part = jnp.dot(order[...], part, preferred_element_type=F32)
        if t != 1:
            part = part * keep[t // 2]
        out[:, CPAD * t : CPAD * t + CPAD] = part.astype(BF)
    out[:, 3 * CPAD :] = order[...]


def final_kernel(hidden0, hidden1, hidden2, stats, gain, shift, same, bias, w, out):
    total = stats[0]
    for n in range(1, 32):
        total = total + stats[n]
    s = jnp.concatenate([total[0:1], total[1:2], total[2:3]], axis=1)
    q = jnp.concatenate([total[3:4], total[4:5], total[5:6]], axis=1)
    both = jnp.concatenate([s, q, jnp.zeros((6, CPAD), F32)], axis=0)
    both = exact(both, same[...]) / (CELLS * 32 * C // GROUPS)
    mean, square = both[0:1], both[1:2]
    scale = lax.rsqrt(square - mean * mean + EPS) * gain[...]
    offset = shift[...] - mean * scale
    chunk = 256

    def rows(i, carry):
        here = pl.ds(pl.multiple_of(i * chunk, chunk), chunk)
        parts = [silu(h[here, :].astype(F32) * scale + offset).astype(BF) for h in (hidden0, hidden1, hidden2)]
        parts.append(hidden1[here, :])
        out[here, :] = (nt(jnp.concatenate(parts, axis=1), w[...]) + bias[...]).astype(BF)
        return carry

    lax.fori_loop(0, CELLS // chunk, rows, 0)


FRAME = ("zl", "x")
FORWARD = [(i, i + 1) for i in range(31)]
BACKWARD = [(i + 1, i) for i in range(31)]


def body(video, emb, gain1, shift1, gain2, shift2, sw, tw, bias):
    struct = jax.ShapeDtypeStruct
    const = lambda a, t=BF: jnp.asarray(a, t)
    core = lax.axis_index("core").astype(jnp.int32).reshape(1)
    frame = lax.axis_index(FRAME)
    keep = jnp.stack([frame > 0, frame < 31]).astype(F32)

    pieces = call(pack_kernel, struct((16, 24, 128), BF), n=4)(sw, tw, const(PACK_S), const(PACK_T))
    line = lax.all_to_all(pieces, ("zh", "zl"), 0, 0)
    frames = video.reshape(CELLS, C)
    frame0 = lax.ppermute(frames, FRAME, FORWARD)
    frame2 = lax.ppermute(frames, FRAME, BACKWARD)
    emb1 = emb.reshape(1, C)
    emb0 = lax.ppermute(emb1, FRAME, FORWARD)
    emb2 = lax.ppermute(emb1, FRAME, BACKWARD)

    act = lambda v: call(act_kernel, struct((CELLS + 2 * COLS, KPAD), BF), flops=9_000_000_000, n=5)(
        v, gain1.reshape(1, C), shift1.reshape(1, C), const(SAME1, F32), const(ACT_PERM)
    )
    cols1 = act(frames)
    block = call(line_kernel, struct((16, 48, KPAD), BF), n=2)(line, const(PIECE_PERM))
    own = lax.all_to_all(block, ("y", "x"), 0, 0)
    cols0, cols2 = act(frame0), act(frame2)
    other = lax.ppermute(own, "core", [(0, 1), (1, 0)])

    rows = jnp.concatenate([emb0, emb1, emb2, gain2[None], shift2[None], jnp.zeros((3, C), F32)], axis=0)
    rows = exact(rows, const(ORDER, F32))
    emb0, emb1, emb2, gain2, shift2 = (rows[n : n + 1] for n in range(5))

    weights = pltpu.VMEM((3, CPAD, KPAD), BF)
    hidden = struct((CELLS, CPAD), BF)
    hidden1, stats = call(
        own_kernel, (hidden, struct((32, 8, 128), F32)), flops=4_000_000_000, scratch=[weights], smem=1, n=4
    )(core, cols1, own, other, emb1)
    stats = lax.all_to_all(stats, FRAME, 0, 0)
    own, other, hidden1 = lax.optimization_barrier((own, other, hidden1))
    hidden0, hidden2 = call(near_kernel, (hidden, hidden), flops=8_000_000_000, scratch=[weights], smem=1, n=6)(
        core, cols0, cols2, own, other, emb0, emb2
    )
    w = call(
        temporal_kernel,
        struct((C, 4 * CPAD), BF),
        flops=2_000_000_000,
        scratch=[pltpu.VMEM((CPAD, KPAD), BF)],
        smem=2,
        n=4,
    )(core, keep, own, other, const(TEMP_PERM), const(ORDER))
    out = call(final_kernel, struct((CELLS, C), BF), flops=2_000_000_000, n=9)(
        hidden0, hidden1, hidden2, stats, gain2, shift2, const(SAME2, F32), bias.reshape(1, C), w
    )
    return out.reshape(video.shape)


def solution(mesh):
    split = Mesh(mesh.devices.reshape(4, 2, 2, 8, 4), ("y", "zh", "core", "zl", "x"))
    dp = ("y", "zh", "core")
    data = P(dp, FRAME, None, None, None)
    placed = (data, P(dp, FRAME, None), P(), P(), P(), P(), P(None, FRAME, dp), P(None, FRAME, dp), P())
    return jax.shard_map(body, mesh=split, in_specs=placed, out_specs=data, check_vma=False)
```

time: 648 us -> 160 us (0.25)
  blocking collectives: 468 us -> 27.4 us
  waiting for transfers between devices: 88.8 us -> 11.6 us
  Pallas kernels: 0 us -> 60.6 us
  starting transfers between devices: 3.93 us -> 33.6 us
  other arithmetic: 21.9 us -> 0.08 us
  local copies, waits for them, and re-layouts: 44.6 us -> 23.6 us
  between operations: 13.7 us -> 0.29 us
    all_gather x3 -> x0, blocking collectives: 307 us -> none  [the longest x1 117 us: body(): lax.all_gather(spatial_weight, 'frame', axis=1, tiled=True)]
    psum x1 -> x0, blocking collectives: 100 us -> none  [body(): lax.psum((jnp.sum(grouped, axis=(0, 2)), jnp.sum(grouped * grouped, axis=...]
    all_gather x1 -> x0, waiting for transfers between devices: 88.7 us -> none  [body(): lax.all_gather(spatial_rows, 'dp', axis=2, tiled=True)]
    pallas_call x0 -> x9, Pallas kernels: none -> 60.6 us  [the longest x3 26.3 us: body(): call(act_kernel, struct((CELLS + 2 * COLS, KPAD), BF), flops=9000000000,...]
    all_to_all x1, blocking collectives: 61 us -> 27.4 us  [body(): line = lax.all_to_all(pieces, ('zh', 'zl'), 0, 0)]
    ppermute x0 -> x5, starting transfers between devices: none -> 16.7 us  [the longest x1 5.8 us: body(): other = lax.ppermute(own, 'core', [(0, 1), (1, 0)])]
    slice x4 -> x1, local copies, waits for them, and re-layouts: 13.7 us -> 0.04 us  [body(): emb0, emb1, emb2, gain2, shift2 = (rows[n:n + 1] for n in range(5))]
    all_to_all x1 -> x2, starting transfers between devices: 3.92 us -> 16.9 us  [the longest x1 10 us: body(): stats = lax.all_to_all(stats, FRAME, 0, 0)]
  transfers between devices with their start and end apart: 2 -> 7, of which waited for: 1 -> 2; matrix products, arithmetic and copies ran while one was open for 4% -> 4% of each run, Pallas kernels for 0% -> 28%
where the time goes in v1:
time: 160 us; the launch traced here: 159 us
  Pallas kernels  60.6 us (38%)
  starting transfers between devices  33.6 us (21%)
  blocking collectives  27.4 us (17%)
  local copies, waits for them, and re-layouts  23.6 us (15%)
  waiting for transfers between devices  11.6 us (7%)
    all_to_all x1, blocking collectives, body(): line = lax.all_to_all(pieces, ('zh', 'zl'), 0, 0)  27.4 us
    pallas_call x3, Pallas kernels, body(): call(act_kernel, struct((CELLS + 2 * COLS, KPAD), BF), flops=9000000000,...  26.3 us
    unnamed x54, local copies, waits for them, and re-layouts  18.1 us
    pallas_call x1, Pallas kernels, body(): call(near_kernel, (hidden, hidden), flops=8000000000, scratch=[weights],...  14.3 us
    ppermute x1, waiting for transfers between devices, body(): frame0 = lax.ppermute(frames, FRAME, FORWARD)  11.4 us
    all_to_all x1, starting transfers between devices, body(): stats = lax.all_to_all(stats, FRAME, 0, 0)  10 us
    pallas_call x1, Pallas kernels, body(): call(own_kernel, (hidden, struct((32, 8, 128), F32)), flops=4000000000, s...  9.1 us
    all_to_all x1, starting transfers between devices, body(): own = lax.all_to_all(block, ('y', 'x'), 0, 0)  6.89 us
  transfers between devices with their start and end apart: 7, of which 2 were waited for; matrix products, arithmetic and copies ran while one was open for 4% of the time, Pallas kernels for 28%

profile of v1, /device:TPU:1, one launch (start us, length us, event | category | flops | bytes accessed | tf_op | source)
XLA Modules:
  0.0 158.6 jit_solution(6365155602968156391)
XLA Ops:
  3.2 27.4 %all_to_all.15.pieces = bf16[16,24,128]{2,1,0:T(8,128)(2,1)S(1)} all-to-all(bf16[16,24,128]{2,1,0:T(8,128)(2,1)S(1)} %shard_map.210), channel_id=1, replica_groups=mesh['y'=4,'zh'=2,'core'=2,'zl'=8,'x'=4] {'zh','zl'}, dimensions={0} | all-to-all | bytes 196608 | tf_op jit(solution)/shard_map/all_to_all | solution.py:245
  30.6 1.6 %copy-done = bf16[8,128,1024]{2,1,0:T(8,128)(2,1)S(1)} copy-done((bf16[8,128,1024]{2,1,0:T(8,128)(2,1)S(1)}, bf16[8,128,1024]{2,1,0:T(8,128)(2,1)}, u32[]{:S(2)}) %copy-start) | copy-done | bytes 2097176
  32.2 1.7 %shard_map.211 = bf16[16,48,1024]{2,1,0:T(8,128)(2,1)} custom-call(bf16[16,24,128]{2,1,0:T(8,128)(2,1)S(1)} %all_to_all.15.pieces, bf16[8,128,1024]{2,1,0:T(8,128)(2,1)S(1)} %copy-done), custom_call_target="tpu_custom_call" | custom-call | bytes 4000000 | tf_op jit(solution)/shard_map/pallas_call | solution.py:257
  33.9 6.9 %all-to-all-start.1 = ((bf16[16,48,1024]{2,1,0:T(8,128)(2,1)}), bf16[16,48,1024]{2,1,0:T(8,128)(2,1)S(1)}, u32[]{:S(2)}, u32[]{:S(2)}) async-start(bf16[16,48,1024]{2,1,0:T(8,128)(2,1)} %shard_map.211), calls=%async_computation.1 | async-start | bytes 3145728 | tf_op jit(solution)/shard_map/all_to_all | solution.py:258
  40.8 3.4 %collective-permute-start.3 = (f32[1,320]{1,0:T(1,128)S(1)}, f32[1,320]{1,0:T(1,128)S(1)}, u32[]{:S(2)}, u32[]{:S(2)}) collective-permute-start(f32[1,320]{1,0:T(1,128)S(1)} %bitcast.10), channel_id=1, source_target_pairs={{0,1},{1,2},{2,3},{3,4},{4,5},{5,6},{6,7},{7,8},{8,9},{9,10},{10,1... | collective-permute-start | bytes 3848 | tf_op jit(solution)/shard_map/ppermute | solution.py:250
  44.2 1.3 collective-permute-start.4
  45.5 1.4 copy.25
  46.9 5.0 %collective-permute-start = (bf16[1536,320]{0,1:T(8,128)(2,1)}, bf16[1536,320]{0,1:T(8,128)(2,1)}, u32[]{:S(2)}, u32[]{:S(2)}) collective-permute-start(bf16[1536,320]{0,1:T(8,128)(2,1)} %copy.25), channel_id=1, source_target_pairs={{0,1},{1,2},{2,3},{3,4},{4,5},{5,6},{6,7},{7,8},{8,9},{9,10},{10,1... | collective-permute-start | bytes 2949128 | tf_op jit(solution)/shard_map/ppermute | solution.py:247
  53.2 1.5 copy-done.7
  54.8 8.7 %shard_map.212.cols = bf16[1664,1024]{1,0:T(8,128)(2,1)} custom-call(bf16[1536,320]{1,0:T(8,128)(2,1)S(1)} %bitcast.9, f32[1,320]{1,0:T(1,128)S(1)} %reshape.27.gain, f32[1,320]{1,0:T(1,128)S(1)} %reshape.28.shift, f32[320,320]{1,0:T(8,128)S(1)} %copy-done.10, bf16[3,320,1024]{2,1,0:T(8,128)(2,1)S(1)} %copy-done.7), custom_call_target="tpu_custom_call" | custom-call | flops 8999999488 | bytes 4000000 | tf_op jit(solution)/shard_map/pallas_call | solution.py:253
  63.7 1.3 fusion.1
  65.1 11.4 %collective-permute-done = bf16[1536,320]{0,1:T(8,128)(2,1)} collective-permute-done((bf16[1536,320]{0,1:T(8,128)(2,1)}, bf16[1536,320]{0,1:T(8,128)(2,1)}, u32[]{:S(2)}, u32[]{:S(2)}) %collective-permute-start) | collective-permute-done | bytes 983072 | tf_op jit(solution)/shard_map/ppermute | solution.py:247
  76.5 1.7 %copy.26.video = bf16[1536,320]{1,0:T(8,128)(2,1)S(1)} copy(bf16[1536,320]{0,1:T(8,128)(2,1)} %collective-permute-done) | data formatting | bytes 1966080 | tf_op jit(solution)/shard_map/ppermute | solution.py:247
  78.4 2.3 %copy.28.video = bf16[1536,320]{1,0:T(8,128)(2,1)} copy(bf16[1536,320]{0,1:T(8,128)(2,1)} %collective-permute-done.1) | data formatting | bytes 1966080 | tf_op jit(solution)/shard_map/ppermute | solution.py:248
  80.7 5.8 %collective-permute-start.2 = (bf16[16,48,1024]{2,1,0:T(8,128)(2,1)S(1)}, bf16[16,48,1024]{2,1,0:T(8,128)(2,1)S(1)}, u32[]{:S(2)}, u32[]{:S(2)}) collective-permute-start(bf16[16,48,1024]{2,1,0:T(8,128)(2,1)S(1)} %all-to-all-done.1.own), channel_id=1, source_target_pairs={{0,32},{32,0},{1,33},{33,1},{2,34},{34,2},{3,35},{35,3},{4,36},{36... | collective-permute-start | bytes 4718600 | tf_op jit(solution)/shard_map/ppermute | solution.py:260
  86.5 1.5 copy-done.8
  88.1 8.8 %shard_map.208.before = bf16[1664,1024]{1,0:T(8,128)(2,1)} custom-call(bf16[1536,320]{1,0:T(8,128)(2,1)S(1)} %copy.26.video, f32[1,320]{1,0:T(1,128)S(1)} %reshape.27.gain, f32[1,320]{1,0:T(1,128)S(1)} %reshape.28.shift, f32[320,320]{1,0:T(8,128)S(1)} %copy-done.10, bf16[3,320,1024]{2,1,0:T(8,128)(2,1)S(1)} %copy-done.8), custom_call_target="tpu_custom_call" | custom-call | flops 8999999488 | bytes 4000000 | tf_op jit(solution)/shard_map/pallas_call | solution.py:253
  96.8 8.8 %shard_map.209.after = bf16[1664,1024]{1,0:T(8,128)(2,1)} custom-call(bf16[1536,320]{1,0:T(8,128)(2,1)S(1)} %copy-done.2, f32[1,320]{1,0:T(1,128)S(1)} %reshape.27.gain, f32[1,320]{1,0:T(1,128)S(1)} %reshape.28.shift, f32[320,320]{1,0:T(8,128)S(1)} %copy-done.10, bf16[3,320,1024]{2,1,0:T(8,128)(2,1)S(1)} %copy-done.8), custom_call_target="tpu_custom_call" | custom-call | flops 8999999488 | bytes 4000000 | tf_op jit(solution)/shard_map/pallas_call | solution.py:253
  105.6 9.1 %shard_map.213 = (bf16[1536,384]{1,0:T(8,128)(2,1)S(1)}, f32[32,8,128]{2,1,0:T(8,128)}) custom-call(s32[1]{0:T(128)} %bitcast.core, bf16[1664,1024]{1,0:T(8,128)(2,1)} %shard_map.212.cols, bf16[16,48,1024]{2,1,0:T(8,128)(2,1)S(1)} %all-to-all-done.1.own, bf16[16,48,1024]{2,1,0:T(8,128)(2,1)S(1)} %collective-permute-done.2.other, ...), custom_call_target="tpu_custom_call" | custom-call | flops 4000000000 | bytes 4000000 | tf_op jit(solution)/shard_map/pallas_call | solution.py:268
  115.8 10.0 %all-to-all-start.2 = ((f32[32,8,128]{2,1,0:T(8,128)}), f32[32,8,128]{2,1,0:T(8,128)S(1)}, u32[]{:S(2)}, u32[]{:S(2)}) async-start(f32[32,8,128]{2,1,0:T(8,128)} %get-tuple-element.18), calls=%async_computation.2 | async-start | bytes 262144 | tf_op jit(solution)/shard_map/all_to_all | solution.py:271
  125.8 1.4 copy-done.6
  127.2 3.9 %shard_map.215.w = bf16[320,1536]{1,0:T(8,128)(2,1)S(1)} custom-call(s32[1]{0:T(128)} %bitcast.core, f32[2]{0:T(128)S(1)} %add_convert_fusion.keep, bf16[16,48,1024]{2,1,0:T(8,128)(2,1)S(1)} %all-to-all-done.1.own, bf16[16,48,1024]{2,1,0:T(8,128)(2,1)S(1)} %copy-done.6, bf16[1024,1152]{1,0:T(8,128)(2,1)} %constant.47.clone.perm, bf16[320,384]{1,0:T(8,128)(2,1)S(1)} %copy-done.11), custom_call_target="tpu_custom_call" | custom-call | flops 2000000000 | bytes 4000000 | tf_op jit(solution)/shard_map/pallas_call | solution.py:276
  132.1 14.3 %shard_map.214 = (bf16[1536,384]{1,0:T(8,128)(2,1)S(1)}, bf16[1536,384]{1,0:T(8,128)(2,1)S(1)}) custom-call(s32[1]{0:T(128)} %bitcast.core, bf16[1664,1024]{1,0:T(8,128)(2,1)} %shard_map.208.before, bf16[1664,1024]{1,0:T(8,128)(2,1)} %shard_map.209.after, bf16[16,48,1024]{2,1,0:T(8,128)(2,1)S(1)} %all-to-all-done.1.own, bf16[16,48,1024]{2,1,0:T(8,128)(2,1)S(1)} %copy-done.6, ...), custom_call_target="tpu_custom_call" | custom-call | flops 8000000000 | bytes 4000000 | tf_op jit(solution)/shard_map/pallas_call | solution.py:273
  153.4 5.2 %shard_map.216 = bf16[1536,320]{1,0:T(8,128)(2,1)} custom-call(bf16[1536,384]{1,0:T(8,128)(2,1)S(1)} %copy-done.17, bf16[1536,384]{1,0:T(8,128)(2,1)S(1)} %copy-done.15, bf16[1536,384]{1,0:T(8,128)(2,1)S(1)} %copy-done.19, f32[32,8,128]{2,1,0:T(8,128)S(1)} %all-to-all-done.2.stats, f32[1,384]{1,0:T(1,128)S(1)} %get-tuple-element.20.gain, ...), custom_call_target="tpu_custom_call" | custom-call | flops 2000000000 | bytes 4000000 | tf_op jit(solution)/shard_map/pallas_call | solution.py:284
  (67 shorter events, 13.9 us)
Async XLA Ops:
  30.6 1.6 %copy-start = (bf16[8,128,1024]{2,1,0:T(8,128)(2,1)S(1)}, bf16[8,128,1024]{2,1,0:T(8,128)(2,1)}, u32[]{:S(2)}) copy-start(bf16[8,128,1024]{2,1,0:T(8,128)(2,1)} %constant.45.clone.perm) | copy-start | bytes 6291460
  33.9 6.9 %copy-start.25 = (f32[1,1,320]{2,1,0:T(1,128)S(1)}, f32[1,1,320]{2,1,0:T(1,128)}, u32[]{:S(2)}) copy-start(f32[1,1,320]{2,1,0:T(1,128)} %param.23) | copy-start | bytes 3844
  33.9 11.6 %copy-start.1 = (bf16[1,1,24,64,320]{4,3,2,1,0:T(8,128)(2,1)S(1)}, bf16[1,1,24,64,320]{4,3,2,1,0:T(8,128)(2,1)}, u32[]{:S(2)}) copy-start(bf16[1,1,24,64,320]{4,3,2,1,0:T(8,128)(2,1)} %param.22) | copy-start | bytes 2949124
  33.9 46.8 %all-to-all-start.1 = ((bf16[16,48,1024]{2,1,0:T(8,128)(2,1)}), bf16[16,48,1024]{2,1,0:T(8,128)(2,1)S(1)}, u32[]{:S(2)}, u32[]{:S(2)}) async-start(bf16[16,48,1024]{2,1,0:T(8,128)(2,1)} %shard_map.211), calls=%async_computation.1 | async-start | bytes 3145728 | tf_op jit(solution)/shard_map/all_to_all | solution.py:258
  40.8 12.4 %copy-start.20 = (f32[320]{0:T(512)S(1)}, f32[320]{0:T(512)}, u32[]{:S(2)}) copy-start(f32[320]{0:T(512)} %param.24) | copy-start | bytes 3844
  40.8 12.4 %copy-start.21 = (f32[320]{0:T(512)S(1)}, f32[320]{0:T(512)}, u32[]{:S(2)}) copy-start(f32[320]{0:T(512)} %param.25) | copy-start | bytes 3844
  40.8 12.4 %copy-start.10 = (f32[320,320]{1,0:T(8,128)S(1)}, f32[320,320]{1,0:T(8,128)}, u32[]{:S(2)}) copy-start(f32[320,320]{1,0:T(8,128)} %constant.43.clone.same) | copy-start | bytes 1228804
  40.8 22.8 %collective-permute-start.3 = (f32[1,320]{1,0:T(1,128)S(1)}, f32[1,320]{1,0:T(1,128)S(1)}, u32[]{:S(2)}, u32[]{:S(2)}) collective-permute-start(f32[1,320]{1,0:T(1,128)S(1)} %bitcast.10), channel_id=1, source_target_pairs={{0,1},{1,2},{2,3},{3,4},{4,5},{5,6},{6,7},{7,8},{8,9},{9,10},{10,1... | collective-permute-start | bytes 3848 | tf_op jit(solution)/shard_map/ppermute | solution.py:250
  44.2 19.4 %collective-permute-start.4 = (f32[1,320]{1,0:T(1,128)S(1)}, f32[1,320]{1,0:T(1,128)S(1)}, u32[]{:S(2)}, u32[]{:S(2)}) collective-permute-start(f32[1,320]{1,0:T(1,128)S(1)} %bitcast.11), channel_id=1, source_target_pairs={{1,0},{2,1},{3,2},{4,3},{5,4},{6,5},{7,6},{8,7},{9,8},{10,9},{11,1... | collective-permute-start | bytes 3848 | tf_op jit(solution)/shard_map/ppermute | solution.py:251
  46.9 29.5 %collective-permute-start = (bf16[1536,320]{0,1:T(8,128)(2,1)}, bf16[1536,320]{0,1:T(8,128)(2,1)}, u32[]{:S(2)}, u32[]{:S(2)}) collective-permute-start(bf16[1536,320]{0,1:T(8,128)(2,1)} %copy.25), channel_id=1, source_target_pairs={{0,1},{1,2},{2,3},{3,4},{4,5},{5,6},{6,7},{7,8},{8,9},{9,10},{10,1... | collective-permute-start | bytes 2949128 | tf_op jit(solution)/shard_map/ppermute | solution.py:247
  51.9 26.5 %collective-permute-start.1 = (bf16[1536,320]{0,1:T(8,128)(2,1)}, bf16[1536,320]{0,1:T(8,128)(2,1)}, u32[]{:S(2)}, u32[]{:S(2)}) collective-permute-start(bf16[1536,320]{0,1:T(8,128)(2,1)} %copy.25), channel_id=1, source_target_pairs={{1,0},{2,1},{3,2},{4,3},{5,4},{6,5},{7,6},{8,7},{9,8},{10,9},{11,1... | collective-permute-start | bytes 2949128 | tf_op jit(solution)/shard_map/ppermute | solution.py:248
  53.2 1.5 copy-start.7
  54.8 8.8 %copy-start.22 = (f32[320]{0:T(512)S(1)}, f32[320]{0:T(512)}, u32[]{:S(2)}) copy-start(f32[320]{0:T(512)} %param.27) | copy-start | bytes 3844
  54.8 8.8 %copy-start.23 = (f32[320]{0:T(512)S(1)}, f32[320]{0:T(512)}, u32[]{:S(2)}) copy-start(f32[320]{0:T(512)} %param.26) | copy-start | bytes 3844
  54.8 8.8 %copy-start.24 = (f32[320]{0:T(512)S(1)}, f32[320]{0:T(512)}, u32[]{:S(2)}) copy-start(f32[320]{0:T(512)} %param.30) | copy-start | bytes 3844
  80.7 16.1 %copy-start.2 = (bf16[1536,320]{1,0:T(8,128)(2,1)S(1)}, bf16[1536,320]{1,0:T(8,128)(2,1)}, u32[]{:S(2)}) copy-start(bf16[1536,320]{1,0:T(8,128)(2,1)} %copy.28.video) | copy-start | bytes 2949124
  80.7 24.9 %collective-permute-start.2 = (bf16[16,48,1024]{2,1,0:T(8,128)(2,1)S(1)}, bf16[16,48,1024]{2,1,0:T(8,128)(2,1)S(1)}, u32[]{:S(2)}, u32[]{:S(2)}) collective-permute-start(bf16[16,48,1024]{2,1,0:T(8,128)(2,1)S(1)} %all-to-all-done.1.own), channel_id=1, source_target_pairs={{0,32},{32,0},{1,33},{33,1},{2,34},{34,2},{3,35},{35,3},{4,36},{36... | collective-permute-start | bytes 4718600 | tf_op jit(solution)/shard_map/ppermute | solution.py:260
  86.5 1.5 copy-start.8
  105.6 9.1 %copy-start.5 = (bf16[16,48,1024]{2,1,0:T(8,128)(2,1)}, bf16[16,48,1024]{2,1,0:T(8,128)(2,1)S(1)}, u32[]{:S(2)}) copy-start(bf16[16,48,1024]{2,1,0:T(8,128)(2,1)S(1)} %collective-permute-done.2.other) | copy-start | bytes 4718596
  105.6 20.2 %copy-start.11 = (bf16[320,384]{1,0:T(8,128)(2,1)S(1)}, bf16[320,384]{1,0:T(8,128)(2,1)}, u32[]{:S(2)}) copy-start(bf16[320,384]{1,0:T(8,128)(2,1)} %constant.48.clone.order) | copy-start | bytes 737284
  115.8 32.6 %all-to-all-start.2 = ((f32[32,8,128]{2,1,0:T(8,128)}), f32[32,8,128]{2,1,0:T(8,128)S(1)}, u32[]{:S(2)}, u32[]{:S(2)}) async-start(f32[32,8,128]{2,1,0:T(8,128)} %get-tuple-element.18), calls=%async_computation.2 | async-start | bytes 262144 | tf_op jit(solution)/shard_map/all_to_all | solution.py:271
  125.8 1.4 copy-start.6
  132.0 16.3 %copy-start.9 = (f32[384,384]{1,0:T(8,128)S(1)}, f32[384,384]{1,0:T(8,128)}, u32[]{:S(2)}) copy-start(f32[384,384]{1,0:T(8,128)} %constant.49.clone.same) | copy-start | bytes 1769476
  150.9 1.3 copy-start.17
  (9 other events, 9.2 us)

commit v2 on v1

v2 whole, which is shorter than its diff:
```python
import functools

import jax
import jax.numpy as jnp
import numpy as np
from jax import lax
from jax.experimental import pallas as pl
from jax.experimental.pallas import tpu as pltpu
from jax.sharding import Mesh, PartitionSpec as P

GROUPS = 32
C = 320
CELLS = 1536
COLS = 64
EPS = 1e-5
BF = jnp.bfloat16
F32 = jnp.float32
KPAD = 1024
CPAD = 384
HALF = 192
PACKED = CELLS * 5 // 2 + 16
VMEM = 60 * 1024 * 1024


def _consts():
    act_perm = np.zeros((KPAD, KPAD), np.float32)
    for f in range(32):
        zl, x = divmod(f, 4)
        for kk in range(30):
            b, i = divmod(30 * f + kk, C)
            row = 256 * b + i if i < 256 else 768 + 64 * b + i - 256
            act_perm[row, 256 * x + 30 * zl + kk] = 1
    piece_perm = np.zeros((8, 128, KPAD), np.float32)
    for zl in range(8):
        for a in range(3):
            for kk in range(30):
                piece_perm[zl, 30 * a + kk, 256 * a + 30 * zl + kk] = 1
            for kk in range(10):
                piece_perm[zl, 90 + 10 * a + kk, 768 + 80 * a + 10 * zl + kk] = 1
    chan = np.zeros(C, np.int64)
    for i in range(C):
        d, j = divmod(i, 20)
        y, zh, core = d // 4, (d // 2) % 2, d % 2
        chan[i] = HALF * core + 48 * y + 24 * zh + j
    order = np.zeros((C, CPAD), np.float32)
    order[np.arange(C), chan] = 1
    temp_perm = np.zeros((KPAD, 3 * CPAD), np.float32)
    for x in range(4):
        for t in range(3):
            for zl in range(8):
                for kk in range(10):
                    i = 40 * zl + 10 * x + kk
                    temp_perm[256 * x + 80 * t + 10 * zl + kk, CPAD * t + chan[i]] = 1
    same1 = np.kron(np.eye(GROUPS), np.ones((10, 10))).astype(np.float32)
    same2 = order.T @ same1 @ order
    return act_perm, piece_perm, order, temp_perm, same1, same2


ACT_PERM, PIECE_PERM, ORDER, TEMP_PERM, SAME1, SAME2 = _consts()


def call(kernel, out_shape, flops=0, smem=0, n=0):
    specs = [pl.BlockSpec(memory_space=pltpu.SMEM)] * smem + [pl.BlockSpec(memory_space=pltpu.VMEM)] * n
    return pl.pallas_call(
        kernel,
        out_shape=out_shape,
        in_specs=specs,
        out_specs=jax.tree.map(lambda _: pl.BlockSpec(memory_space=pltpu.VMEM), out_shape),
        compiler_params=pltpu.CompilerParams(vmem_limit_bytes=VMEM),
        cost_estimate=pl.CostEstimate(flops=flops, bytes_accessed=0, transcendentals=0),
    )


def exact(a, b):
    return jnp.dot(a, b, precision=lax.Precision.HIGHEST, preferred_element_type=F32)


def nt(a, b):
    return lax.dot_general(a, b, (((1,), (1,)), ((), ())), preferred_element_type=F32)


def silu(v):
    half = 0.5 * v
    return half + half * jnp.tanh(half)


def pack_kernel(sw, tw, out):
    total = jnp.zeros((20, 128), F32)
    for a in range(3):
        lane = lax.broadcasted_iota(jnp.int32, (30, 128), 1) - lax.broadcasted_iota(jnp.int32, (30, 128), 0)
        total += jnp.dot(sw[a], (lane == 30 * a).astype(F32).astype(BF), preferred_element_type=F32)
        lane = lane[:10]
        spread = (lane == 90 + 10 * a).astype(F32).astype(BF)
        total += lax.dot_general(tw[a], spread, (((0,), (0,)), ((), ())), preferred_element_type=F32)
    piece = jnp.concatenate([total, jnp.zeros((4, 128), F32)], axis=0).astype(BF)
    for n in range(16):
        out[n] = piece


def frame_kernel(video, emb, out):
    out[pl.ds(0, CELLS), :] = video[:, 0:128]
    out[pl.ds(CELLS, CELLS), :] = video[:, 128:256]
    out[pl.ds(2 * CELLS, CELLS // 2), :] = jnp.concatenate(
        [video[: CELLS // 2, 256:320], video[CELLS // 2 :, 256:320]], axis=1
    )
    rest = jnp.concatenate([emb[...], jnp.zeros((1, 64), F32)], axis=1)
    rows = []
    for n in range(3):
        part = rest.astype(BF).astype(F32)
        rest = rest - part
        rows += [part[:, 0:128], part[:, 128:256], part[:, 256:384]]
    rows.append(jnp.zeros((7, 128), F32))
    out[pl.ds(PACKED - 16, 16), :] = jnp.concatenate(rows, axis=0).astype(BF)


def line_kernel(pieces, perm, out):
    total = jnp.zeros((48, KPAD), F32)
    for zl in range(8):
        both = jnp.concatenate([pieces[zl].astype(F32), pieces[8 + zl].astype(F32)], axis=0)
        total += jnp.dot(both.astype(BF), perm[zl], preferred_element_type=F32)
    block = total.astype(BF)
    for n in range(16):
        out[n] = block


def act_kernel(frame, gain, shift, same, order, perm, out, emb):
    chunk = 256
    half = CELLS // 2

    def load(i):
        start = i * chunk
        a = frame[pl.ds(start, chunk), :]
        b = frame[pl.ds(CELLS + start, chunk), :]
        c = frame[pl.ds(2 * CELLS + start % half, chunk), :]
        c = c[:, :64] if start < half else c[:, 64:]
        return jnp.concatenate([a.astype(F32), b.astype(F32), c.astype(F32)], axis=1)

    s = jnp.zeros((8, C), F32)
    q = jnp.zeros((8, C), F32)
    for i in range(CELLS // chunk):
        v = load(i).reshape(chunk // 8, 8, C)
        s, q = s + jnp.sum(v, axis=0), q + jnp.sum(v * v, axis=0)
    count = CELLS * C // GROUPS
    both = exact(jnp.concatenate([s, q], axis=0), same[...]) / count
    mean = jnp.sum(both[:8], axis=0, keepdims=True)
    square = jnp.sum(both[8:], axis=0, keepdims=True)
    scale = lax.rsqrt(square - mean * mean + EPS) * gain[...]
    offset = shift[...] - mean * scale
    column = lax.rem(lax.broadcasted_iota(jnp.int32, (chunk, C), 0), COLS)
    out[pl.ds(0, COLS), :] = jnp.zeros((COLS, KPAD), BF)
    out[pl.ds(CELLS + COLS, COLS), :] = jnp.zeros((COLS, KPAD), BF)
    for i in range(CELLS // chunk):
        v = silu(load(i) * scale + offset).astype(BF).astype(F32)
        before = jnp.where(column == 0, 0.0, pltpu.roll(v, 1, 0))
        after = jnp.where(column == COLS - 1, 0.0, pltpu.roll(v, chunk - 1, 0))
        rest = [before[:, 256:], v[:, 256:], after[:, 256:], jnp.zeros((chunk, 64), F32)]
        taps = jnp.concatenate([before[:, :256], v[:, :256], after[:, :256]] + rest, axis=1).astype(BF)
        total = jnp.dot(taps, perm[...], preferred_element_type=F32)
        out[pl.ds(i * chunk + COLS, chunk), :] = total.astype(BF)
    rows = frame[pl.ds(PACKED - 16, 16), :].astype(F32)
    parts = [jnp.concatenate([rows[3 * n : 3 * n + 1], rows[3 * n + 1 : 3 * n + 2], rows[3 * n + 2 : 3 * n + 3, :64]], axis=1) for n in range(3)]
    parts = jnp.concatenate(parts + [jnp.zeros((5, C), F32)], axis=0).astype(BF)
    emb[...] = jnp.sum(jnp.dot(parts, order[...], preferred_element_type=F32), axis=0, keepdims=True)


def place_weights(core, own, other, w):
    mine = core * HALF
    theirs = HALF - mine
    for y in range(4):
        for x in range(4):
            for a in range(4):
                lanes = pl.ds(256 * x, 256)
                w[a, pl.ds(pl.multiple_of(mine + 48 * y, 16), 48), lanes] = own[4 * y + x, :, 256 * a : 256 * a + 256]
                w[a, pl.ds(pl.multiple_of(theirs + 48 * y, 16), 48), lanes] = other[4 * y + x, :, 256 * a : 256 * a + 256]


def convolve(cols, w, emb, hidden, stats):
    chunk = 256
    s = jnp.zeros((8, CPAD), F32)
    q = jnp.zeros((8, CPAD), F32)
    for i in range(CELLS // chunk):
        total = jnp.zeros((CPAD, chunk), F32)
        for a in range(3):
            total += nt(w[a], cols[pl.ds(i * chunk + COLS * a, chunk), :])
        h = (total.T + emb).astype(BF)
        hidden[pl.ds(i * chunk, chunk), :] = h
        if stats:
            h = h.astype(F32).reshape(chunk // 8, 8, CPAD)
            s, q = s + jnp.sum(h, axis=0), q + jnp.sum(h * h, axis=0)
    return s, q


def own_kernel(core, cols, own, other, emb, hidden, stats, w):
    place_weights(core[0], own, other, w)
    s, q = convolve(cols, w, emb[...], hidden, True)
    s = jnp.sum(s, axis=0, keepdims=True)
    q = jnp.sum(q, axis=0, keepdims=True)
    rows = [s[:, :128], s[:, 128:256], s[:, 256:], q[:, :128], q[:, 128:256], q[:, 256:], jnp.zeros((2, 128), F32)]
    block = jnp.concatenate(rows, axis=0)
    for n in range(32):
        stats[n] = block


def near_kernel(before, after, w, emb0, emb2, hidden0, hidden2):
    convolve(before, w, emb0[...], hidden0, False)
    convolve(after, w, emb2[...], hidden2, False)


def temporal_kernel(keep, w, perm, order, out):
    for t in range(3):
        part = jnp.dot(w[3], perm[:, CPAD * t : CPAD * t + CPAD], preferred_element_type=F32).astype(BF)
        part = jnp.dot(order[...], part, preferred_element_type=F32)
        if t != 1:
            part = part * keep[t // 2]
        out[:, CPAD * t : CPAD * t + CPAD] = part.astype(BF)
    out[:, 3 * CPAD :] = order[...]


def final_kernel(hidden0, hidden1, hidden2, stats, gain, shift, same, bias, w, out):
    total = stats[0]
    for n in range(1, 32):
        total = total + stats[n]
    s = jnp.concatenate([total[0:1], total[1:2], total[2:3]], axis=1)
    q = jnp.concatenate([total[3:4], total[4:5], total[5:6]], axis=1)
    both = jnp.concatenate([s, q, jnp.zeros((6, CPAD), F32)], axis=0)
    both = exact(both, same[...]) / (CELLS * 32 * C // GROUPS)
    mean, square = both[0:1], both[1:2]
    scale = lax.rsqrt(square - mean * mean + EPS) * gain[...]
    offset = shift[...] - mean * scale
    chunk = 256
    for i in range(CELLS // chunk):
        here = pl.ds(i * chunk, chunk)
        parts = [silu(h[here, :].astype(F32) * scale + offset).astype(BF) for h in (hidden0, hidden1, hidden2)]
        parts.append(hidden1[here, :])
        out[here, :] = (nt(jnp.concatenate(parts, axis=1), w[...]) + bias[...]).astype(BF)


FILL = 7_500_000_000
FRAME = ("zl", "x")
FORWARD = [(i, i + 1) for i in range(31)]
BACKWARD = [(i + 1, i) for i in range(31)]


def body(video, emb, gain1, shift1, gain2, shift2, sw, tw, bias):
    struct = jax.ShapeDtypeStruct
    const = lambda a, t=BF: jnp.asarray(a, t)
    core = lax.axis_index("core").astype(jnp.int32).reshape(1)
    frame = lax.axis_index(FRAME)
    keep = jnp.stack([frame > 0, frame < 31]).astype(F32)

    pieces = call(pack_kernel, struct((16, 24, 128), BF), n=2)(sw.transpose(0, 2, 1), tw)
    frame1 = call(frame_kernel, struct((PACKED, 128), BF), n=2)(video.reshape(CELLS, C), emb.reshape(1, C))
    line = lax.all_to_all(pieces, ("zh", "zl"), 0, 0)
    frame0 = lax.ppermute(frame1, FRAME, FORWARD)
    frame2 = lax.ppermute(frame1, FRAME, BACKWARD)

    act = lambda v, flops=100_000_000: call(act_kernel, (struct((CELLS + 2 * COLS, KPAD), BF), struct((1, CPAD), F32)), flops=flops, n=6)(
        v, gain1.reshape(1, C), shift1.reshape(1, C), const(SAME1, F32), const(ORDER), const(ACT_PERM)
    )
    cols1, emb1 = act(frame1)
    line, cols1 = lax.optimization_barrier((line, cols1))
    block = call(line_kernel, struct((16, 48, KPAD), BF), n=2)(line, const(PIECE_PERM))
    own = lax.all_to_all(block, ("y", "x"), 0, 0)
    frame0, frame2 = lax.optimization_barrier((frame0, frame2))
    cols0, emb0 = act(frame0, FILL)
    own, cols0 = lax.optimization_barrier((own, cols0))
    other = lax.ppermute(own, "core", [(0, 1), (1, 0)])
    cols2, emb2 = act(frame2)
    other, cols2 = lax.optimization_barrier((other, cols2))
    rows = exact(jnp.concatenate([gain2[None], shift2[None], jnp.zeros((6, C), F32)], axis=0), const(ORDER, F32))

    hidden = struct((CELLS, CPAD), BF)
    hidden1, stats, w = call(
        own_kernel, (hidden, struct((32, 8, 128), F32), struct((4, CPAD, KPAD), BF)), smem=1, n=4
    )(core, cols1, own, other, emb1)
    stats = lax.all_to_all(stats, FRAME, 0, 0)
    hidden0, hidden2 = call(near_kernel, (hidden, hidden), flops=7_300_000_000, n=5)(cols0, cols2, w, emb0, emb2)
    w = call(temporal_kernel, struct((C, 4 * CPAD), BF), flops=1_000_000_000, smem=1, n=3)(keep, w, const(TEMP_PERM), const(ORDER))
    out = call(final_kernel, struct((CELLS, C), BF), n=9)(
        hidden0, hidden1, hidden2, stats, rows[0:1], rows[1:2], const(SAME2, F32), bias.reshape(1, C), w
    )
    return out.reshape(video.shape)


def solution(mesh):
    split = Mesh(mesh.devices.reshape(4, 2, 2, 8, 4), ("y", "zh", "core", "zl", "x"))
    dp = ("y", "zh", "core")
    data = P(dp, FRAME, None, None, None)
    placed = (data, P(dp, FRAME, None), P(), P(), P(), P(), P(None, FRAME, dp), P(None, FRAME, dp), P())
    return jax.shard_map(body, mesh=split, in_specs=placed, out_specs=data, check_vma=False)
```

time: 160 us -> 133 us (0.83)
  blocking collectives: 27.4 us -> 0 us
  local copies, waits for them, and re-layouts: 23.6 us -> 6.2 us
  starting transfers between devices: 33.6 us -> 43.9 us
  Pallas kernels: 60.6 us -> 67 us
    all_to_all x1 -> x0, blocking collectives: 27.4 us -> none  [body(): line = lax.all_to_all(pieces, ('zh', 'zl'), 0, 0)]
    all_to_all x0 -> x1, starting transfers between devices: none -> 15.7 us  [body(): line = lax.all_to_all(pieces, ('zh', 'zl'), 0, 0)]
    unnamed x54 -> x21, local copies, waits for them, and re-layouts: 18.1 us -> 3.79 us
    all_to_all x1, waiting for transfers between devices: 0.01 us -> 9.86 us  [body(): own = lax.all_to_all(block, ('y', 'x'), 0, 0)]
    ppermute x4 -> x2, waiting for transfers between devices: 11.6 us -> 2.77 us  [the longest x1 2.77 us: body(): frame2 = lax.ppermute(frame1, FRAME, BACKWARD)]
    ppermute x4 -> x2, starting transfers between devices: 10.9 us -> 5.44 us  [the longest x1 4.16 us: body(): frame0 = lax.ppermute(frame1, FRAME, FORWARD)]
    pallas_call x8 -> x9, Pallas kernels: 58.9 us -> 63.6 us  [the longest x3 25.2 us: body(): call(act_kernel, (struct((CELLS + 2 * COLS, KPAD), BF), struct((1, CPAD),...]
    ppermute x2 -> x0, local copies, waits for them, and re-layouts: 4 us -> none  [the longest x1 2.34 us: body(): frame2 = lax.ppermute(frames, FRAME, BACKWARD)]
  transfers between devices with their start and end apart: 7 -> 6, of which waited for: 2 -> 2; matrix products, arithmetic and copies ran while one was open for 4% -> 3% of each run, Pallas kernels for 28% -> 37%
where the time goes in v2:
time: 133 us; the launch traced here: 132 us
  Pallas kernels  67 us (50%)
  starting transfers between devices  43.9 us (33%)
  waiting for transfers between devices  12.6 us (9%)
  local copies, waits for them, and re-layouts  6.2 us (5%)
  matrix products  1.4 us (1%)
    pallas_call x3, Pallas kernels, body(): call(act_kernel, (struct((CELLS + 2 * COLS, KPAD), BF), struct((1, CPAD),...  25.2 us
    all_to_all x1, starting transfers between devices, body(): line = lax.all_to_all(pieces, ('zh', 'zl'), 0, 0)  15.7 us
    pallas_call x1, Pallas kernels, body(): call(near_kernel, (hidden, hidden), flops=7300000000, n=5)  12.6 us
    all_to_all x1, starting transfers between devices, body(): stats = lax.all_to_all(stats, FRAME, 0, 0)  11.4 us
    all_to_all x1, waiting for transfers between devices, body(): own = lax.all_to_all(block, ('y', 'x'), 0, 0)  9.86 us
    pallas_call x1, Pallas kernels, body(): call(own_kernel, (hidden, struct((32, 8, 128), F32), struct((4, CPAD, KPA...  9.49 us
    pallas_call x1, Pallas kernels, body(): call(final_kernel, struct((CELLS, C), BF), n=9)  6.7 us
    all_to_all x1, starting transfers between devices, body(): own = lax.all_to_all(block, ('y', 'x'), 0, 0)  6.59 us
  transfers between devices with their start and end apart: 6, of which 2 were waited for; matrix products, arithmetic and copies ran while one was open for 3% of the time, Pallas kernels for 37%

profile of v2, /device:TPU:1, one launch (start us, length us, event | category | flops | bytes accessed | tf_op | source)
XLA Modules:
  0.0 132.0 jit_solution(9065297673027906321)
XLA Ops:
  0.0 1.3 %copy.24.tw = bf16[3,10,20]{2,1,0:T(8,128)(2,1)} copy(bf16[3,10,20]{2,0,1:T(4,128)(2,1)} %param.30) | data formatting | bytes 2400 | tf_op args[7]
  1.3 1.6 %shard_map.217 = bf16[16,24,128]{2,1,0:T(8,128)(2,1)} custom-call(bf16[3,20,30]{2,1,0:T(8,128)(2,1)} %bitcast.9, bf16[3,10,20]{2,1,0:T(8,128)(2,1)} %copy.24.tw), custom_call_target="tpu_custom_call" | custom-call | tf_op jit(solution)/shard_map/pallas_call | solution.py:251
  2.9 15.7 %all-to-all-start = ((bf16[16,24,128]{2,1,0:T(8,128)(2,1)}), bf16[16,24,128]{2,1,0:T(8,128)(2,1)S(1)}, u32[]{:S(2)}, u32[]{:S(2)}) async-start(bf16[16,24,128]{2,1,0:T(8,128)(2,1)} %shard_map.217), calls=%async_computation | async-start | bytes 196608 | tf_op jit(solution)/shard_map/all_to_all | solution.py:253
  18.6 2.4 %shard_map.218.frame = bf16[3856,128]{1,0:T(8,128)(2,1)} custom-call(bf16[1536,320]{1,0:T(8,128)(2,1)} %bitcast.8, f32[1,320]{1,0:T(1,128)} %bitcast.10), custom_call_target="tpu_custom_call" | custom-call | tf_op jit(solution)/shard_map/pallas_call | solution.py:252
  21.1 4.2 %collective-permute-start = (bf16[3856,128]{1,0:T(8,128)(2,1)}, bf16[3856,128]{1,0:T(8,128)(2,1)}, u32[]{:S(2)}, u32[]{:S(2)}) collective-permute-start(bf16[3856,128]{1,0:T(8,128)(2,1)} %shard_map.218.frame), channel_id=1, source_target_pairs={{0,1},{1,2},{2,3},{3,4},{4,5},{5,6},{6,7},{7,8},{8,9},{9,10},{10,1... | collective-permute-start | bytes 2961416 | tf_op jit(solution)/shard_map/ppermute | solution.py:254
  25.2 1.3 collective-permute-start.1
  27.6 8.3 %shard_map.219 = (bf16[1664,1024]{1,0:T(8,128)(2,1)}, f32[1,384]{1,0:T(1,128)}) custom-call(bf16[3856,128]{1,0:T(8,128)(2,1)} %shard_map.218.frame, f32[1,320]{1,0:T(1,128)} %reshape.27.gain, f32[1,320]{1,0:T(1,128)} %reshape.28.shift, f32[320,320]{1,0:T(8,128)} %constant.37.clone.same, bf16[320,384]{1,0:T(8,128)(2,1)} %constant.38.clone.order, ...), custom_call_target="tpu_custom_call" | custom-call | flops 100000000 | tf_op jit(solution)/shard_map/pallas_call | solution.py:257
  35.9 0.6 copy-done.4
  36.6 3.4 %shard_map.220 = bf16[16,48,1024]{2,1,0:T(8,128)(2,1)} custom-call(bf16[16,24,128]{2,1,0:T(8,128)(2,1)} %copy-done.4, bf16[8,128,1024]{2,1,0:T(8,128)(2,1)} %constant.40.clone.perm), custom_call_target="tpu_custom_call" | custom-call | tf_op jit(solution)/shard_map/pallas_call | solution.py:262
  40.0 6.6 %all-to-all-start.1 = ((bf16[16,48,1024]{2,1,0:T(8,128)(2,1)}), bf16[16,48,1024]{2,1,0:T(8,128)(2,1)S(1)}, u32[]{:S(2)}, u32[]{:S(2)}) async-start(bf16[16,48,1024]{2,1,0:T(8,128)(2,1)} %shard_map.220), calls=%async_computation.1 | async-start | bytes 3145728 | tf_op jit(solution)/shard_map/all_to_all | solution.py:263
  46.6 2.8 %collective-permute-done.1.frame = bf16[3856,128]{1,0:T(8,128)(2,1)S(1)} collective-permute-done((bf16[3856,128]{1,0:T(8,128)(2,1)}, bf16[3856,128]{1,0:T(8,128)(2,1)S(1)}, u32[]{:S(2)}, u32[]{:S(2)}) %collective-permute-start.1) | collective-permute-done | bytes 987168 | tf_op jit(solution)/shard_map/ppermute | solution.py:255
  49.4 8.6 %shard_map.221 = (bf16[1664,1024]{1,0:T(8,128)(2,1)}, f32[1,384]{1,0:T(1,128)}) custom-call(bf16[3856,128]{1,0:T(8,128)(2,1)} %collective-permute-done.frame, f32[1,320]{1,0:T(1,128)} %reshape.27.gain, f32[1,320]{1,0:T(1,128)} %reshape.28.shift, f32[320,320]{1,0:T(8,128)} %constant.37.clone.same, bf16[320,384]{1,0:T(8,128)(2,1)} %constant.38.clone.order, ...), custom_call_target="tpu_custom_call" | custom-call | flops 7500000256 | tf_op jit(solution)/shard_map/pallas_call | solution.py:257
  58.0 9.9 %all-to-all-done.1.own = bf16[16,48,1024]{2,1,0:T(8,128)(2,1)S(1)} async-done(((bf16[16,48,1024]{2,1,0:T(8,128)(2,1)}), bf16[16,48,1024]{2,1,0:T(8,128)(2,1)S(1)}, u32[]{:S(2)}, u32[]{:S(2)}) %all-to-all-start.1) | async-done | bytes 1572896 | tf_op jit(solution)/shard_map/all_to_all | solution.py:263
  67.8 4.8 %collective-permute-start.2 = (bf16[16,48,1024]{2,1,0:T(8,128)(2,1)S(1)}, bf16[16,48,1024]{2,1,0:T(8,128)(2,1)S(1)}, u32[]{:S(2)}, u32[]{:S(2)}) collective-permute-start(bf16[16,48,1024]{2,1,0:T(8,128)(2,1)S(1)} %all-to-all-done.1.own), channel_id=1, source_target_pairs={{0,32},{32,0},{1,33},{33,1},{2,34},{34,2},{3,35},{35,3},{4,36},{36... | collective-permute-start | bytes 4718600 | tf_op jit(solution)/shard_map/ppermute | solution.py:267
  73.4 0.7 add_convert_fusion.keep
  74.0 1.4 %fusion = f32[8,384]{1,0:T(8,128)S(1)} fusion(f32[320,384]{1,0:T(8,128)} %constant.41.clone, f32[1,320]{1,0:T(1,128)S(1)} %broadcast_in_dim.10, f32[1,320]{1,0:T(1,128)S(1)} %broadcast_in_dim.9, f32[8]{0:T(128)S(1)} %pad.4.clone), kind=kOutput, calls=%fused_computation.1 | convolution fusion | flops 11801600 | bytes 506400 | tf_op jit(solution)/shard_map/dot_general | solution.py:75
  76.0 8.3 %shard_map.222 = (bf16[1664,1024]{1,0:T(8,128)(2,1)}, f32[1,384]{1,0:T(1,128)}) custom-call(bf16[3856,128]{1,0:T(8,128)(2,1)} %copy-done.2, f32[1,320]{1,0:T(1,128)} %reshape.27.gain, f32[1,320]{1,0:T(1,128)} %reshape.28.shift, f32[320,320]{1,0:T(8,128)} %constant.37.clone.same, bf16[320,384]{1,0:T(8,128)(2,1)} %constant.38.clone.order, ...), custom_call_target="tpu_custom_call" | custom-call | flops 100000000 | tf_op jit(solution)/shard_map/pallas_call | solution.py:257
  84.4 1.1 copy-done.1
  85.5 9.5 %shard_map.223 = (bf16[1536,384]{1,0:T(8,128)(2,1)}, f32[32,8,128]{2,1,0:T(8,128)}, bf16[4,384,1024]{2,1,0:T(8,128)(2,1)}) custom-call(s32[1]{0:T(128)} %bitcast.3.core, bf16[1664,1024]{1,0:T(8,128)(2,1)} %get-tuple-element.33.cols, bf16[16,48,1024]{2,1,0:T(8,128)(2,1)} %copy-done, bf16[16,48,1024]{2,1,0:T(8,128)(2,1)} %copy-done.1, ...), custom_call_target="tpu_custom_call" | custom-call | tf_op jit(solution)/shard_map/pallas_call | solution.py:273
  95.0 11.4 %all-to-all-start.2 = ((f32[32,8,128]{2,1,0:T(8,128)}), f32[32,8,128]{2,1,0:T(8,128)S(1)}, u32[]{:S(2)}, u32[]{:S(2)}) async-start(f32[32,8,128]{2,1,0:T(8,128)} %get-tuple-element.42), calls=%async_computation.2 | async-start | bytes 262144 | tf_op jit(solution)/shard_map/all_to_all | solution.py:276
  106.4 5.7 %shard_map.225.w = bf16[320,1536]{1,0:T(8,128)(2,1)} custom-call(f32[2]{0:T(128)} %add_convert_fusion.keep, bf16[4,384,1024]{2,1,0:T(8,128)(2,1)} %get-tuple-element.36.w, bf16[1024,1152]{1,0:T(8,128)(2,1)} %constant.42.clone.perm, bf16[320,384]{1,0:T(8,128)(2,1)} %constant.38.clone.order), custom_call_target="tpu_custom_call" | custom-call | flops 1000000000 | tf_op jit(solution)/shard_map/pallas_call | solution.py:278
  112.1 12.6 %shard_map.224 = (bf16[1536,384]{1,0:T(8,128)(2,1)}, bf16[1536,384]{1,0:T(8,128)(2,1)}) custom-call(bf16[1664,1024]{1,0:T(8,128)(2,1)} %get-tuple-element.28.before, bf16[1664,1024]{1,0:T(8,128)(2,1)} %get-tuple-element.32.after, bf16[4,384,1024]{2,1,0:T(8,128)(2,1)} %get-tuple-element.36.w, f32[1,384]{1,0:T(1,128)} %get-tuple-element.37.emb0, ...), custom_call_target="tpu_custom_call" | custom-call | flops 7299999744 | tf_op jit(solution)/shard_map/pallas_call | solution.py:277
  124.7 0.6 copy-done.3
  125.3 6.7 %shard_map.226 = bf16[1536,320]{1,0:T(8,128)(2,1)} custom-call(bf16[1536,384]{1,0:T(8,128)(2,1)} %get-tuple-element.39.hidden0, bf16[1536,384]{1,0:T(8,128)(2,1)} %get-tuple-element.40.hidden1, bf16[1536,384]{1,0:T(8,128)(2,1)} %get-tuple-element.41.hidden2, f32[32,8,128]{2,1,0:T(8,128)} %copy-done.3, f32[1,384]{1,0:T(1,128)} %get-tuple-element.44.gain, ...), custom_call_target="tpu_custom_call" | custom-call | tf_op jit(solution)/shard_map/pallas_call | solution.py:279
  (29 shorter events, 2.5 us)
Async XLA Ops:
  0.0 26.5 %copy-start.5 = (f32[320]{0:T(512)S(1)}, f32[320]{0:T(512)}, u32[]{:S(2)}) copy-start(f32[320]{0:T(512)} %param.25) | copy-start | bytes 3844
  0.0 27.0 %copy-start.6 = (f32[320]{0:T(512)S(1)}, f32[320]{0:T(512)}, u32[]{:S(2)}) copy-start(f32[320]{0:T(512)} %param.26) | copy-start | bytes 3844
  2.9 33.0 %all-to-all-start = ((bf16[16,24,128]{2,1,0:T(8,128)(2,1)}), bf16[16,24,128]{2,1,0:T(8,128)(2,1)S(1)}, u32[]{:S(2)}, u32[]{:S(2)}) async-start(bf16[16,24,128]{2,1,0:T(8,128)(2,1)} %shard_map.217), calls=%async_computation | async-start | bytes 196608 | tf_op jit(solution)/shard_map/all_to_all | solution.py:253
  21.1 25.6 %collective-permute-start = (bf16[3856,128]{1,0:T(8,128)(2,1)}, bf16[3856,128]{1,0:T(8,128)(2,1)}, u32[]{:S(2)}, u32[]{:S(2)}) collective-permute-start(bf16[3856,128]{1,0:T(8,128)(2,1)} %shard_map.218.frame), channel_id=1, source_target_pairs={{0,1},{1,2},{2,3},{3,4},{4,5},{5,6},{6,7},{7,8},{8,9},{9,10},{10,1... | collective-permute-start | bytes 2961416 | tf_op jit(solution)/shard_map/ppermute | solution.py:254
  25.2 24.2 %collective-permute-start.1 = (bf16[3856,128]{1,0:T(8,128)(2,1)}, bf16[3856,128]{1,0:T(8,128)(2,1)S(1)}, u32[]{:S(2)}, u32[]{:S(2)}) collective-permute-start(bf16[3856,128]{1,0:T(8,128)(2,1)} %shard_map.218.frame), channel_id=1, source_target_pairs={{1,0},{2,1},{3,2},{4,3},{5,4},{6,5},{7,6},{8,7},{9,8},{10,9},{11,1... | collective-permute-start | bytes 2961416 | tf_op jit(solution)/shard_map/ppermute | solution.py:255
  35.9 0.6 copy-start.4
  40.0 27.9 %all-to-all-start.1 = ((bf16[16,48,1024]{2,1,0:T(8,128)(2,1)}), bf16[16,48,1024]{2,1,0:T(8,128)(2,1)S(1)}, u32[]{:S(2)}, u32[]{:S(2)}) async-start(bf16[16,48,1024]{2,1,0:T(8,128)(2,1)} %shard_map.220), calls=%async_computation.1 | async-start | bytes 3145728 | tf_op jit(solution)/shard_map/all_to_all | solution.py:263
  46.6 26.1 %copy-start.7 = (f32[320]{0:T(512)S(1)}, f32[320]{0:T(512)}, u32[]{:S(2)}) copy-start(f32[320]{0:T(512)} %param.28) | copy-start | bytes 3844
  46.6 26.1 %copy-start.8 = (f32[320]{0:T(512)S(1)}, f32[320]{0:T(512)}, u32[]{:S(2)}) copy-start(f32[320]{0:T(512)} %param.27) | copy-start | bytes 3844
  46.6 26.1 %copy-start.9 = (f32[320]{0:T(512)S(1)}, f32[320]{0:T(512)}, u32[]{:S(2)}) copy-start(f32[320]{0:T(512)} %param.31) | copy-start | bytes 3844
  49.4 8.6 %copy-start.2 = (bf16[3856,128]{1,0:T(8,128)(2,1)}, bf16[3856,128]{1,0:T(8,128)(2,1)S(1)}, u32[]{:S(2)}) copy-start(bf16[3856,128]{1,0:T(8,128)(2,1)S(1)} %collective-permute-done.1.frame) | copy-start | bytes 2961412
  67.8 16.5 %copy-start = (bf16[16,48,1024]{2,1,0:T(8,128)(2,1)}, bf16[16,48,1024]{2,1,0:T(8,128)(2,1)S(1)}, u32[]{:S(2)}) copy-start(bf16[16,48,1024]{2,1,0:T(8,128)(2,1)S(1)} %all-to-all-done.1.own) | copy-start | bytes 4718596
  67.8 16.5 %collective-permute-start.2 = (bf16[16,48,1024]{2,1,0:T(8,128)(2,1)S(1)}, bf16[16,48,1024]{2,1,0:T(8,128)(2,1)S(1)}, u32[]{:S(2)}, u32[]{:S(2)}) collective-permute-start(bf16[16,48,1024]{2,1,0:T(8,128)(2,1)S(1)} %all-to-all-done.1.own), channel_id=1, source_target_pairs={{0,32},{32,0},{1,33},{33,1},{2,34},{34,2},{3,35},{35,3},{4,36},{36... | collective-permute-start | bytes 4718600 | tf_op jit(solution)/shard_map/ppermute | solution.py:267
  84.4 1.2 copy-start.1
  95.0 29.7 %all-to-all-start.2 = ((f32[32,8,128]{2,1,0:T(8,128)}), f32[32,8,128]{2,1,0:T(8,128)S(1)}, u32[]{:S(2)}, u32[]{:S(2)}) async-start(f32[32,8,128]{2,1,0:T(8,128)} %get-tuple-element.42), calls=%async_computation.2 | async-start | bytes 262144 | tf_op jit(solution)/shard_map/all_to_all | solution.py:276
  124.7 0.6 copy-start.3

commit v3 on v2

v3 whole, which is shorter than its diff:
```python
import functools

import jax
import jax.numpy as jnp
import numpy as np
from jax import lax
from jax.experimental import pallas as pl
from jax.experimental.pallas import tpu as pltpu
from jax.sharding import Mesh, PartitionSpec as P

GROUPS = 32
C = 320
CELLS = 1536
COLS = 64
EPS = 1e-5
BF = jnp.bfloat16
F32 = jnp.float32
KPAD = 1024
CPAD = 384
HALF = 192
PACKED = CELLS * 5 // 2 + 16
VMEM = 60 * 1024 * 1024


def _consts():
    act_perm = np.zeros((KPAD, KPAD), np.float32)
    for f in range(32):
        zl, x = divmod(f, 4)
        for kk in range(30):
            b, i = divmod(30 * f + kk, C)
            row = 256 * b + i if i < 256 else 768 + 64 * b + i - 256
            act_perm[row, 256 * x + 30 * zl + kk] = 1
    chan = np.zeros(C, np.int64)
    for i in range(C):
        d, j = divmod(i, 20)
        y, zh, core = d // 4, (d // 2) % 2, d % 2
        chan[i] = HALF * core + 48 * y + 24 * zh + j
    order = np.zeros((C, CPAD), np.float32)
    order[np.arange(C), chan] = 1
    temp_perm = np.zeros((KPAD, 3 * CPAD), np.float32)
    for x in range(4):
        for t in range(3):
            for zl in range(8):
                for kk in range(10):
                    i = 40 * zl + 10 * x + kk
                    temp_perm[256 * x + 30 * zl + 10 * t + kk, CPAD * t + chan[i]] = 1
    same1 = np.kron(np.eye(GROUPS), np.ones((10, 10))).astype(np.float32)
    same2 = order.T @ same1 @ order
    return act_perm, order, temp_perm, same1, same2


ACT_PERM, ORDER, TEMP_PERM, SAME1, SAME2 = _consts()


def call(kernel, out_shape, ins, outs=None, scratch=(), flops=0, vmem=VMEM):
    space = {"v": pltpu.VMEM, "a": pl.ANY}
    specs = lambda letters: [pl.BlockSpec(memory_space=space[c]) for c in letters]
    outs = specs(outs or "v" * len(out_shape))
    return pl.pallas_call(
        kernel,
        out_shape=tuple(out_shape),
        in_specs=specs(ins),
        out_specs=tuple(outs),
        scratch_shapes=list(scratch),
        compiler_params=pltpu.CompilerParams(vmem_limit_bytes=vmem),
        cost_estimate=pl.CostEstimate(flops=flops, bytes_accessed=0, transcendentals=0),
    )


class Mover:
    def __init__(self, sems):
        self.sems, self.used = sems, 0

    def start(self, src, dst):
        copy = pltpu.make_async_copy(src, dst, self.sems.at[self.used])
        self.used += 1
        copy.start()
        return copy


def exact(a, b):
    return jnp.dot(a, b, precision=lax.Precision.HIGHEST, preferred_element_type=F32)


def nt(a, b):
    return lax.dot_general(a, b, (((1,), (1,)), ((), ())), preferred_element_type=F32)


def silu(v):
    half = 0.5 * v
    return half + half * jnp.tanh(half)


def pack_kernel(sw, tw, out):
    lane = lax.broadcasted_iota(jnp.int32, (30, 128), 1)
    row = lax.broadcasted_iota(jnp.int32, (30, 128), 0)
    total = jnp.zeros((20, 128), F32)
    for a in range(3):
        total += jnp.dot(sw[a], (lane == row + 30 * a).astype(F32).astype(BF), preferred_element_type=F32)
    rows = jnp.concatenate([tw[r].astype(F32) for r in range(10)], axis=0).astype(BF)
    spread = (lane == 90 + 10 * lax.rem(row, 3) + lax.div(row, 3)).astype(F32).astype(BF)
    total += lax.dot_general(rows, spread, (((0,), (0,)), ((), ())), preferred_element_type=F32)
    piece = jnp.concatenate([total, jnp.zeros((4, 128), F32)], axis=0).astype(BF)
    for n in range(16):
        out[n] = piece


def frame_kernel(video, emb, out):
    out[pl.ds(0, CELLS), :] = video[:, 0:128]
    out[pl.ds(CELLS, CELLS), :] = video[:, 128:256]
    out[pl.ds(2 * CELLS, CELLS // 2), :] = jnp.concatenate(
        [video[: CELLS // 2, 256:320], video[CELLS // 2 :, 256:320]], axis=1
    )
    rest = jnp.concatenate([emb[0], jnp.zeros((1, 64), F32)], axis=1)
    rows = []
    for n in range(3):
        part = rest.astype(BF).astype(F32)
        rest = rest - part
        rows += [part[:, 0:128], part[:, 128:256], part[:, 256:384]]
    rows.append(jnp.zeros((7, 128), F32))
    out[pl.ds(PACKED - 16, 16), :] = jnp.concatenate(rows, axis=0).astype(BF)


def line_kernel(pieces, out):
    both = [jnp.concatenate([pieces[zl].astype(F32), pieces[8 + zl].astype(F32)], axis=0) for zl in range(8)]
    pad = jnp.zeros((48, 16), F32)
    groups = [jnp.concatenate([b[:, 30 * a : 30 * a + 30] for b in both] + [pad], axis=1) for a in range(4)]
    block = jnp.concatenate(groups, axis=1).astype(BF)
    for n in range(16):
        out[n] = block


def act_kernel(*refs):
    count = (len(refs) - 8) // 3
    frames = refs[:count]
    gain, shift, same, order, perm_hbm = refs[count : count + 5]
    outs = refs[count + 5 : 3 * count + 5]
    perm, out, sems = refs[3 * count + 5 :]
    move = Mover(sems)
    perm_copy = move.start(perm_hbm, perm)
    chunk = 256
    half = CELLS // 2
    column = lax.rem(lax.broadcasted_iota(jnp.int32, (chunk, 256), 0), COLS)
    low = lax.broadcasted_iota(jnp.int32, (chunk, 128), 1) < 64
    cells = CELLS * C // GROUPS

    def shifted(v):
        edge = column[:, : v.shape[1]]
        before = jnp.where(edge == 0, 0.0, pltpu.roll(v, 1, 0))
        after = jnp.where(edge == COLS - 1, 0.0, pltpu.roll(v, chunk - 1, 0))
        return before, v, after

    copies = []
    for f, frame in enumerate(frames):
        main = lambda i: jnp.concatenate(
            [frame[pl.ds(i * chunk, chunk), :], frame[pl.ds(CELLS + i * chunk, chunk), :]], axis=1
        ).astype(F32)
        rest = lambda i: frame[pl.ds(2 * CELLS + i * chunk, chunk), :].astype(F32)
        s = jnp.zeros((8, 256), F32)
        q = jnp.zeros((8, 256), F32)
        for i in range(CELLS // chunk):
            v = main(i).reshape(chunk // 8, 8, 256)
            s, q = s + jnp.sum(v, axis=0), q + jnp.sum(v * v, axis=0)
        s2 = jnp.zeros((8, 128), F32)
        q2 = jnp.zeros((8, 128), F32)
        for i in range(half // chunk):
            v = rest(i).reshape(chunk // 8, 8, 128)
            s2, q2 = s2 + jnp.sum(v, axis=0), q2 + jnp.sum(v * v, axis=0)
        s = jnp.concatenate([s, s2[:, :64] + s2[:, 64:]], axis=1)
        q = jnp.concatenate([q, q2[:, :64] + q2[:, 64:]], axis=1)
        both = exact(jnp.concatenate([s, q], axis=0), same[...]) / cells
        mean = jnp.sum(both[:8], axis=0, keepdims=True)
        square = jnp.sum(both[8:], axis=0, keepdims=True)
        scale = lax.rsqrt(square - mean * mean + EPS) * gain[...].reshape(1, C)
        offset = shift[...].reshape(1, C) - mean * scale
        scale2 = jnp.concatenate([scale[:, 256:], scale[:, 256:]], axis=1)
        offset2 = jnp.concatenate([offset[:, 256:], offset[:, 256:]], axis=1)
        scale, offset = scale[:, :256], offset[:, :256]
        rows = frame[pl.ds(PACKED - 16, 16), :].astype(F32)
        parts = [
            jnp.concatenate([rows[n : n + 1], rows[n + 1 : n + 2], rows[n + 2 : n + 3, :64]], axis=1) for n in (0, 3, 6)
        ]
        parts = jnp.concatenate(parts + [jnp.zeros((5, C), F32)], axis=0).astype(BF)
        outs[2 * f + 1][...] = jnp.sum(jnp.dot(parts, order[...], preferred_element_type=F32), axis=0, keepdims=True)
        out[f, pl.ds(0, COLS), :] = jnp.zeros((COLS, KPAD), BF)
        out[f, pl.ds(CELLS + COLS, COLS), :] = jnp.zeros((COLS, KPAD), BF)
        if f == 0:
            perm_copy.wait()
        for i in range(half // chunk):
            before2, v2, after2 = shifted(silu(rest(i) * scale2 + offset2).astype(BF).astype(F32))
            swap = lambda v: pltpu.roll(v, 64, 1)
            tails = [
                (jnp.where(low, before2, swap(v2)), jnp.where(low, after2, 0.0)),
                (jnp.where(low, swap(before2), v2), jnp.where(low, swap(after2), 0.0)),
            ]
            for n in range(2):
                at = i + n * (half // chunk)
                taps = shifted(silu(main(at) * scale + offset).astype(BF).astype(F32))
                taps = jnp.concatenate(taps + tails[n], axis=1).astype(BF)
                total = jnp.dot(taps, perm[...], preferred_element_type=F32)
                out[f, pl.ds(at * chunk + COLS, chunk), :] = total.astype(BF)
        copies.append(move.start(out.at[f], outs[2 * f]))
    for copy in copies:
        copy.wait()


def place_weights(half, block, w):
    for y in range(4):
        for x in range(4):
            for a in range(4):
                rows = pl.ds(pl.multiple_of(half + 48 * y, 16), 48)
                w[a, rows, 256 * x : 256 * x + 256] = block[4 * y + x, :, 256 * a : 256 * a + 256]


def convolve(i, cols, w, emb):
    total = jnp.zeros((CPAD, 256), F32)
    for a in range(3):
        total += nt(w[a], cols[pl.ds(i * 256 + COLS * a, 256), :])
    return (total.T + emb).astype(BF)


def own_kernel(cols_hbm, own_hbm, other_hbm, emb, hidden_hbm, stats, w_hbm, cols, own, other, hidden, w, sems):
    move = Mover(sems)
    own_copy = move.start(own_hbm, own)
    other_copy = move.start(other_hbm, other)
    cols_copy = move.start(cols_hbm, cols)
    mine = lax.axis_index("core") * HALF
    own_copy.wait()
    place_weights(mine, own, w)
    other_copy.wait()
    place_weights(HALF - mine, other, w)
    cols_copy.wait()
    copies = [move.start(w, w_hbm)]
    s = jnp.zeros((8, CPAD), F32)
    q = jnp.zeros((8, CPAD), F32)
    for i in range(CELLS // 256):
        h = convolve(i, cols, w, emb[...])
        hidden[pl.ds(i * 256, 256), :] = h
        h = h.astype(F32).reshape(32, 8, CPAD)
        s, q = s + jnp.sum(h, axis=0), q + jnp.sum(h * h, axis=0)
    copies.append(move.start(hidden, hidden_hbm))
    s = jnp.sum(s, axis=0, keepdims=True)
    q = jnp.sum(q, axis=0, keepdims=True)
    rows = [s[:, :128], s[:, 128:256], s[:, 256:], q[:, :128], q[:, 128:256], q[:, 256:], jnp.zeros((2, 128), F32)]
    block = jnp.concatenate(rows, axis=0)
    for n in range(32):
        stats[n] = block
    for copy in copies:
        copy.wait()


def temporal_kernel(w_hbm, perm, order, gain, shift, out, affine, w, sems):
    move = Mover(sems)
    move.start(w_hbm.at[3], w).wait()
    frame = lax.axis_index("zl") * 4 + lax.axis_index("x")
    keep = [(frame > 0).astype(F32), 1.0, (frame < 31).astype(F32)]
    for t in range(3):
        part = jnp.dot(w[...], perm[:, CPAD * t : CPAD * t + CPAD], preferred_element_type=F32).astype(BF)
        part = jnp.dot(order[...], part, preferred_element_type=F32) * keep[t]
        out[:, CPAD * t : CPAD * t + CPAD] = part.astype(BF)
    out[:, 3 * CPAD :] = order[...]
    rest = jnp.concatenate([gain[...].reshape(1, C), shift[...].reshape(1, C), jnp.zeros((6, C), F32)], axis=0)
    total = jnp.zeros((8, CPAD), F32)
    for n in range(3):
        part = rest.astype(BF)
        rest = rest - part.astype(F32)
        total += jnp.dot(part, order[...], preferred_element_type=F32)
    affine[...] = total


def final_kernel(
    cols0_hbm, cols2_hbm, w_hbm, hidden_hbm, last_hbm, emb0, emb2, stats, affine, same, bias, out_hbm,
    cols0, cols2, w, hidden, last, out, sems,
):
    move = Mover(sems)
    first, second = pl.ds(0, 1024), pl.ds(1024, CELLS + 2 * COLS - 1024)
    begin = [move.start(w_hbm.at[pl.ds(0, 3)], w)]
    begin += [move.start(h.at[first], c.at[first]) for h, c in ((cols0_hbm, cols0), (cols2_hbm, cols2))]
    begin += [move.start(hidden_hbm, hidden), move.start(last_hbm, last)]
    later = [move.start(h.at[second], c.at[second]) for h, c in ((cols0_hbm, cols0), (cols2_hbm, cols2))]
    total = stats[0]
    for n in range(1, 32):
        total = total + stats[n]
    s = jnp.concatenate([total[0:1], total[1:2], total[2:3]], axis=1)
    q = jnp.concatenate([total[3:4], total[4:5], total[5:6]], axis=1)
    both = jnp.concatenate([s, q, jnp.zeros((6, CPAD), F32)], axis=0)
    both = exact(both, same[...]) / (CELLS * 32 * C // GROUPS)
    mean, square = both[0:1], both[1:2]
    scale = lax.rsqrt(square - mean * mean + EPS) * affine[0:1]
    offset = affine[1:2] - mean * scale
    bias_row = bias[...].reshape(1, C)
    mix = lambda h: silu(h.astype(F32) * scale + offset).astype(BF)
    for copy in begin:
        copy.wait()
    near = lambda i: (convolve(i, cols0, w, emb0[...]), convolve(i, cols2, w, emb2[...]))
    now = near(0)
    copies = []
    for i in range(CELLS // 256):
        if i == 2:
            for copy in later:
                copy.wait()
        later_now = near(i + 1) if i < CELLS // 256 - 1 else None
        here = pl.ds(i * 256, 256)
        h = hidden[here, :]
        taps = jnp.concatenate([mix(now[0]), mix(h), mix(now[1]), h], axis=1)
        out[here, :] = (nt(taps, last[...]) + bias_row).astype(BF)
        now = later_now
        if i == 2:
            copies.append(move.start(out.at[pl.ds(0, 768)], out_hbm.at[pl.ds(0, 768)]))
    copies.append(move.start(out.at[pl.ds(768, 768)], out_hbm.at[pl.ds(768, 768)]))
    for copy in copies:
        copy.wait()


FILL = 15_000_000_000
FRAME = ("zl", "x")
FORWARD = [(i, i + 1) for i in range(31)]
BACKWARD = [(i + 1, i) for i in range(31)]


def body(video, emb, gain1, shift1, gain2, shift2, sw, tw, bias):
    struct = jax.ShapeDtypeStruct
    const = lambda a, t=BF: jnp.asarray(a, t)
    sems = pltpu.SemaphoreType.DMA
    buffer = lambda *shape: pltpu.VMEM(shape, BF)
    cols = (CELLS + 2 * COLS, KPAD)

    (pieces,) = call(pack_kernel, [struct((16, 24, 128), BF)], "vv")(sw.transpose(0, 2, 1), tw.transpose(1, 0, 2))
    (frame1,) = call(frame_kernel, [struct((PACKED, 128), BF)], "vv")(video.reshape(CELLS, C), emb)
    line = lax.all_to_all(pieces, ("zh", "zl"), 0, 0)
    frame0 = lax.ppermute(frame1, FRAME, FORWARD)
    frame2 = lax.ppermute(frame1, FRAME, BACKWARD)

    act = lambda frames, flops=100_000_000: call(
        act_kernel,
        [struct(cols, BF), struct((1, CPAD), F32)] * len(frames),
        "v" * len(frames) + "vvvva",
        "av" * len(frames),
        [buffer(KPAD, KPAD), buffer(len(frames), *cols), sems((1 + len(frames),))],
        flops,
    )(*frames, gain1, shift1, const(SAME1, F32), const(ORDER), const(ACT_PERM))
    cols1, emb1 = act([frame1])
    line, cols1 = lax.optimization_barrier((line, cols1))
    (block,) = call(line_kernel, [struct((16, 48, KPAD), BF)], "v")(line)
    own = lax.all_to_all(block, ("y", "x"), 0, 0)
    cols0, emb0, cols2, emb2 = act([frame0, frame2], FILL)
    own, cols0 = lax.optimization_barrier((own, cols0))
    other = lax.ppermute(own, "core", [(0, 1), (1, 0)])

    blocks = (16, 48, KPAD)
    hidden1, stats, w = call(
        own_kernel,
        [struct((CELLS, CPAD), BF), struct((32, 8, 128), F32), struct((4, CPAD, KPAD), BF)],
        "aaav",
        "ava",
        [buffer(*cols), buffer(*blocks), buffer(*blocks), buffer(CELLS, CPAD), buffer(4, CPAD, KPAD), sems((5,))],
    )(cols1, own, other, emb1)
    stats = lax.all_to_all(stats, FRAME, 0, 0)
    last, affine = call(
        temporal_kernel,
        [struct((C, 4 * CPAD), BF), struct((8, CPAD), F32)],
        "avvvv",
        scratch=[buffer(CPAD, KPAD), sems((1,))],
        flops=3_000_000_000,
    )(w, const(TEMP_PERM), const(ORDER), gain2, shift2)
    (out,) = call(
        final_kernel,
        [struct((CELLS, C), BF)],
        "aaaaavvvvvv",
        "a",
        [
            buffer(*cols),
            buffer(*cols),
            buffer(3, CPAD, KPAD),
            buffer(CELLS, CPAD),
            buffer(C, 4 * CPAD),
            buffer(CELLS, C),
            sems((9,)),
        ],
    )(cols0, cols2, w, hidden1, last, emb0, emb2, stats, affine, const(SAME2, F32), bias)
    return out.reshape(video.shape)


def solution(mesh):
    split = Mesh(mesh.devices.reshape(4, 2, 2, 8, 4), ("y", "zh", "core", "zl", "x"))
    dp = ("y", "zh", "core")
    data = P(dp, FRAME, None, None, None)
    placed = (data, P(dp, FRAME, None), P(), P(), P(), P(), P(None, FRAME, dp), P(None, FRAME, dp), P())
    return jax.shard_map(body, mesh=split, in_specs=placed, out_specs=data, check_vma=False)
```

time: 133 us -> 131 us (0.985)
  Pallas kernels: 67 us -> 60.2 us
  waiting for transfers between devices: 12.6 us -> 18.7 us
  starting transfers between devices: 43.9 us -> 46.9 us
  local copies, waits for them, and re-layouts: 6.2 us -> 4.35 us
  matrix products: 1.4 us -> 0 us
    all_to_all x1, starting transfers between devices: 11.4 us -> 4.09 us  [body(): stats = lax.all_to_all(stats, FRAME, 0, 0)]
    pallas_call x10 -> x8, Pallas kernels: 67 us -> 60.2 us  [the longest x2 22.3 us: body(): call(act_kernel, [struct(cols, BF), struct((1, CPAD), F32)] * len(frames)...]
    all_to_all x1, starting transfers between devices: 6.59 us -> 13.3 us  [body(): own = lax.all_to_all(block, ('y', 'x'), 0, 0)]
    all_to_all x1, waiting for transfers between devices: 0.01 us -> 5.81 us  [body(): stats = lax.all_to_all(stats, FRAME, 0, 0)]
    all_to_all x1, waiting for transfers between devices: 0.01 us -> 5.74 us  [body(): line = lax.all_to_all(pieces, ('zh', 'zl'), 0, 0)]
    all_to_all x1, waiting for transfers between devices: 9.86 us -> 4.16 us  [body(): own = lax.all_to_all(block, ('y', 'x'), 0, 0)]
    ppermute x1, waiting for transfers between devices: 0.01 us -> 3.01 us  [body(): other = lax.ppermute(own, 'core', [(0, 1), (1, 0)])]
    ppermute x1, waiting for transfers between devices: 2.77 us -> 0.01 us  [body(): frame2 = lax.ppermute(frame1, FRAME, BACKWARD)]
  transfers between devices with their start and end apart: 6 -> 6, of which waited for: 2 -> 4; matrix products, arithmetic and copies ran while one was open for 3% -> 0% of each run, Pallas kernels for 37% -> 25%
where the time goes in v3:
time: 131 us; the launch traced here: 130 us
  Pallas kernels  60.2 us (46%)
  starting transfers between devices  46.9 us (36%)
  waiting for transfers between devices  18.7 us (14%)
  local copies, waits for them, and re-layouts  4.35 us (3%)
    pallas_call x2, Pallas kernels, body(): call(act_kernel, [struct(cols, BF), struct((1, CPAD), F32)] * len(frames)...  22.3 us
    pallas_call x1, Pallas kernels, body(): call(final_kernel, [struct((CELLS, C), BF)], 'aaaaavvvvvv', 'a', [buffer(...  16.2 us
    all_to_all x1, starting transfers between devices, body(): line = lax.all_to_all(pieces, ('zh', 'zl'), 0, 0)  16.1 us
    all_to_all x1, starting transfers between devices, body(): own = lax.all_to_all(block, ('y', 'x'), 0, 0)  13.3 us
    pallas_call x1, Pallas kernels, body(): call(own_kernel, [struct((CELLS, CPAD), BF), struct((32, 8, 128), F32), s...  9.35 us
    ppermute x1, starting transfers between devices, body(): other = lax.ppermute(own, 'core', [(0, 1), (1, 0)])  7.47 us
    pallas_call x1, Pallas kernels, body(): call(temporal_kernel, [struct((C, 4 * CPAD), BF), struct((8, CPAD), F32)]...  6.09 us
    all_to_all x1, waiting for transfers between devices, body(): stats = lax.all_to_all(stats, FRAME, 0, 0)  5.81 us
  transfers between devices with their start and end apart: 6, of which 4 were waited for; matrix products, arithmetic and copies ran while one was open for 0% of the time, Pallas kernels for 25%

profile of v3, /device:TPU:1, one launch (start us, length us, event | category | flops | bytes accessed | tf_op | source)
XLA Modules:
  0.0 130.4 jit_solution(520472623400885253)
XLA Ops:
  0.0 2.4 %shard_map.173.refs_0_ = bf16[3856,128]{1,0:T(8,128)(2,1)} custom-call(bf16[1536,320]{1,0:T(8,128)(2,1)} %bitcast.4, f32[1,1,320]{2,1,0:T(1,128)} %emb.1), custom_call_target="tpu_custom_call" | custom-call | tf_op jit(solution)/shard_map/pallas_call | solution.py:329
  2.4 1.3 collective-permute-start.1
  3.7 4.6 %collective-permute-start = (bf16[3856,128]{1,0:T(8,128)(2,1)}, bf16[3856,128]{1,0:T(8,128)(2,1)S(1)}, u32[]{:S(2)}, u32[]{:S(2)}) collective-permute-start(bf16[3856,128]{1,0:T(8,128)(2,1)} %shard_map.173.refs_0_), channel_id=1, source_target_pairs={{0,1},{1,2},{2,3},{3,4},{4,5},{5,6},{6,7},{7,8},{8,9},{9,10},{10,1... | collective-permute-start | bytes 2961416 | tf_op jit(solution)/shard_map/ppermute | solution.py:331
  8.3 1.6 %shard_map.172 = bf16[16,24,128]{2,1,0:T(8,128)(2,1)} custom-call(bf16[3,20,30]{2,1,0:T(8,128)(2,1)} %bitcast.5, bf16[10,3,20]{2,1,0:T(4,128)(2,1)} %bitcast.6), custom_call_target="tpu_custom_call" | custom-call | tf_op jit(solution)/shard_map/pallas_call | solution.py:328
  9.9 16.1 %all-to-all-start = ((bf16[16,24,128]{2,1,0:T(8,128)(2,1)}), bf16[16,24,128]{2,1,0:T(8,128)(2,1)S(1)}, u32[]{:S(2)}, u32[]{:S(2)}) async-start(bf16[16,24,128]{2,1,0:T(8,128)(2,1)} %shard_map.172), calls=%async_computation | async-start | bytes 196608 | tf_op jit(solution)/shard_map/all_to_all | solution.py:330
  26.0 8.9 %shard_map.174 = (bf16[1664,1024]{1,0:T(8,128)(2,1)}, f32[1,384]{1,0:T(1,128)}) custom-call(bf16[3856,128]{1,0:T(8,128)(2,1)} %shard_map.173.refs_0_, f32[320]{0:T(512)} %refs_2_.3, f32[320]{0:T(512)} %refs_3_.2, f32[320,320]{1,0:T(8,128)} %constant.10.clone.refs_3_.refs_4_, bf16[320,384]{1,0:T(8,128)(2,1)} %constant.11.clone.refs_4_.refs_5_.order, ...), custom_call_target="tpu_custom_call" | custom-call | flops 100000000 | tf_op jit(solution)/shard_map/pallas_call | solution.py:334
  35.0 5.7 %all-to-all-done.pieces = bf16[16,24,128]{2,1,0:T(8,128)(2,1)S(1)} async-done(((bf16[16,24,128]{2,1,0:T(8,128)(2,1)}), bf16[16,24,128]{2,1,0:T(8,128)(2,1)S(1)}, u32[]{:S(2)}, u32[]{:S(2)}) %all-to-all-start) | async-done | bytes 98336 | tf_op jit(solution)/shard_map/all_to_all | solution.py:330
  40.7 0.6 copy-done.3
  41.4 2.3 %shard_map.175 = bf16[16,48,1024]{2,1,0:T(8,128)(2,1)} custom-call(bf16[16,24,128]{2,1,0:T(8,128)(2,1)} %copy-done.3), custom_call_target="tpu_custom_call" | custom-call | tf_op jit(solution)/shard_map/pallas_call | solution.py:344
  43.7 13.3 %all-to-all-start.1 = ((bf16[16,48,1024]{2,1,0:T(8,128)(2,1)}), bf16[16,48,1024]{2,1,0:T(8,128)(2,1)S(1)}, u32[]{:S(2)}, u32[]{:S(2)}) async-start(bf16[16,48,1024]{2,1,0:T(8,128)(2,1)} %shard_map.175), calls=%async_computation.1 | async-start | bytes 3145728 | tf_op jit(solution)/shard_map/all_to_all | solution.py:345
  57.0 0.0 collective-permute-done.refs_0_
  57.0 1.0 copy-done.4
  58.0 0.9 copy-done.5
  58.9 13.3 %shard_map.176 = (bf16[1664,1024]{1,0:T(8,128)(2,1)}, f32[1,384]{1,0:T(1,128)}, bf16[1664,1024]{1,0:T(8,128)(2,1)}, f32[1,384]{1,0:T(1,128)}) custom-call(bf16[3856,128]{1,0:T(8,128)(2,1)} %copy-done.5, bf16[3856,128]{1,0:T(8,128)(2,1)} %copy-done.4, f32[320]{0:T(512)} %refs_2_.3, f32[320]{0:T(512)} %refs_3_.2, f32[320,320]{1,0:T(8,128)} %constant.10.clone.refs_3_.refs_4_, ...), custom_call_target="tpu_custom_call" | custom-call | flops 15000000512 | tf_op jit(solution)/shard_map/pallas_call | solution.py:334
  72.2 4.2 %all-to-all-done.1.own_hbm = bf16[16,48,1024]{2,1,0:T(8,128)(2,1)S(1)} async-done(((bf16[16,48,1024]{2,1,0:T(8,128)(2,1)}), bf16[16,48,1024]{2,1,0:T(8,128)(2,1)S(1)}, u32[]{:S(2)}, u32[]{:S(2)}) %all-to-all-start.1) | async-done | bytes 1572896 | tf_op jit(solution)/shard_map/all_to_all | solution.py:345
  76.4 7.5 %collective-permute-start.2 = (bf16[16,48,1024]{2,1,0:T(8,128)(2,1)S(1)}, bf16[16,48,1024]{2,1,0:T(8,128)(2,1)S(1)}, u32[]{:S(2)}, u32[]{:S(2)}) collective-permute-start(bf16[16,48,1024]{2,1,0:T(8,128)(2,1)S(1)} %all-to-all-done.1.own_hbm), channel_id=1, source_target_pairs={{0,32},{32,0},{1,33},{33,1},{2,34},{34,2},{3,35},{35,3},{4,36},{36... | collective-permute-start | bytes 4718600 | tf_op jit(solution)/shard_map/ppermute | solution.py:348
  83.9 3.0 %collective-permute-done.2.other_hbm = bf16[16,48,1024]{2,1,0:T(8,128)(2,1)S(1)} collective-permute-done((bf16[16,48,1024]{2,1,0:T(8,128)(2,1)S(1)}, bf16[16,48,1024]{2,1,0:T(8,128)(2,1)S(1)}, u32[]{:S(2)}, u32[]{:S(2)}) %collective-permute-start.2) | collective-permute-done | bytes 1572896 | tf_op jit(solution)/shard_map/ppermute | solution.py:348
  86.9 1.2 copy-done.1
  88.0 9.3 %shard_map.177 = (bf16[1536,384]{1,0:T(8,128)(2,1)}, f32[32,8,128]{2,1,0:T(8,128)}, bf16[4,384,1024]{2,1,0:T(8,128)(2,1)}) custom-call(bf16[1664,1024]{1,0:T(8,128)(2,1)} %get-tuple-element.25.cols_hbm, bf16[16,48,1024]{2,1,0:T(8,128)(2,1)} %copy-done, bf16[16,48,1024]{2,1,0:T(8,128)(2,1)} %copy-done.1, f32[1,384]{1,0:T(1,128)} %get-tuple-element.27.emb), custom_call_target="tpu_custom_call" | custom-call | tf_op jit(solution)/shard_map/pallas_call | solution.py:351
  97.4 4.1 %all-to-all-start.2 = ((f32[32,8,128]{2,1,0:T(8,128)}), f32[32,8,128]{2,1,0:T(8,128)S(1)}, u32[]{:S(2)}, u32[]{:S(2)}) async-start(f32[32,8,128]{2,1,0:T(8,128)} %get-tuple-element.33), calls=%async_computation.2 | async-start | bytes 262144 | tf_op jit(solution)/shard_map/all_to_all | solution.py:358
  101.5 6.1 %shard_map.178 = (bf16[320,1536]{1,0:T(8,128)(2,1)}, f32[8,384]{1,0:T(8,128)}) custom-call(bf16[4,384,1024]{2,1,0:T(8,128)(2,1)} %get-tuple-element.28.w_hbm, bf16[1024,1152]{1,0:T(8,128)(2,1)} %constant.13.clone.perm, bf16[320,384]{1,0:T(8,128)(2,1)} %constant.11.clone.refs_4_.refs_5_.order, f32[320]{0:T(512)} %gain.1, f32[320]{0:T(512)} %shift.1), custom_call_target="tpu_custom_call" | custom-call | flops 3000000000 | tf_op jit(solution)/shard_map/pallas_call | solution.py:359
  107.6 5.8 %all-to-all-done.2.stats = f32[32,8,128]{2,1,0:T(8,128)S(1)} async-done(((f32[32,8,128]{2,1,0:T(8,128)}), f32[32,8,128]{2,1,0:T(8,128)S(1)}, u32[]{:S(2)}, u32[]{:S(2)}) %all-to-all-start.2) | async-done | bytes 131104 | tf_op jit(solution)/shard_map/all_to_all | solution.py:358
  113.4 0.6 copy-done.2
  114.1 16.2 %shard_map.179 = bf16[1536,320]{1,0:T(8,128)(2,1)} custom-call(bf16[1664,1024]{1,0:T(8,128)(2,1)} %get-tuple-element.23.cols0_hbm, bf16[1664,1024]{1,0:T(8,128)(2,1)} %get-tuple-element.24.cols2_hbm, bf16[4,384,1024]{2,1,0:T(8,128)(2,1)} %get-tuple-element.28.w_hbm, bf16[1536,384]{1,0:T(8,128)(2,1)} %get-tuple-element.29.hidden_hbm, ...), custom_call_target="tpu_custom_call" | custom-call | tf_op jit(solution)/shard_map/pallas_call | solution.py:366
  (8 shorter events, 0.0 us)
Async XLA Ops:
  2.4 54.6 %collective-permute-start.1 = (bf16[3856,128]{1,0:T(8,128)(2,1)}, bf16[3856,128]{1,0:T(8,128)(2,1)S(1)}, u32[]{:S(2)}, u32[]{:S(2)}) collective-permute-start(bf16[3856,128]{1,0:T(8,128)(2,1)} %shard_map.173.refs_0_), channel_id=1, source_target_pairs={{1,0},{2,1},{3,2},{4,3},{5,4},{6,5},{7,6},{8,7},{9,8},{10,9},{11,1... | collective-permute-start | bytes 2961416 | tf_op jit(solution)/shard_map/ppermute | solution.py:332
  3.7 53.3 %collective-permute-start = (bf16[3856,128]{1,0:T(8,128)(2,1)}, bf16[3856,128]{1,0:T(8,128)(2,1)S(1)}, u32[]{:S(2)}, u32[]{:S(2)}) collective-permute-start(bf16[3856,128]{1,0:T(8,128)(2,1)} %shard_map.173.refs_0_), channel_id=1, source_target_pairs={{0,1},{1,2},{2,3},{3,4},{4,5},{5,6},{6,7},{7,8},{8,9},{9,10},{10,1... | collective-permute-start | bytes 2961416 | tf_op jit(solution)/shard_map/ppermute | solution.py:331
  9.9 30.8 %all-to-all-start = ((bf16[16,24,128]{2,1,0:T(8,128)(2,1)}), bf16[16,24,128]{2,1,0:T(8,128)(2,1)S(1)}, u32[]{:S(2)}, u32[]{:S(2)}) async-start(bf16[16,24,128]{2,1,0:T(8,128)(2,1)} %shard_map.172), calls=%async_computation | async-start | bytes 196608 | tf_op jit(solution)/shard_map/all_to_all | solution.py:330
  40.7 0.6 copy-start.3
  43.7 32.7 %all-to-all-start.1 = ((bf16[16,48,1024]{2,1,0:T(8,128)(2,1)}), bf16[16,48,1024]{2,1,0:T(8,128)(2,1)S(1)}, u32[]{:S(2)}, u32[]{:S(2)}) async-start(bf16[16,48,1024]{2,1,0:T(8,128)(2,1)} %shard_map.175), calls=%async_computation.1 | async-start | bytes 3145728 | tf_op jit(solution)/shard_map/all_to_all | solution.py:345
  57.0 1.0 copy-start.4
  58.0 0.9 copy-start.5
  76.4 10.5 %copy-start = (bf16[16,48,1024]{2,1,0:T(8,128)(2,1)}, bf16[16,48,1024]{2,1,0:T(8,128)(2,1)S(1)}, u32[]{:S(2)}) copy-start(bf16[16,48,1024]{2,1,0:T(8,128)(2,1)S(1)} %all-to-all-done.1.own_hbm) | copy-start | bytes 4718596
  76.4 10.5 %collective-permute-start.2 = (bf16[16,48,1024]{2,1,0:T(8,128)(2,1)S(1)}, bf16[16,48,1024]{2,1,0:T(8,128)(2,1)S(1)}, u32[]{:S(2)}, u32[]{:S(2)}) collective-permute-start(bf16[16,48,1024]{2,1,0:T(8,128)(2,1)S(1)} %all-to-all-done.1.own_hbm), channel_id=1, source_target_pairs={{0,32},{32,0},{1,33},{33,1},{2,34},{34,2},{3,35},{35,3},{4,36},{36... | collective-permute-start | bytes 4718600 | tf_op jit(solution)/shard_map/ppermute | solution.py:348
  86.9 1.2 copy-start.1
  97.4 16.0 %all-to-all-start.2 = ((f32[32,8,128]{2,1,0:T(8,128)}), f32[32,8,128]{2,1,0:T(8,128)S(1)}, u32[]{:S(2)}, u32[]{:S(2)}) async-start(f32[32,8,128]{2,1,0:T(8,128)} %get-tuple-element.33), calls=%async_computation.2 | async-start | bytes 262144 | tf_op jit(solution)/shard_map/all_to_all | solution.py:358
  113.4 0.6 copy-start.2

commit v4 on v3

--- a/solution.py
+++ b/solution.py
@@ -37,13 +37,13 @@
         chan[i] = HALF * core + 48 * y + 24 * zh + j
     order = np.zeros((C, CPAD), np.float32)
     order[np.arange(C), chan] = 1
-    temp_perm = np.zeros((KPAD, 3 * CPAD), np.float32)
+    temp_perm = np.zeros((4, 256, 768), np.float32)
     for x in range(4):
         for t in range(3):
             for zl in range(8):
                 for kk in range(10):
-                    i = 40 * zl + 10 * x + kk
-                    temp_perm[256 * x + 30 * zl + 10 * t + kk, CPAD * t + chan[i]] = 1
+                    to = chan[40 * zl + 10 * x + kk] - 128 * (x // 2)
+                    temp_perm[x, 30 * zl + 10 * t + kk, 256 * t + to] = 1
     same1 = np.kron(np.eye(GROUPS), np.ones((10, 10))).astype(np.float32)
     same2 = order.T @ same1 @ order
     return act_perm, order, temp_perm, same1, same2
@@ -254,8 +254,11 @@
     move.start(w_hbm.at[3], w).wait()
     frame = lax.axis_index("zl") * 4 + lax.axis_index("x")
     keep = [(frame > 0).astype(F32), 1.0, (frame < 31).astype(F32)]
+    spread = [jnp.dot(w[:, 256 * x : 256 * x + 256], perm[x], preferred_element_type=F32) for x in range(4)]
+    left, right = spread[0] + spread[1], spread[2] + spread[3]
     for t in range(3):
-        part = jnp.dot(w[...], perm[:, CPAD * t : CPAD * t + CPAD], preferred_element_type=F32).astype(BF)
+        a, b = left[:, 256 * t : 256 * t + 256], right[:, 256 * t : 256 * t + 256]
+        part = jnp.concatenate([a[:, :128], a[:, 128:] + b[:, :128], b[:, 128:]], axis=1).astype(BF)
         part = jnp.dot(order[...], part, preferred_element_type=F32) * keep[t]
         out[:, CPAD * t : CPAD * t + CPAD] = part.astype(BF)
     out[:, 3 * CPAD :] = order[...]
@@ -273,11 +276,11 @@
     cols0, cols2, w, hidden, last, out, sems,
 ):
     move = Mover(sems)
-    first, second = pl.ds(0, 1024), pl.ds(1024, CELLS + 2 * COLS - 1024)
+    first, second = pl.ds(0, 640), pl.ds(640, CELLS + 2 * COLS - 640)
     begin = [move.start(w_hbm.at[pl.ds(0, 3)], w)]
     begin += [move.start(h.at[first], c.at[first]) for h, c in ((cols0_hbm, cols0), (cols2_hbm, cols2))]
-    begin += [move.start(hidden_hbm, hidden), move.start(last_hbm, last)]
     later = [move.start(h.at[second], c.at[second]) for h, c in ((cols0_hbm, cols0), (cols2_hbm, cols2))]
+    later += [move.start(hidden_hbm, hidden), move.start(last_hbm, last)]
     total = stats[0]
     for n in range(1, 32):
         total = total + stats[n]
@@ -293,18 +296,18 @@
     for copy in begin:
         copy.wait()
     near = lambda i: (convolve(i, cols0, w, emb0[...]), convolve(i, cols2, w, emb2[...]))
-    now = near(0)
+    ready = [near(0), near(1)]
+    for copy in later:
+        copy.wait()
     copies = []
     for i in range(CELLS // 256):
-        if i == 2:
-            for copy in later:
-                copy.wait()
-        later_now = near(i + 1) if i < CELLS // 256 - 1 else None
+        now = ready.pop(0)
+        if i < CELLS // 256 - 2:
+            ready.append(near(i + 2))
         here = pl.ds(i * 256, 256)
         h = hidden[here, :]
         taps = jnp.concatenate([mix(now[0]), mix(h), mix(now[1]), h], axis=1)
-        out[here, :] = (nt(taps, last[...]) + bias_row).astype(BF)
-        now = later_now
+        out[here, :] = (nt(last[...], taps).T + bias_row).astype(BF)
         if i == 2:
             copies.append(move.start(out.at[pl.ds(0, 768)], out_hbm.at[pl.ds(0, 768)]))
     copies.append(move.start(out.at[pl.ds(768, 768)], out_hbm.at[pl.ds(768, 768)]))
@@ -312,7 +315,7 @@
         copy.wait()
 
 
-FILL = 15_000_000_000
+FILL = 7_500_000_000
 FRAME = ("zl", "x")
 FORWARD = [(i, i + 1) for i in range(31)]
 BACKWARD = [(i + 1, i) for i in range(31)]
@@ -340,11 +343,10 @@
         flops,
     )(*frames, gain1, shift1, const(SAME1, F32), const(ORDER), const(ACT_PERM))
     cols1, emb1 = act([frame1])
-    line, cols1 = lax.optimization_barrier((line, cols1))
     (block,) = call(line_kernel, [struct((16, 48, KPAD), BF)], "v")(line)
     own = lax.all_to_all(block, ("y", "x"), 0, 0)
     cols0, emb0, cols2, emb2 = act([frame0, frame2], FILL)
-    own, cols0 = lax.optimization_barrier((own, cols0))
+    own, cols0, cols1 = lax.optimization_barrier((own, cols0, cols1))
     other = lax.ppermute(own, "core", [(0, 1), (1, 0)])
 
     blocks = (16, 48, KPAD)

time: 131 us -> 127 us (0.969)
  starting transfers between devices: 46.9 us -> 43.8 us
  Pallas kernels: 60.2 us -> 57.3 us
    all_to_all x1, starting transfers between devices: 4.09 us -> 10.7 us  [body(): stats = lax.all_to_all(stats, FRAME, 0, 0)]
    all_to_all x1, starting transfers between devices: 13.3 us -> 6.75 us  [body(): own = lax.all_to_all(block, ('y', 'x'), 0, 0)]
    ppermute x1, starting transfers between devices: 7.47 us -> 5.33 us  [body(): other = lax.ppermute(own, 'core', [(0, 1), (1, 0)])]
    pallas_call x1, Pallas kernels: 16.2 us -> 14.5 us  [body(): call(final_kernel, [struct((CELLS, C), BF)], 'aaaaavvvvvv', 'a', [buffer(...]
    all_to_all x1, waiting for transfers between devices: 5.74 us -> 4.1 us  [body(): line = lax.all_to_all(pieces, ('zh', 'zl'), 0, 0)]
    all_to_all x1, waiting for transfers between devices: 5.81 us -> 7.18 us  [body(): stats = lax.all_to_all(stats, FRAME, 0, 0)]
  transfers between devices with their start and end apart: 6 -> 6, of which waited for: 4 -> 4; matrix products, arithmetic and copies ran while one was open for 0% -> 0% of each run, Pallas kernels for 25% -> 26%
where the time goes in v4:
time: 127 us; the launch traced here: 125 us
  Pallas kernels  57.3 us (45%)
  starting transfers between devices  43.8 us (34%)
  waiting for transfers between devices  19.3 us (15%)
  local copies, waits for them, and re-layouts  4.35 us (3%)
    pallas_call x2, Pallas kernels, body(): call(act_kernel, [struct(cols, BF), struct((1, CPAD), F32)] * len(frames)...  22.3 us
    all_to_all x1, starting transfers between devices, body(): line = lax.all_to_all(pieces, ('zh', 'zl'), 0, 0)  15.7 us
    pallas_call x1, Pallas kernels, body(): call(final_kernel, [struct((CELLS, C), BF)], 'aaaaavvvvvv', 'a', [buffer(...  14.5 us
    all_to_all x1, starting transfers between devices, body(): stats = lax.all_to_all(stats, FRAME, 0, 0)  10.7 us
    pallas_call x1, Pallas kernels, body(): call(own_kernel, [struct((CELLS, CPAD), BF), struct((32, 8, 128), F32), s...  9.35 us
    all_to_all x1, waiting for transfers between devices, body(): stats = lax.all_to_all(stats, FRAME, 0, 0)  7.18 us
    all_to_all x1, starting transfers between devices, body(): own = lax.all_to_all(block, ('y', 'x'), 0, 0)  6.75 us
    ppermute x1, starting transfers between devices, body(): other = lax.ppermute(own, 'core', [(0, 1), (1, 0)])  5.33 us
  transfers between devices with their start and end apart: 6, of which 4 were waited for; matrix products, arithmetic and copies ran while one was open for 0% of the time, Pallas kernels for 26%

profile of v4, /device:TPU:1, one launch (start us, length us, event | category | flops | bytes accessed | tf_op | source)
XLA Modules:
  0.0 125.1 jit_solution(1181869159164502268)
XLA Ops:
  0.0 1.6 %shard_map.172 = bf16[16,24,128]{2,1,0:T(8,128)(2,1)} custom-call(bf16[3,20,30]{2,1,0:T(8,128)(2,1)} %bitcast.5, bf16[10,3,20]{2,1,0:T(4,128)(2,1)} %bitcast.6), custom_call_target="tpu_custom_call" | custom-call | tf_op jit(solution)/shard_map/pallas_call | solution.py:331
  1.6 15.7 %all-to-all-start = ((bf16[16,24,128]{2,1,0:T(8,128)(2,1)}), bf16[16,24,128]{2,1,0:T(8,128)(2,1)S(1)}, u32[]{:S(2)}, u32[]{:S(2)}) async-start(bf16[16,24,128]{2,1,0:T(8,128)(2,1)} %shard_map.172), calls=%async_computation | async-start | bytes 196608 | tf_op jit(solution)/shard_map/all_to_all | solution.py:333
  17.3 2.4 %shard_map.174.refs_0_ = bf16[3856,128]{1,0:T(8,128)(2,1)} custom-call(bf16[1536,320]{1,0:T(8,128)(2,1)} %bitcast.4, f32[1,1,320]{2,1,0:T(1,128)} %emb.1), custom_call_target="tpu_custom_call" | custom-call | tf_op jit(solution)/shard_map/pallas_call | solution.py:332
  19.7 1.3 %collective-permute-start.1 = (bf16[3856,128]{1,0:T(8,128)(2,1)}, bf16[3856,128]{1,0:T(8,128)(2,1)S(1)}, u32[]{:S(2)}, u32[]{:S(2)}) collective-permute-start(bf16[3856,128]{1,0:T(8,128)(2,1)} %shard_map.174.refs_0_), channel_id=1, source_target_pairs={{1,0},{2,1},{3,2},{4,3},{5,4},{6,5},{7,6},{8,7},{9,8},{10,9},{11,1... | collective-permute-start | bytes 2961416 | tf_op jit(solution)/shard_map/ppermute | solution.py:335
  21.0 4.0 %collective-permute-start = (bf16[3856,128]{1,0:T(8,128)(2,1)}, bf16[3856,128]{1,0:T(8,128)(2,1)S(1)}, u32[]{:S(2)}, u32[]{:S(2)}) collective-permute-start(bf16[3856,128]{1,0:T(8,128)(2,1)} %shard_map.174.refs_0_), channel_id=1, source_target_pairs={{0,1},{1,2},{2,3},{3,4},{4,5},{5,6},{6,7},{7,8},{8,9},{9,10},{10,1... | collective-permute-start | bytes 2961416 | tf_op jit(solution)/shard_map/ppermute | solution.py:334
  25.1 4.1 %all-to-all-done.pieces = bf16[16,24,128]{2,1,0:T(8,128)(2,1)S(1)} async-done(((bf16[16,24,128]{2,1,0:T(8,128)(2,1)}), bf16[16,24,128]{2,1,0:T(8,128)(2,1)S(1)}, u32[]{:S(2)}, u32[]{:S(2)}) %all-to-all-start) | async-done | bytes 98336 | tf_op jit(solution)/shard_map/all_to_all | solution.py:333
  29.2 0.6 copy-done.3
  29.8 2.3 %shard_map.173 = bf16[16,48,1024]{2,1,0:T(8,128)(2,1)} custom-call(bf16[16,24,128]{2,1,0:T(8,128)(2,1)} %copy-done.3), custom_call_target="tpu_custom_call" | custom-call | tf_op jit(solution)/shard_map/pallas_call | solution.py:346
  32.1 6.8 %all-to-all-start.1 = ((bf16[16,48,1024]{2,1,0:T(8,128)(2,1)}), bf16[16,48,1024]{2,1,0:T(8,128)(2,1)S(1)}, u32[]{:S(2)}, u32[]{:S(2)}) async-start(bf16[16,48,1024]{2,1,0:T(8,128)(2,1)} %shard_map.173), calls=%async_computation.1 | async-start | bytes 3145728 | tf_op jit(solution)/shard_map/all_to_all | solution.py:347
  38.9 8.9 %shard_map.176 = (bf16[1664,1024]{1,0:T(8,128)(2,1)}, f32[1,384]{1,0:T(1,128)}) custom-call(bf16[3856,128]{1,0:T(8,128)(2,1)} %shard_map.174.refs_0_, f32[320]{0:T(512)} %refs_1_.1, f32[320]{0:T(512)} %refs_2_.3, f32[320,320]{1,0:T(8,128)} %constant.10.clone.refs_4_.refs_3_, bf16[320,384]{1,0:T(8,128)(2,1)} %constant.11.clone.refs_5_.refs_4_.order, ...), custom_call_target="tpu_custom_call" | custom-call | flops 100000000 | tf_op jit(solution)/shard_map/pallas_call | solution.py:337
  47.9 0.0 collective-permute-done.refs_0_
  47.9 1.0 copy-done.4
  48.8 0.9 copy-done.5
  49.8 13.3 %shard_map.175 = (bf16[1664,1024]{1,0:T(8,128)(2,1)}, f32[1,384]{1,0:T(1,128)}, bf16[1664,1024]{1,0:T(8,128)(2,1)}, f32[1,384]{1,0:T(1,128)}) custom-call(bf16[3856,128]{1,0:T(8,128)(2,1)} %copy-done.5, bf16[3856,128]{1,0:T(8,128)(2,1)} %copy-done.4, f32[320]{0:T(512)} %refs_1_.1, f32[320]{0:T(512)} %refs_2_.3, f32[320,320]{1,0:T(8,128)} %constant.10.clone.refs_4_.refs_3_, ...), custom_call_target="tpu_custom_call" | custom-call | flops 7500000256 | tf_op jit(solution)/shard_map/pallas_call | solution.py:337
  63.1 5.2 %all-to-all-done.1.own_hbm = bf16[16,48,1024]{2,1,0:T(8,128)(2,1)S(1)} async-done(((bf16[16,48,1024]{2,1,0:T(8,128)(2,1)}), bf16[16,48,1024]{2,1,0:T(8,128)(2,1)S(1)}, u32[]{:S(2)}, u32[]{:S(2)}) %all-to-all-start.1) | async-done | bytes 1572896 | tf_op jit(solution)/shard_map/all_to_all | solution.py:347
  68.3 5.3 %collective-permute-start.2 = (bf16[16,48,1024]{2,1,0:T(8,128)(2,1)S(1)}, bf16[16,48,1024]{2,1,0:T(8,128)(2,1)S(1)}, u32[]{:S(2)}, u32[]{:S(2)}) collective-permute-start(bf16[16,48,1024]{2,1,0:T(8,128)(2,1)S(1)} %all-to-all-done.1.own_hbm), channel_id=1, source_target_pairs={{0,32},{32,0},{1,33},{33,1},{2,34},{34,2},{3,35},{35,3},{4,36},{36... | collective-permute-start | bytes 4718600 | tf_op jit(solution)/shard_map/ppermute | solution.py:350
  73.7 2.8 %collective-permute-done.2.other_hbm = bf16[16,48,1024]{2,1,0:T(8,128)(2,1)S(1)} collective-permute-done((bf16[16,48,1024]{2,1,0:T(8,128)(2,1)S(1)}, bf16[16,48,1024]{2,1,0:T(8,128)(2,1)S(1)}, u32[]{:S(2)}, u32[]{:S(2)}) %collective-permute-start.2) | collective-permute-done | bytes 1572896 | tf_op jit(solution)/shard_map/ppermute | solution.py:350
  76.5 1.2 copy-done.1
  77.7 9.3 %shard_map.177 = (bf16[1536,384]{1,0:T(8,128)(2,1)}, f32[32,8,128]{2,1,0:T(8,128)}, bf16[4,384,1024]{2,1,0:T(8,128)(2,1)}) custom-call(bf16[1664,1024]{1,0:T(8,128)(2,1)} %get-tuple-element.23.cols_hbm, bf16[16,48,1024]{2,1,0:T(8,128)(2,1)} %copy-done, bf16[16,48,1024]{2,1,0:T(8,128)(2,1)} %copy-done.1, f32[1,384]{1,0:T(1,128)} %get-tuple-element.25.emb), custom_call_target="tpu_custom_call" | custom-call | tf_op jit(solution)/shard_map/pallas_call | solution.py:353
  87.0 10.7 %all-to-all-start.2 = ((f32[32,8,128]{2,1,0:T(8,128)}), f32[32,8,128]{2,1,0:T(8,128)S(1)}, u32[]{:S(2)}, u32[]{:S(2)}) async-start(f32[32,8,128]{2,1,0:T(8,128)} %get-tuple-element.31), calls=%async_computation.2 | async-start | bytes 262144 | tf_op jit(solution)/shard_map/all_to_all | solution.py:360
  97.7 4.9 %shard_map.178 = (bf16[320,1536]{1,0:T(8,128)(2,1)}, f32[8,384]{1,0:T(8,128)}) custom-call(bf16[4,384,1024]{2,1,0:T(8,128)(2,1)} %get-tuple-element.26.w_hbm, bf16[4,256,768]{2,1,0:T(8,128)(2,1)} %constant.13.clone.perm, bf16[320,384]{1,0:T(8,128)(2,1)} %constant.11.clone.refs_5_.refs_4_.order, f32[320]{0:T(512)} %gain.1, f32[320]{0:T(512)} %shift.1), custom_call_target="tpu_custom_call" | custom-call | flops 3000000000 | tf_op jit(solution)/shard_map/pallas_call | solution.py:361
  102.6 7.2 %all-to-all-done.2.stats = f32[32,8,128]{2,1,0:T(8,128)S(1)} async-done(((f32[32,8,128]{2,1,0:T(8,128)}), f32[32,8,128]{2,1,0:T(8,128)S(1)}, u32[]{:S(2)}, u32[]{:S(2)}) %all-to-all-start.2) | async-done | bytes 131104 | tf_op jit(solution)/shard_map/all_to_all | solution.py:360
  109.8 0.6 copy-done.2
  110.4 14.5 %shard_map.179 = bf16[1536,320]{1,0:T(8,128)(2,1)} custom-call(bf16[1664,1024]{1,0:T(8,128)(2,1)} %get-tuple-element.21.cols0_hbm, bf16[1664,1024]{1,0:T(8,128)(2,1)} %get-tuple-element.22.cols2_hbm, bf16[4,384,1024]{2,1,0:T(8,128)(2,1)} %get-tuple-element.26.w_hbm, bf16[1536,384]{1,0:T(8,128)(2,1)} %get-tuple-element.27.hidden_hbm, ...), custom_call_target="tpu_custom_call" | custom-call | tf_op jit(solution)/shard_map/pallas_call | solution.py:368
  (8 shorter events, 0.0 us)
Async XLA Ops:
  1.6 27.6 %all-to-all-start = ((bf16[16,24,128]{2,1,0:T(8,128)(2,1)}), bf16[16,24,128]{2,1,0:T(8,128)(2,1)S(1)}, u32[]{:S(2)}, u32[]{:S(2)}) async-start(bf16[16,24,128]{2,1,0:T(8,128)(2,1)} %shard_map.172), calls=%async_computation | async-start | bytes 196608 | tf_op jit(solution)/shard_map/all_to_all | solution.py:333
  19.7 28.1 %collective-permute-start.1 = (bf16[3856,128]{1,0:T(8,128)(2,1)}, bf16[3856,128]{1,0:T(8,128)(2,1)S(1)}, u32[]{:S(2)}, u32[]{:S(2)}) collective-permute-start(bf16[3856,128]{1,0:T(8,128)(2,1)} %shard_map.174.refs_0_), channel_id=1, source_target_pairs={{1,0},{2,1},{3,2},{4,3},{5,4},{6,5},{7,6},{8,7},{9,8},{10,9},{11,1... | collective-permute-start | bytes 2961416 | tf_op jit(solution)/shard_map/ppermute | solution.py:335
  21.0 26.9 %collective-permute-start = (bf16[3856,128]{1,0:T(8,128)(2,1)}, bf16[3856,128]{1,0:T(8,128)(2,1)S(1)}, u32[]{:S(2)}, u32[]{:S(2)}) collective-permute-start(bf16[3856,128]{1,0:T(8,128)(2,1)} %shard_map.174.refs_0_), channel_id=1, source_target_pairs={{0,1},{1,2},{2,3},{3,4},{4,5},{5,6},{6,7},{7,8},{8,9},{9,10},{10,1... | collective-permute-start | bytes 2961416 | tf_op jit(solution)/shard_map/ppermute | solution.py:334
  29.2 0.6 copy-start.3
  32.1 36.2 %all-to-all-start.1 = ((bf16[16,48,1024]{2,1,0:T(8,128)(2,1)}), bf16[16,48,1024]{2,1,0:T(8,128)(2,1)S(1)}, u32[]{:S(2)}, u32[]{:S(2)}) async-start(bf16[16,48,1024]{2,1,0:T(8,128)(2,1)} %shard_map.173), calls=%async_computation.1 | async-start | bytes 3145728 | tf_op jit(solution)/shard_map/all_to_all | solution.py:347
  47.9 1.0 copy-start.4
  48.8 0.9 copy-start.5
  68.3 8.2 %copy-start = (bf16[16,48,1024]{2,1,0:T(8,128)(2,1)}, bf16[16,48,1024]{2,1,0:T(8,128)(2,1)S(1)}, u32[]{:S(2)}) copy-start(bf16[16,48,1024]{2,1,0:T(8,128)(2,1)S(1)} %all-to-all-done.1.own_hbm) | copy-start | bytes 4718596
  68.3 8.2 %collective-permute-start.2 = (bf16[16,48,1024]{2,1,0:T(8,128)(2,1)S(1)}, bf16[16,48,1024]{2,1,0:T(8,128)(2,1)S(1)}, u32[]{:S(2)}, u32[]{:S(2)}) collective-permute-start(bf16[16,48,1024]{2,1,0:T(8,128)(2,1)S(1)} %all-to-all-done.1.own_hbm), channel_id=1, source_target_pairs={{0,32},{32,0},{1,33},{33,1},{2,34},{34,2},{3,35},{35,3},{4,36},{36... | collective-permute-start | bytes 4718600 | tf_op jit(solution)/shard_map/ppermute | solution.py:350
  76.5 1.2 copy-start.1
  87.0 22.8 %all-to-all-start.2 = ((f32[32,8,128]{2,1,0:T(8,128)}), f32[32,8,128]{2,1,0:T(8,128)S(1)}, u32[]{:S(2)}, u32[]{:S(2)}) async-start(f32[32,8,128]{2,1,0:T(8,128)} %get-tuple-element.31), calls=%async_computation.2 | async-start | bytes 262144 | tf_op jit(solution)/shard_map/all_to_all | solution.py:360
  109.8 0.6 copy-start.2

commit v5 on v3

v5 whole, which is shorter than its diff:
```python
import functools

import jax
import jax.numpy as jnp
import numpy as np
from jax import lax
from jax.experimental import pallas as pl
from jax.experimental.pallas import tpu as pltpu
from jax.sharding import Mesh, PartitionSpec as P

GROUPS = 32
C = 320
CELLS = 1536
COLS = 64
EPS = 1e-5
BF = jnp.bfloat16
F32 = jnp.float32
KPAD = 1024
CPAD = 384
HALF = 192
PACKED = CELLS * 5 // 2
VMEM = 60 * 1024 * 1024


def _consts():
    act_perm = np.zeros((KPAD, KPAD), np.float32)
    for f in range(32):
        zl, x = divmod(f, 4)
        for kk in range(30):
            b, i = divmod(30 * f + kk, C)
            row = 256 * b + i if i < 256 else 768 + 64 * b + i - 256
            act_perm[row, 256 * x + 30 * zl + kk] = 1
    chan = np.zeros(C, np.int64)
    for i in range(C):
        d, j = divmod(i, 20)
        y, zh, core = d // 4, (d // 2) % 2, d % 2
        chan[i] = HALF * core + 48 * y + 24 * zh + j
    order = np.zeros((C, CPAD), np.float32)
    order[np.arange(C), chan] = 1
    temp_perm = np.zeros((KPAD, KPAD), np.float32)
    for x in range(4):
        for t in range(3):
            for zl in range(8):
                for kk in range(10):
                    i = 40 * zl + 10 * x + kk
                    to = 256 * t + i if i < 256 else 768 + 64 * t + i - 256
                    temp_perm[256 * x + 30 * zl + 10 * t + kk, to] = 1
    same1 = np.kron(np.eye(GROUPS), np.ones((10, 10))).astype(np.float32)
    return act_perm, order, temp_perm, same1


ACT_PERM, ORDER, TEMP_PERM, SAME1 = _consts()


def call(kernel, out_shape, ins, outs=None, scratch=(), flops=0, vmem=VMEM):
    space = {"v": pltpu.VMEM, "a": pl.ANY}
    specs = lambda letters: [pl.BlockSpec(memory_space=space[c]) for c in letters]
    outs = specs(outs or "v" * len(out_shape))
    return pl.pallas_call(
        kernel,
        out_shape=tuple(out_shape),
        in_specs=specs(ins),
        out_specs=tuple(outs),
        scratch_shapes=list(scratch),
        compiler_params=pltpu.CompilerParams(vmem_limit_bytes=vmem),
        cost_estimate=pl.CostEstimate(flops=flops, bytes_accessed=0, transcendentals=0),
    )


class Mover:
    def __init__(self, sems):
        self.sems, self.used = sems, 0

    def start(self, src, dst):
        copy = pltpu.make_async_copy(src, dst, self.sems.at[self.used])
        self.used += 1
        copy.start()
        return copy


def exact(a, b):
    return jnp.dot(a, b, precision=lax.Precision.HIGHEST, preferred_element_type=F32)


def nt(a, b):
    return lax.dot_general(a, b, (((1,), (1,)), ((), ())), preferred_element_type=F32)


def silu(v):
    half = 0.5 * v
    return half + half * jnp.tanh(half)


def pack_kernel(sw, tw, out):
    lane = lax.broadcasted_iota(jnp.int32, (30, 128), 1)
    row = lax.broadcasted_iota(jnp.int32, (30, 128), 0)
    total = jnp.zeros((20, 128), F32)
    for a in range(3):
        total += jnp.dot(sw[a], (lane == row + 30 * a).astype(F32).astype(BF), preferred_element_type=F32)
    rows = jnp.concatenate([tw[r].astype(F32) for r in range(10)], axis=0).astype(BF)
    spread = (lane == 90 + 10 * lax.rem(row, 3) + lax.div(row, 3)).astype(F32).astype(BF)
    total += lax.dot_general(rows, spread, (((0,), (0,)), ((), ())), preferred_element_type=F32)
    piece = jnp.concatenate([total, jnp.zeros((4, 128), F32)], axis=0).astype(BF)
    for n in range(16):
        out[n] = piece


def line_kernel(pieces, out):
    both = [jnp.concatenate([pieces[zl].astype(F32), pieces[8 + zl].astype(F32)], axis=0) for zl in range(8)]
    pad = jnp.zeros((48, 16), F32)
    groups = [jnp.concatenate([b[:, 30 * a : 30 * a + 30] for b in both] + [pad], axis=1) for a in range(4)]
    block = jnp.concatenate(groups, axis=1).astype(BF)
    for n in range(16):
        out[n] = block


def pair(v):
    return v[:, :64] + v[:, 64:]


def moments(chunks):
    s = q = 0.0
    for v in chunks:
        v = v.reshape(-1, 8, v.shape[1])
        s, q = s + jnp.sum(v, axis=0), q + jnp.sum(v * v, axis=0)
    return s, q


def act_kernel(video, gain, shift, same, perm_hbm, out_hbm, perm, out, sems):
    move = Mover(sems)
    perm_copy = move.start(perm_hbm, perm)
    chunk = 256
    column = lax.rem(lax.broadcasted_iota(jnp.int32, (chunk, 256), 0), COLS)
    low = lax.broadcasted_iota(jnp.int32, (chunk, 128), 1) < 64

    def shifted(v):
        edge = column[:, : v.shape[1]]
        before = jnp.where(edge == 0, 0.0, pltpu.roll(v, 1, 0))
        after = jnp.where(edge == COLS - 1, 0.0, pltpu.roll(v, chunk - 1, 0))
        return before, v, after

    main = lambda i: video[pl.ds(i * chunk, chunk), 0:256].astype(F32)
    tail = lambda i: video[pl.ds(i * chunk, chunk), 256:320].astype(F32)
    rest = lambda i: jnp.concatenate([tail(i), tail(i + 3)], axis=1)
    s, q = moments(main(i) for i in range(6))
    s2, q2 = moments(rest(i) for i in range(3))
    s = jnp.concatenate([s, pair(s2)], axis=1)
    q = jnp.concatenate([q, pair(q2)], axis=1)
    both = exact(jnp.concatenate([s, q], axis=0), same[...]) / (CELLS * C // GROUPS)
    mean = jnp.sum(both[:8], axis=0, keepdims=True)
    square = jnp.sum(both[8:], axis=0, keepdims=True)
    scale = lax.rsqrt(square - mean * mean + EPS) * gain[...].reshape(1, C)
    offset = shift[...].reshape(1, C) - mean * scale
    scale2 = jnp.concatenate([scale[:, 256:], scale[:, 256:]], axis=1)
    offset2 = jnp.concatenate([offset[:, 256:], offset[:, 256:]], axis=1)
    scale, offset = scale[:, :256], offset[:, :256]
    out[pl.ds(0, COLS), :] = jnp.zeros((COLS, KPAD), BF)
    out[pl.ds(CELLS + COLS, COLS), :] = jnp.zeros((COLS, KPAD), BF)
    perm_copy.wait()
    swap = lambda v: pltpu.roll(v, 64, 1)
    for i in range(3):
        before2, v2, after2 = shifted(silu(rest(i) * scale2 + offset2).astype(BF).astype(F32))
        tails = [
            (jnp.where(low, before2, swap(v2)), jnp.where(low, after2, 0.0)),
            (jnp.where(low, swap(before2), v2), jnp.where(low, swap(after2), 0.0)),
        ]
        for n in range(2):
            at = i + 3 * n
            taps = shifted(silu(main(at) * scale + offset).astype(BF).astype(F32))
            taps = jnp.concatenate(taps + tails[n], axis=1).astype(BF)
            total = jnp.dot(taps, perm[...], preferred_element_type=F32)
            out[pl.ds(at * chunk + COLS, chunk), :] = total.astype(BF)
    move.start(out, out_hbm).wait()


def place_weights(half, block, w):
    for y in range(4):
        for x in range(4):
            for a in range(4):
                rows = pl.ds(pl.multiple_of(half + 48 * y, 16), 48)
                w[a, rows, 256 * x : 256 * x + 256] = block[4 * y + x, :, 256 * a : 256 * a + 256]


def own_kernel(cols_hbm, own_hbm, other_hbm, emb, order, hidden_hbm, stats, last_hbm, cols, own, other, hidden, w, natural, sems):
    move = Mover(sems)
    own_copy = move.start(own_hbm, own)
    other_copy = move.start(other_hbm, other)
    cols_copy = move.start(cols_hbm, cols)
    mine = lax.axis_index("core") * HALF
    own_copy.wait()
    place_weights(mine, own, w)
    other_copy.wait()
    place_weights(HALF - mine, other, w)
    cols_copy.wait()
    for a in range(4):
        natural[a] = jnp.dot(order[...], w[a], preferred_element_type=F32).astype(BF)
    s = q = jnp.zeros((8, C), F32)
    for i in (0, 3, 1, 4, 2, 5):
        total = jnp.zeros((C, 256), F32)
        for a in range(3):
            total += nt(natural[a], cols[pl.ds(i * 256 + COLS * a, 256), :])
        h = (total.T + emb[0]).astype(BF)
        hidden[pl.ds(i * 256, 256), :] = h[:, :128]
        hidden[pl.ds(CELLS + i * 256, 256), :] = h[:, 128:256]
        h = h.astype(F32)
        if i < 3:
            rest = h[:, 256:]
        else:
            both = jnp.concatenate([rest, h[:, 256:]], axis=1)
            hidden[pl.ds(2 * CELLS + (i - 3) * 256, 256), :] = both.astype(BF)
        h = h.reshape(32, 8, C)
        s, q = s + jnp.sum(h, axis=0), q + jnp.sum(h * h, axis=0)
    copies = [move.start(hidden, hidden_hbm), move.start(natural.at[3], last_hbm)]
    s = jnp.sum(s, axis=0, keepdims=True)
    q = jnp.sum(q, axis=0, keepdims=True)
    tail = jnp.concatenate([s[:, 256:], q[:, 256:]], axis=1)
    rows = [s[:, :128], s[:, 128:256], q[:, :128], q[:, 128:256], tail, jnp.zeros((3, 128), F32)]
    block = jnp.concatenate(rows, axis=0)
    for n in range(32):
        stats[n] = block
    for copy in copies:
        copy.wait()


def temporal_kernel(w, perm, out):
    frame = lax.axis_index("zl") * 4 + lax.axis_index("x")
    lane = lax.broadcasted_iota(jnp.int32, (1, KPAD), 1)
    tap = jnp.where(lane < 768, lane // 256, (lane - 768) // 64)
    keep = jnp.where(tap == 0, (frame > 0).astype(F32), jnp.where(tap == 2, (frame < 31).astype(F32), 1.0))
    out[...] = (jnp.dot(w[...], perm[...], preferred_element_type=F32) * keep).astype(BF)


def final_kernel(hidden0, hidden1, hidden2, stats, gain, shift, same, bias, last, out):
    total = stats[0]
    for n in range(1, 32):
        total = total + stats[n]
    s = jnp.concatenate([total[0:1], total[1:2], total[4:5, :64]], axis=1)
    q = jnp.concatenate([total[2:3], total[3:4], total[4:5, 64:]], axis=1)
    both = jnp.concatenate([s, q, jnp.zeros((6, C), F32)], axis=0)
    both = exact(both, same[...]) / (CELLS * 32 * C // GROUPS)
    mean, square = both[0:1], both[1:2]
    scale = lax.rsqrt(square - mean * mean + EPS) * gain[...].reshape(1, C)
    offset = shift[...].reshape(1, C) - mean * scale
    tiles = [(scale[:, n : n + 128], offset[:, n : n + 128]) for n in (0, 128)]
    tiles.append(tuple(jnp.concatenate([v[:, 256:], v[:, 256:]], axis=1) for v in (scale, offset)))
    bias_row = bias[...].reshape(1, C)
    low = lax.broadcasted_iota(jnp.int32, (256, 128), 1) < 64
    swap = lambda v: pltpu.roll(v, 64, 1)
    frames = (hidden0, hidden1, hidden2)

    def mix(h, start, tile):
        v = h[pl.ds(start, 256), :].astype(F32)
        return silu(v * tiles[tile][0] + tiles[tile][1])

    for i in range(3):
        a, b, c = (mix(h, 2 * CELLS + i * 256, 2) for h in frames)
        tails = [
            (jnp.where(low, a, swap(b)), jnp.where(low, c, 0.0)),
            (jnp.where(low, swap(a), b), jnp.where(low, swap(c), 0.0)),
        ]
        rest = hidden1[pl.ds(2 * CELLS + i * 256, 256), :].astype(F32)
        for n in range(2):
            at = i + 3 * n
            parts = [mix(h, tile * CELLS + at * 256, tile) for h in frames for tile in range(2)]
            taps = jnp.concatenate(parts + list(tails[n]), axis=1).astype(BF)
            moved = (nt(last[...], taps).T + bias_row).astype(BF).astype(F32)
            here = pl.ds(at * 256, 256)
            h = [hidden1[pl.ds(tile * CELLS + at * 256, 256), :].astype(F32) for tile in range(2)]
            h.append(rest[:, :64] if n == 0 else rest[:, 64:])
            out[here, :] = (moved + jnp.concatenate(h, axis=1)).astype(BF)


FILL = 5_000_000_000
FRAME = ("zl", "x")
FORWARD = [(i, i + 1) for i in range(31)]
BACKWARD = [(i + 1, i) for i in range(31)]


def body(video, emb, gain1, shift1, gain2, shift2, sw, tw, bias):
    struct = jax.ShapeDtypeStruct
    const = lambda a, t=BF: jnp.asarray(a, t)
    sems = pltpu.SemaphoreType.DMA
    buffer = lambda *shape: pltpu.VMEM(shape, BF)
    cols = (CELLS + 2 * COLS, KPAD)
    blocks = (16, 48, KPAD)

    (pieces,) = call(pack_kernel, [struct((16, 24, 128), BF)], "vv")(sw.transpose(0, 2, 1), tw.transpose(1, 0, 2))
    line = lax.all_to_all(pieces, ("zh", "zl"), 0, 0)
    (block,) = call(line_kernel, [struct(blocks, BF)], "v")(line)
    own = lax.all_to_all(block, ("y", "x"), 0, 0)
    (cols1,) = call(
        act_kernel,
        [struct(cols, BF)],
        "vvvva",
        "a",
        [buffer(KPAD, KPAD), buffer(*cols), sems((2,))],
        FILL,
    )(video.reshape(CELLS, C), gain1, shift1, const(SAME1, F32), const(ACT_PERM))
    own, cols1 = lax.optimization_barrier((own, cols1))
    other = lax.ppermute(own, "core", [(0, 1), (1, 0)])

    hidden1, stats, w = call(
        own_kernel,
        [struct((PACKED, 128), BF), struct((32, 8, 128), F32), struct((C, KPAD), BF)],
        "aaavv",
        "ava",
        [
            buffer(*cols),
            buffer(*blocks),
            buffer(*blocks),
            buffer(PACKED, 128),
            buffer(4, CPAD, KPAD),
            buffer(4, C, KPAD),
            sems((5,)),
        ],
    )(cols1, own, other, emb, const(ORDER))
    hidden0 = lax.ppermute(hidden1, FRAME, FORWARD)
    hidden2 = lax.ppermute(hidden1, FRAME, BACKWARD)
    stats = lax.all_to_all(stats, FRAME, 0, 0)
    (last,) = call(temporal_kernel, [struct((C, KPAD), BF)], "vv", flops=5_000_000_000)(w, const(TEMP_PERM))
    (out,) = call(final_kernel, [struct((CELLS, C), BF)], "v" * 9)(
        hidden0, hidden1, hidden2, stats, gain2, shift2, const(SAME1, F32), bias, last
    )
    return out.reshape(video.shape)


def solution(mesh):
    split = Mesh(mesh.devices.reshape(4, 2, 2, 8, 4), ("y", "zh", "core", "zl", "x"))
    dp = ("y", "zh", "core")
    data = P(dp, FRAME, None, None, None)
    placed = (data, P(dp, FRAME, None), P(), P(), P(), P(), P(None, FRAME, dp), P(None, FRAME, dp), P())
    return jax.shard_map(body, mesh=split, in_specs=placed, out_specs=data, check_vma=False)
```

time: 131 us -> 122 us (0.931)
  blocking collectives: 0 us -> 27.7 us
  Pallas kernels: 60.2 us -> 32.7 us
  starting transfers between devices: 46.9 us -> 25.3 us
  waiting for transfers between devices: 18.7 us -> 32.6 us
    all_to_all x0 -> x1, blocking collectives: none -> 27.7 us  [body(): line = lax.all_to_all(pieces, ('zh', 'zl'), 0, 0)]
    pallas_call x7 -> x5, Pallas kernels: 58.6 us -> 31.1 us  [the longest x1 10.6 us: body(): call(own_kernel, [struct((PACKED, 128), BF), struct((32, 8, 128), F32), s...]
    all_to_all x1 -> x0, starting transfers between devices: 16.1 us -> none  [body(): line = lax.all_to_all(pieces, ('zh', 'zl'), 0, 0)]
    all_to_all x1, waiting for transfers between devices: 5.81 us -> 18.2 us  [body(): stats = lax.all_to_all(stats, FRAME, 0, 0)]
    all_to_all x1, waiting for transfers between devices: 4.16 us -> 11.3 us  [body(): own = lax.all_to_all(block, ('y', 'x'), 0, 0)]
    all_to_all x1, starting transfers between devices: 13.3 us -> 6.75 us  [body(): own = lax.all_to_all(block, ('y', 'x'), 0, 0)]
    all_to_all x1 -> x0, waiting for transfers between devices: 5.74 us -> none  [body(): line = lax.all_to_all(pieces, ('zh', 'zl'), 0, 0)]
    all_to_all x1, starting transfers between devices: 4.09 us -> 6.4 us  [body(): stats = lax.all_to_all(stats, FRAME, 0, 0)]
  transfers between devices with their start and end apart: 6 -> 5, of which waited for: 4 -> 3; matrix products, arithmetic and copies ran while one was open for 0% -> 0% of each run, Pallas kernels for 25% -> 10%
where the time goes in v5:
time: 122 us; the launch traced here: 121 us
  Pallas kernels  32.7 us (27%)
  waiting for transfers between devices  32.6 us (27%)
  blocking collectives  27.7 us (23%)
  starting transfers between devices  25.3 us (21%)
  local copies, waits for them, and re-layouts  3.17 us (3%)
    all_to_all x1, blocking collectives, body(): line = lax.all_to_all(pieces, ('zh', 'zl'), 0, 0)  27.7 us
    all_to_all x1, waiting for transfers between devices, body(): stats = lax.all_to_all(stats, FRAME, 0, 0)  18.2 us
    all_to_all x1, waiting for transfers between devices, body(): own = lax.all_to_all(block, ('y', 'x'), 0, 0)  11.3 us
    pallas_call x1, Pallas kernels, body(): call(own_kernel, [struct((PACKED, 128), BF), struct((32, 8, 128), F32), s...  10.6 us
    pallas_call x1, Pallas kernels, body(): call(act_kernel, [struct(cols, BF)], 'vvvva', 'a', [buffer(KPAD, KPAD), b...  8.42 us
    ppermute x1, starting transfers between devices, body(): other = lax.ppermute(own, 'core', [(0, 1), (1, 0)])  6.82 us
    all_to_all x1, starting transfers between devices, body(): own = lax.all_to_all(block, ('y', 'x'), 0, 0)  6.75 us
    all_to_all x1, starting transfers between devices, body(): stats = lax.all_to_all(stats, FRAME, 0, 0)  6.4 us
  transfers between devices with their start and end apart: 5, of which 3 were waited for; matrix products, arithmetic and copies ran while one was open for 0% of the time, Pallas kernels for 10%

profile of v5, /device:TPU:1, one launch (start us, length us, event | category | flops | bytes accessed | tf_op | source)
XLA Modules:
  0.0 121.5 jit_solution(4337055120194202955)
XLA Ops:
  0.0 1.6 %shard_map.136 = bf16[16,24,128]{2,1,0:T(8,128)(2,1)} custom-call(bf16[3,20,30]{2,1,0:T(8,128)(2,1)} %bitcast.4, bf16[10,3,20]{2,1,0:T(4,128)(2,1)} %bitcast.5), custom_call_target="tpu_custom_call" | custom-call | tf_op jit(solution)/shard_map/pallas_call | solution.py:287
  1.6 27.7 %all_to_all.15.pieces = bf16[16,24,128]{2,1,0:T(8,128)(2,1)} all-to-all(bf16[16,24,128]{2,1,0:T(8,128)(2,1)} %shard_map.136), channel_id=1, replica_groups=mesh['y'=4,'zh'=2,'core'=2,'zl'=8,'x'=4] {'zh','zl'}, dimensions={0} | all-to-all | bytes 196608 | tf_op jit(solution)/shard_map/all_to_all | solution.py:288
  29.3 2.4 %shard_map.137 = bf16[16,48,1024]{2,1,0:T(8,128)(2,1)} custom-call(bf16[16,24,128]{2,1,0:T(8,128)(2,1)} %all_to_all.15.pieces), custom_call_target="tpu_custom_call" | custom-call | tf_op jit(solution)/shard_map/pallas_call | solution.py:289
  31.6 6.8 %all-to-all-start.1 = ((bf16[16,48,1024]{2,1,0:T(8,128)(2,1)}), bf16[16,48,1024]{2,1,0:T(8,128)(2,1)S(1)}, u32[]{:S(2)}, u32[]{:S(2)}) async-start(bf16[16,48,1024]{2,1,0:T(8,128)(2,1)} %shard_map.137), calls=%async_computation.1 | async-start | bytes 3145728 | tf_op jit(solution)/shard_map/all_to_all | solution.py:290
  38.4 8.4 %shard_map.138.cols_hbm = bf16[1664,1024]{1,0:T(8,128)(2,1)} custom-call(bf16[1536,320]{1,0:T(8,128)(2,1)} %bitcast.6, f32[320]{0:T(512)} %gain.2, f32[320]{0:T(512)} %shift.2, f32[320,320]{1,0:T(8,128)} %constant.8.clone.same, bf16[1024,1024]{1,0:T(8,128)(2,1)} %constant.9.clone.perm_hbm), custom_call_target="tpu_custom_call" | custom-call | flops 5000000000 | tf_op jit(solution)/shard_map/pallas_call | solution.py:291
  46.8 11.3 %all-to-all-done.1.own_hbm = bf16[16,48,1024]{2,1,0:T(8,128)(2,1)S(1)} async-done(((bf16[16,48,1024]{2,1,0:T(8,128)(2,1)}), bf16[16,48,1024]{2,1,0:T(8,128)(2,1)S(1)}, u32[]{:S(2)}, u32[]{:S(2)}) %all-to-all-start.1) | async-done | bytes 1572896 | tf_op jit(solution)/shard_map/all_to_all | solution.py:290
  58.1 0.0 copy-start
  58.1 6.8 %collective-permute-start = (bf16[16,48,1024]{2,1,0:T(8,128)(2,1)S(1)}, bf16[16,48,1024]{2,1,0:T(8,128)(2,1)S(1)}, u32[]{:S(2)}, u32[]{:S(2)}) collective-permute-start(bf16[16,48,1024]{2,1,0:T(8,128)(2,1)S(1)} %all-to-all-done.1.own_hbm), channel_id=1, source_target_pairs={{0,32},{32,0},{1,33},{33,1},{2,34},{34,2},{3,35},{35,3},{4,36},{36... | collective-permute-start | bytes 4718600 | tf_op jit(solution)/shard_map/ppermute | solution.py:300
  65.0 3.0 %collective-permute-done.other_hbm = bf16[16,48,1024]{2,1,0:T(8,128)(2,1)S(1)} collective-permute-done((bf16[16,48,1024]{2,1,0:T(8,128)(2,1)S(1)}, bf16[16,48,1024]{2,1,0:T(8,128)(2,1)S(1)}, u32[]{:S(2)}, u32[]{:S(2)}) %collective-permute-start) | collective-permute-done | bytes 1572896 | tf_op jit(solution)/shard_map/ppermute | solution.py:300
  68.0 0.0 copy-done
  68.0 0.0 copy-start.1
  68.0 1.2 copy-done.1
  69.2 10.6 %shard_map.139 = (bf16[3840,128]{1,0:T(8,128)(2,1)}, f32[32,8,128]{2,1,0:T(8,128)}, bf16[320,1024]{1,0:T(8,128)(2,1)}) custom-call(bf16[1664,1024]{1,0:T(8,128)(2,1)} %shard_map.138.cols_hbm, bf16[16,48,1024]{2,1,0:T(8,128)(2,1)} %copy-done, bf16[16,48,1024]{2,1,0:T(8,128)(2,1)} %copy-done.1, f32[1,1,320]{2,1,0:T(1,128)} %emb.1, ...), custom_call_target="tpu_custom_call" | custom-call | tf_op jit(solution)/shard_map/pallas_call | solution.py:302
  79.7 1.3 %collective-permute-start.2 = (bf16[3840,128]{1,0:T(8,128)(2,1)}, bf16[3840,128]{1,0:T(8,128)(2,1)S(1)}, u32[]{:S(2)}, u32[]{:S(2)}) collective-permute-start(bf16[3840,128]{1,0:T(8,128)(2,1)} %get-tuple-element.12.hidden1), channel_id=1, source_target_pairs={{1,0},{2,1},{3,2},{4,3},{5,4},{6,5},{7,6},{8,7},{9,8},{10,9},{11,1... | collective-permute-start | bytes 2949128 | tf_op jit(solution)/shard_map/ppermute | solution.py:318
  81.0 4.0 %collective-permute-start.1 = (bf16[3840,128]{1,0:T(8,128)(2,1)}, bf16[3840,128]{1,0:T(8,128)(2,1)S(1)}, u32[]{:S(2)}, u32[]{:S(2)}) collective-permute-start(bf16[3840,128]{1,0:T(8,128)(2,1)} %get-tuple-element.12.hidden1), channel_id=1, source_target_pairs={{0,1},{1,2},{2,3},{3,4},{4,5},{5,6},{6,7},{7,8},{8,9},{9,10},{10,1... | collective-permute-start | bytes 2949128 | tf_op jit(solution)/shard_map/ppermute | solution.py:317
  85.1 6.4 %all-to-all-start.2 = ((f32[32,8,128]{2,1,0:T(8,128)}), f32[32,8,128]{2,1,0:T(8,128)S(1)}, u32[]{:S(2)}, u32[]{:S(2)}) async-start(f32[32,8,128]{2,1,0:T(8,128)} %get-tuple-element.13), calls=%async_computation.2 | async-start | bytes 262144 | tf_op jit(solution)/shard_map/all_to_all | solution.py:319
  91.5 3.5 %shard_map.140.last = bf16[320,1024]{1,0:T(8,128)(2,1)} custom-call(bf16[320,1024]{1,0:T(8,128)(2,1)} %get-tuple-element.14.w, bf16[1024,1024]{1,0:T(8,128)(2,1)} %constant.11.clone.perm), custom_call_target="tpu_custom_call" | custom-call | flops 5000000000 | tf_op jit(solution)/shard_map/pallas_call | solution.py:320
  95.0 18.2 %all-to-all-done.2.stats = f32[32,8,128]{2,1,0:T(8,128)S(1)} async-done(((f32[32,8,128]{2,1,0:T(8,128)}), f32[32,8,128]{2,1,0:T(8,128)S(1)}, u32[]{:S(2)}, u32[]{:S(2)}) %all-to-all-start.2) | async-done | bytes 131104 | tf_op jit(solution)/shard_map/all_to_all | solution.py:319
  113.3 0.0 collective-permute-done.2.hidden2
  113.3 0.0 collective-permute-done.1.hidden0
  113.3 0.6 copy-done.4
  113.9 0.4 copy-done.2
  114.3 0.9 copy-done.3
  115.2 6.3 %shard_map.141 = bf16[1536,320]{1,0:T(8,128)(2,1)} custom-call(bf16[3840,128]{1,0:T(8,128)(2,1)} %copy-done.3, bf16[3840,128]{1,0:T(8,128)(2,1)} %get-tuple-element.12.hidden1, bf16[3840,128]{1,0:T(8,128)(2,1)} %copy-done.2, f32[32,8,128]{2,1,0:T(8,128)} %copy-done.4, f32[320]{0:T(512)} %gain.3, f32[320]{0:T(512)} %shift.3, f32[320,320]{1,0:T(8,128)} %constant.8.clone.same, ...), custom_call_target="tpu_custom_call" | custom-call | tf_op jit(solution)/shard_map/pallas_call | solution.py:321
  (3 shorter events, 0.0 us)
Async XLA Ops:
  31.6 26.5 %all-to-all-start.1 = ((bf16[16,48,1024]{2,1,0:T(8,128)(2,1)}), bf16[16,48,1024]{2,1,0:T(8,128)(2,1)S(1)}, u32[]{:S(2)}, u32[]{:S(2)}) async-start(bf16[16,48,1024]{2,1,0:T(8,128)(2,1)} %shard_map.137), calls=%async_computation.1 | async-start | bytes 3145728 | tf_op jit(solution)/shard_map/all_to_all | solution.py:290
  58.1 9.8 %copy-start = (bf16[16,48,1024]{2,1,0:T(8,128)(2,1)}, bf16[16,48,1024]{2,1,0:T(8,128)(2,1)S(1)}, u32[]{:S(2)}) copy-start(bf16[16,48,1024]{2,1,0:T(8,128)(2,1)S(1)} %all-to-all-done.1.own_hbm) | copy-start | bytes 4718596
  58.1 9.8 %collective-permute-start = (bf16[16,48,1024]{2,1,0:T(8,128)(2,1)S(1)}, bf16[16,48,1024]{2,1,0:T(8,128)(2,1)S(1)}, u32[]{:S(2)}, u32[]{:S(2)}) collective-permute-start(bf16[16,48,1024]{2,1,0:T(8,128)(2,1)S(1)} %all-to-all-done.1.own_hbm), channel_id=1, source_target_pairs={{0,32},{32,0},{1,33},{33,1},{2,34},{34,2},{3,35},{35,3},{4,36},{36... | collective-permute-start | bytes 4718600 | tf_op jit(solution)/shard_map/ppermute | solution.py:300
  68.0 1.2 copy-start.1
  79.7 33.5 %collective-permute-start.2 = (bf16[3840,128]{1,0:T(8,128)(2,1)}, bf16[3840,128]{1,0:T(8,128)(2,1)S(1)}, u32[]{:S(2)}, u32[]{:S(2)}) collective-permute-start(bf16[3840,128]{1,0:T(8,128)(2,1)} %get-tuple-element.12.hidden1), channel_id=1, source_target_pairs={{1,0},{2,1},{3,2},{4,3},{5,4},{6,5},{7,6},{8,7},{9,8},{10,9},{11,1... | collective-permute-start | bytes 2949128 | tf_op jit(solution)/shard_map/ppermute | solution.py:318
  81.0 32.2 %collective-permute-start.1 = (bf16[3840,128]{1,0:T(8,128)(2,1)}, bf16[3840,128]{1,0:T(8,128)(2,1)S(1)}, u32[]{:S(2)}, u32[]{:S(2)}) collective-permute-start(bf16[3840,128]{1,0:T(8,128)(2,1)} %get-tuple-element.12.hidden1), channel_id=1, source_target_pairs={{0,1},{1,2},{2,3},{3,4},{4,5},{5,6},{6,7},{7,8},{8,9},{9,10},{10,1... | collective-permute-start | bytes 2949128 | tf_op jit(solution)/shard_map/ppermute | solution.py:317
  85.1 28.2 %all-to-all-start.2 = ((f32[32,8,128]{2,1,0:T(8,128)}), f32[32,8,128]{2,1,0:T(8,128)S(1)}, u32[]{:S(2)}, u32[]{:S(2)}) async-start(f32[32,8,128]{2,1,0:T(8,128)} %get-tuple-element.13), calls=%async_computation.2 | async-start | bytes 262144 | tf_op jit(solution)/shard_map/all_to_all | solution.py:319
  113.3 0.6 copy-start.4
  113.3 1.0 copy-start.2
  114.3 0.9 copy-start.3

commit v6 on v5

--- a/solution.py
+++ b/solution.py
@@ -19,6 +19,7 @@
 CPAD = 384
 HALF = 192
 PACKED = CELLS * 5 // 2
+FIRST = 1792
 VMEM = 60 * 1024 * 1024
 
 
@@ -181,7 +182,7 @@
                 w[a, rows, 256 * x : 256 * x + 256] = block[4 * y + x, :, 256 * a : 256 * a + 256]
 
 
-def own_kernel(cols_hbm, own_hbm, other_hbm, emb, order, hidden_hbm, stats, last_hbm, cols, own, other, hidden, w, natural, sems):
+def own_kernel(cols_hbm, own_hbm, other_hbm, emb, order, first_hbm, second_hbm, stats, last_hbm, cols, own, other, hidden, w, natural, sems):
     move = Mover(sems)
     own_copy = move.start(own_hbm, own)
     other_copy = move.start(other_hbm, other)
@@ -210,7 +211,8 @@
             hidden[pl.ds(2 * CELLS + (i - 3) * 256, 256), :] = both.astype(BF)
         h = h.reshape(32, 8, C)
         s, q = s + jnp.sum(h, axis=0), q + jnp.sum(h * h, axis=0)
-    copies = [move.start(hidden, hidden_hbm), move.start(natural.at[3], last_hbm)]
+    copies = [move.start(hidden.at[pl.ds(0, FIRST)], first_hbm), move.start(hidden.at[pl.ds(FIRST, PACKED - FIRST)], second_hbm)]
+    copies.append(move.start(natural.at[3], last_hbm))
     s = jnp.sum(s, axis=0, keepdims=True)
     q = jnp.sum(q, axis=0, keepdims=True)
     tail = jnp.concatenate([s[:, 256:], q[:, 256:]], axis=1)
@@ -230,7 +232,12 @@
     out[...] = (jnp.dot(w[...], perm[...], preferred_element_type=F32) * keep).astype(BF)
 
 
-def final_kernel(hidden0, hidden1, hidden2, stats, gain, shift, same, bias, last, out):
+def final_kernel(first0, second0, first1, second1, first2, second2, stats, gain, shift, same, bias, last, out):
+    def rows(frame, start):
+        first, second = frame
+        ref, at = (first, start) if start < FIRST else (second, start - FIRST)
+        return ref[pl.ds(at, 256), :].astype(F32)
+
     total = stats[0]
     for n in range(1, 32):
         total = total + stats[n]
@@ -246,10 +253,10 @@
     bias_row = bias[...].reshape(1, C)
     low = lax.broadcasted_iota(jnp.int32, (256, 128), 1) < 64
     swap = lambda v: pltpu.roll(v, 64, 1)
-    frames = (hidden0, hidden1, hidden2)
+    frames = ((first0, second0), (first1, second1), (first2, second2))
 
     def mix(h, start, tile):
-        v = h[pl.ds(start, 256), :].astype(F32)
+        v = rows(h, start)
         return silu(v * tiles[tile][0] + tiles[tile][1])
 
     for i in range(3):
@@ -258,14 +265,14 @@
             (jnp.where(low, a, swap(b)), jnp.where(low, c, 0.0)),
             (jnp.where(low, swap(a), b), jnp.where(low, swap(c), 0.0)),
         ]
-        rest = hidden1[pl.ds(2 * CELLS + i * 256, 256), :].astype(F32)
+        rest = rows(frames[1], 2 * CELLS + i * 256)
         for n in range(2):
             at = i + 3 * n
             parts = [mix(h, tile * CELLS + at * 256, tile) for h in frames for tile in range(2)]
             taps = jnp.concatenate(parts + list(tails[n]), axis=1).astype(BF)
             moved = (nt(last[...], taps).T + bias_row).astype(BF).astype(F32)
             here = pl.ds(at * 256, 256)
-            h = [hidden1[pl.ds(tile * CELLS + at * 256, 256), :].astype(F32) for tile in range(2)]
+            h = [rows(frames[1], tile * CELLS + at * 256) for tile in range(2)]
             h.append(rest[:, :64] if n == 0 else rest[:, 64:])
             out[here, :] = (moved + jnp.concatenate(h, axis=1)).astype(BF)
 
@@ -299,11 +306,16 @@
     own, cols1 = lax.optimization_barrier((own, cols1))
     other = lax.ppermute(own, "core", [(0, 1), (1, 0)])
 
-    hidden1, stats, w = call(
+    first1, second1, stats, w = call(
         own_kernel,
-        [struct((PACKED, 128), BF), struct((32, 8, 128), F32), struct((C, KPAD), BF)],
+        [
+            struct((FIRST, 128), BF),
+            struct((PACKED - FIRST, 128), BF),
+            struct((32, 8, 128), F32),
+            struct((C, KPAD), BF),
+        ],
         "aaavv",
-        "ava",
+        "aava",
         [
             buffer(*cols),
             buffer(*blocks),
@@ -311,15 +323,17 @@
             buffer(PACKED, 128),
             buffer(4, CPAD, KPAD),
             buffer(4, C, KPAD),
-            sems((5,)),
+            sems((6,)),
         ],
     )(cols1, own, other, emb, const(ORDER))
-    hidden0 = lax.ppermute(hidden1, FRAME, FORWARD)
-    hidden2 = lax.ppermute(hidden1, FRAME, BACKWARD)
+    first0 = lax.ppermute(first1, FRAME, FORWARD)
+    first2 = lax.ppermute(first1, FRAME, BACKWARD)
     stats = lax.all_to_all(stats, FRAME, 0, 0)
+    second0 = lax.ppermute(second1, FRAME, FORWARD)
+    second2 = lax.ppermute(second1, FRAME, BACKWARD)
     (last,) = call(temporal_kernel, [struct((C, KPAD), BF)], "vv", flops=5_000_000_000)(w, const(TEMP_PERM))
-    (out,) = call(final_kernel, [struct((CELLS, C), BF)], "v" * 9)(
-        hidden0, hidden1, hidden2, stats, gain2, shift2, const(SAME1, F32), bias, last
+    (out,) = call(final_kernel, [struct((CELLS, C), BF)], "v" * 12)(
+        first0, second0, first1, second1, first2, second2, stats, gain2, shift2, const(SAME1, F32), bias, last
     )
     return out.reshape(video.shape)
 

time: 122 us -> 121 us (level)
  the two profiles are of different devices: /device:TPU:1 before, /device:TPU:128 now
where the time goes in v6:
time: 121 us; the launch traced here: 120 us
  Pallas kernels  32.6 us (27%)
  starting transfers between devices  31.4 us (26%)
  waiting for transfers between devices  29.6 us (24%)
  blocking collectives  23.6 us (20%)
  local copies, waits for them, and re-layouts  3 us (2%)
    all_to_all x1, blocking collectives, body(): line = lax.all_to_all(pieces, ('zh', 'zl'), 0, 0)  23.6 us
    all_to_all x1, waiting for transfers between devices, body(): own = lax.all_to_all(block, ('y', 'x'), 0, 0)  13.7 us
    pallas_call x1, Pallas kernels, body(): call(own_kernel, [struct((FIRST, 128), BF), struct((PACKED - FIRST, 128),...  10.6 us
    all_to_all x1, starting transfers between devices, body(): stats = lax.all_to_all(stats, FRAME, 0, 0)  9.92 us
    pallas_call x1, Pallas kernels, body(): call(act_kernel, [struct(cols, BF)], 'vvvva', 'a', [buffer(KPAD, KPAD), b...  8.42 us
    ppermute x1, waiting for transfers between devices, body(): first0 = lax.ppermute(first1, FRAME, FORWARD)  7.25 us
    all_to_all x1, starting transfers between devices, body(): own = lax.all_to_all(block, ('y', 'x'), 0, 0)  7.03 us
    pallas_call x1, Pallas kernels, body(): call(final_kernel, [struct((CELLS, C), BF)], 'v' * 12)  6.23 us
  transfers between devices with their start and end apart: 7, of which 4 were waited for; matrix products, arithmetic and copies ran while one was open for 0% of the time, Pallas kernels for 10%

profile of v6, /device:TPU:128, one launch (start us, length us, event | category | flops | bytes accessed | tf_op | source)
XLA Modules:
  0.0 120.3 jit_solution(10899188987295289375)
XLA Ops:
  0.0 1.6 %shard_map.136 = bf16[16,24,128]{2,1,0:T(8,128)(2,1)} custom-call(bf16[3,20,30]{2,1,0:T(8,128)(2,1)} %bitcast.4, bf16[10,3,20]{2,1,0:T(4,128)(2,1)} %bitcast.5), custom_call_target="tpu_custom_call" | custom-call | tf_op jit(solution)/shard_map/pallas_call | solution.py:294
  1.6 23.6 %all_to_all.15.pieces = bf16[16,24,128]{2,1,0:T(8,128)(2,1)} all-to-all(bf16[16,24,128]{2,1,0:T(8,128)(2,1)} %shard_map.136), channel_id=1, replica_groups=mesh['y'=4,'zh'=2,'core'=2,'zl'=8,'x'=4] {'zh','zl'}, dimensions={0} | all-to-all | bytes 196608 | tf_op jit(solution)/shard_map/all_to_all | solution.py:295
  25.1 2.3 %shard_map.137 = bf16[16,48,1024]{2,1,0:T(8,128)(2,1)} custom-call(bf16[16,24,128]{2,1,0:T(8,128)(2,1)} %all_to_all.15.pieces), custom_call_target="tpu_custom_call" | custom-call | tf_op jit(solution)/shard_map/pallas_call | solution.py:296
  27.5 7.0 %all-to-all-start.1 = ((bf16[16,48,1024]{2,1,0:T(8,128)(2,1)}), bf16[16,48,1024]{2,1,0:T(8,128)(2,1)S(1)}, u32[]{:S(2)}, u32[]{:S(2)}) async-start(bf16[16,48,1024]{2,1,0:T(8,128)(2,1)} %shard_map.137), calls=%async_computation.1 | async-start | bytes 3145728 | tf_op jit(solution)/shard_map/all_to_all | solution.py:297
  34.5 8.4 %shard_map.138.cols_hbm = bf16[1664,1024]{1,0:T(8,128)(2,1)} custom-call(bf16[1536,320]{1,0:T(8,128)(2,1)} %bitcast.6, f32[320]{0:T(512)} %gain.2, f32[320]{0:T(512)} %shift.2, f32[320,320]{1,0:T(8,128)} %constant.8.clone.same, bf16[1024,1024]{1,0:T(8,128)(2,1)} %constant.9.clone.perm_hbm), custom_call_target="tpu_custom_call" | custom-call | flops 5000000000 | tf_op jit(solution)/shard_map/pallas_call | solution.py:298
  43.0 13.7 %all-to-all-done.1.own_hbm = bf16[16,48,1024]{2,1,0:T(8,128)(2,1)S(1)} async-done(((bf16[16,48,1024]{2,1,0:T(8,128)(2,1)}), bf16[16,48,1024]{2,1,0:T(8,128)(2,1)S(1)}, u32[]{:S(2)}, u32[]{:S(2)}) %all-to-all-start.1) | async-done | bytes 1572896 | tf_op jit(solution)/shard_map/all_to_all | solution.py:297
  56.7 1.9 %collective-permute-start = (bf16[16,48,1024]{2,1,0:T(8,128)(2,1)S(1)}, bf16[16,48,1024]{2,1,0:T(8,128)(2,1)S(1)}, u32[]{:S(2)}, u32[]{:S(2)}) collective-permute-start(bf16[16,48,1024]{2,1,0:T(8,128)(2,1)S(1)} %all-to-all-done.1.own_hbm), channel_id=1, source_target_pairs={{0,32},{32,0},{1,33},{33,1},{2,34},{34,2},{3,35},{35,3},{4,36},{36... | collective-permute-start | bytes 4718600 | tf_op jit(solution)/shard_map/ppermute | solution.py:307
  58.6 3.4 %collective-permute-done.other_hbm = bf16[16,48,1024]{2,1,0:T(8,128)(2,1)S(1)} collective-permute-done((bf16[16,48,1024]{2,1,0:T(8,128)(2,1)S(1)}, bf16[16,48,1024]{2,1,0:T(8,128)(2,1)S(1)}, u32[]{:S(2)}, u32[]{:S(2)}) %collective-permute-start) | collective-permute-done | bytes 1572896 | tf_op jit(solution)/shard_map/ppermute | solution.py:307
  62.0 1.2 copy-done.1
  63.2 10.6 %shard_map.139 = (bf16[1792,128]{1,0:T(8,128)(2,1)}, bf16[2048,128]{1,0:T(8,128)(2,1)}, f32[32,8,128]{2,1,0:T(8,128)}, bf16[320,1024]{1,0:T(8,128)(2,1)}) custom-call(bf16[1664,1024]{1,0:T(8,128)(2,1)} %shard_map.138.cols_hbm, bf16[16,48,1024]{2,1,0:T(8,128)(2,1)} %copy-done, bf16[16,48,1024]{2,1,0:T(8,128)(2,1)} %copy-done.1, f32[1,1,320]{2,1,0:T(1,128)} %emb.1, ...), custom_call_target="tpu_custom_call" | custom-call | tf_op jit(solution)/shard_map/pallas_call | solution.py:309
  73.8 3.8 %collective-permute-start.4 = (bf16[2048,128]{1,0:T(8,128)(2,1)}, bf16[2048,128]{1,0:T(8,128)(2,1)S(1)}, u32[]{:S(2)}, u32[]{:S(2)}) collective-permute-start(bf16[2048,128]{1,0:T(8,128)(2,1)} %get-tuple-element.14.second1), channel_id=1, source_target_pairs={{1,0},{2,1},{3,2},{4,3},{5,4},{6,5},{7,6},{8,7},{9,8},{10,9},{11,1... | collective-permute-start | bytes 1572872 | tf_op jit(solution)/shard_map/ppermute | solution.py:333
  77.6 2.0 %collective-permute-start.2 = (bf16[2048,128]{1,0:T(8,128)(2,1)}, bf16[2048,128]{1,0:T(8,128)(2,1)S(1)}, u32[]{:S(2)}, u32[]{:S(2)}) collective-permute-start(bf16[2048,128]{1,0:T(8,128)(2,1)} %get-tuple-element.14.second1), channel_id=1, source_target_pairs={{0,1},{1,2},{2,3},{3,4},{4,5},{5,6},{6,7},{7,8},{8,9},{9,10},{10,1... | collective-permute-start | bytes 1572872 | tf_op jit(solution)/shard_map/ppermute | solution.py:332
  79.6 9.9 %all-to-all-start.2 = ((f32[32,8,128]{2,1,0:T(8,128)}), f32[32,8,128]{2,1,0:T(8,128)S(1)}, u32[]{:S(2)}, u32[]{:S(2)}) async-start(f32[32,8,128]{2,1,0:T(8,128)} %get-tuple-element.15), calls=%async_computation.2 | async-start | bytes 262144 | tf_op jit(solution)/shard_map/all_to_all | solution.py:331
  89.6 4.6 %collective-permute-start.3 = (bf16[1792,128]{1,0:T(8,128)(2,1)}, bf16[1792,128]{1,0:T(8,128)(2,1)S(1)}, u32[]{:S(2)}, u32[]{:S(2)}) collective-permute-start(bf16[1792,128]{1,0:T(8,128)(2,1)} %get-tuple-element.13.first1), channel_id=1, source_target_pairs={{1,0},{2,1},{3,2},{4,3},{5,4},{6,5},{7,6},{8,7},{9,8},{10,9},{11,1... | collective-permute-start | bytes 1376264 | tf_op jit(solution)/shard_map/ppermute | solution.py:330
  94.1 2.1 %collective-permute-start.1 = (bf16[1792,128]{1,0:T(8,128)(2,1)}, bf16[1792,128]{1,0:T(8,128)(2,1)S(1)}, u32[]{:S(2)}, u32[]{:S(2)}) collective-permute-start(bf16[1792,128]{1,0:T(8,128)(2,1)} %get-tuple-element.13.first1), channel_id=1, source_target_pairs={{0,1},{1,2},{2,3},{3,4},{4,5},{5,6},{6,7},{7,8},{8,9},{9,10},{10,1... | collective-permute-start | bytes 1376264 | tf_op jit(solution)/shard_map/ppermute | solution.py:329
  96.3 3.5 %shard_map.140.last = bf16[320,1024]{1,0:T(8,128)(2,1)} custom-call(bf16[320,1024]{1,0:T(8,128)(2,1)} %get-tuple-element.16.w, bf16[1024,1024]{1,0:T(8,128)(2,1)} %constant.11.clone.perm), custom_call_target="tpu_custom_call" | custom-call | flops 5000000000 | tf_op jit(solution)/shard_map/pallas_call | solution.py:334
  99.8 5.2 %collective-permute-done.3.first2 = bf16[1792,128]{1,0:T(8,128)(2,1)S(1)} collective-permute-done((bf16[1792,128]{1,0:T(8,128)(2,1)}, bf16[1792,128]{1,0:T(8,128)(2,1)S(1)}, u32[]{:S(2)}, u32[]{:S(2)}) %collective-permute-start.3) | collective-permute-done | bytes 458784 | tf_op jit(solution)/shard_map/ppermute | solution.py:330
  105.0 7.3 %collective-permute-done.1.first0 = bf16[1792,128]{1,0:T(8,128)(2,1)S(1)} collective-permute-done((bf16[1792,128]{1,0:T(8,128)(2,1)}, bf16[1792,128]{1,0:T(8,128)(2,1)S(1)}, u32[]{:S(2)}, u32[]{:S(2)}) %collective-permute-start.1) | collective-permute-done | bytes 458784 | tf_op jit(solution)/shard_map/ppermute | solution.py:329
  112.3 0.0 all-to-all-done.2.stats
  112.3 0.0 collective-permute-done.2.second0
  112.3 0.8 copy-done.6
  113.1 0.2 copy-done.3
  113.3 0.8 copy-done.4
  114.1 6.2 %shard_map.141 = bf16[1536,320]{1,0:T(8,128)(2,1)} custom-call(bf16[1792,128]{1,0:T(8,128)(2,1)} %copy-done.6, bf16[2048,128]{1,0:T(8,128)(2,1)} %copy-done.4, bf16[1792,128]{1,0:T(8,128)(2,1)} %get-tuple-element.13.first1, bf16[2048,128]{1,0:T(8,128)(2,1)} %get-tuple-element.14.second1, bf16[1792,128]{1,0:T(8,128)(2,1)} %copy-done.5, ...), custom_call_target="tpu_custom_call" | custom-call | tf_op jit(solution)/shard_map/pallas_call | solution.py:335
  (11 shorter events, 0.0 us)
Async XLA Ops:
  27.5 29.2 %all-to-all-start.1 = ((bf16[16,48,1024]{2,1,0:T(8,128)(2,1)}), bf16[16,48,1024]{2,1,0:T(8,128)(2,1)S(1)}, u32[]{:S(2)}, u32[]{:S(2)}) async-start(bf16[16,48,1024]{2,1,0:T(8,128)(2,1)} %shard_map.137), calls=%async_computation.1 | async-start | bytes 3145728 | tf_op jit(solution)/shard_map/all_to_all | solution.py:297
  56.7 5.3 %copy-start = (bf16[16,48,1024]{2,1,0:T(8,128)(2,1)}, bf16[16,48,1024]{2,1,0:T(8,128)(2,1)S(1)}, u32[]{:S(2)}) copy-start(bf16[16,48,1024]{2,1,0:T(8,128)(2,1)S(1)} %all-to-all-done.1.own_hbm) | copy-start | bytes 4718596
  56.7 5.3 %collective-permute-start = (bf16[16,48,1024]{2,1,0:T(8,128)(2,1)S(1)}, bf16[16,48,1024]{2,1,0:T(8,128)(2,1)S(1)}, u32[]{:S(2)}, u32[]{:S(2)}) collective-permute-start(bf16[16,48,1024]{2,1,0:T(8,128)(2,1)S(1)} %all-to-all-done.1.own_hbm), channel_id=1, source_target_pairs={{0,32},{32,0},{1,33},{33,1},{2,34},{34,2},{3,35},{35,3},{4,36},{36... | collective-permute-start | bytes 4718600 | tf_op jit(solution)/shard_map/ppermute | solution.py:307
  62.0 1.2 copy-start.1
  73.8 38.5 %collective-permute-start.4 = (bf16[2048,128]{1,0:T(8,128)(2,1)}, bf16[2048,128]{1,0:T(8,128)(2,1)S(1)}, u32[]{:S(2)}, u32[]{:S(2)}) collective-permute-start(bf16[2048,128]{1,0:T(8,128)(2,1)} %get-tuple-element.14.second1), channel_id=1, source_target_pairs={{1,0},{2,1},{3,2},{4,3},{5,4},{6,5},{7,6},{8,7},{9,8},{10,9},{11,1... | collective-permute-start | bytes 1572872 | tf_op jit(solution)/shard_map/ppermute | solution.py:333
  77.6 34.7 %collective-permute-start.2 = (bf16[2048,128]{1,0:T(8,128)(2,1)}, bf16[2048,128]{1,0:T(8,128)(2,1)S(1)}, u32[]{:S(2)}, u32[]{:S(2)}) collective-permute-start(bf16[2048,128]{1,0:T(8,128)(2,1)} %get-tuple-element.14.second1), channel_id=1, source_target_pairs={{0,1},{1,2},{2,3},{3,4},{4,5},{5,6},{6,7},{7,8},{8,9},{9,10},{10,1... | collective-permute-start | bytes 1572872 | tf_op jit(solution)/shard_map/ppermute | solution.py:332
  79.6 32.6 %all-to-all-start.2 = ((f32[32,8,128]{2,1,0:T(8,128)}), f32[32,8,128]{2,1,0:T(8,128)S(1)}, u32[]{:S(2)}, u32[]{:S(2)}) async-start(f32[32,8,128]{2,1,0:T(8,128)} %get-tuple-element.15), calls=%async_computation.2 | async-start | bytes 262144 | tf_op jit(solution)/shard_map/all_to_all | solution.py:331
  89.6 15.4 %collective-permute-start.3 = (bf16[1792,128]{1,0:T(8,128)(2,1)}, bf16[1792,128]{1,0:T(8,128)(2,1)S(1)}, u32[]{:S(2)}, u32[]{:S(2)}) collective-permute-start(bf16[1792,128]{1,0:T(8,128)(2,1)} %get-tuple-element.13.first1), channel_id=1, source_target_pairs={{1,0},{2,1},{3,2},{4,3},{5,4},{6,5},{7,6},{8,7},{9,8},{10,9},{11,1... | collective-permute-start | bytes 1376264 | tf_op jit(solution)/shard_map/ppermute | solution.py:330
  94.1 18.1 %collective-permute-start.1 = (bf16[1792,128]{1,0:T(8,128)(2,1)}, bf16[1792,128]{1,0:T(8,128)(2,1)S(1)}, u32[]{:S(2)}, u32[]{:S(2)}) collective-permute-start(bf16[1792,128]{1,0:T(8,128)(2,1)} %get-tuple-element.13.first1), channel_id=1, source_target_pairs={{0,1},{1,2},{2,3},{3,4},{4,5},{5,6},{6,7},{7,8},{8,9},{9,10},{10,1... | collective-permute-start | bytes 1376264 | tf_op jit(solution)/shard_map/ppermute | solution.py:329
  105.0 7.3 %copy-start.5 = (bf16[1792,128]{1,0:T(8,128)(2,1)}, bf16[1792,128]{1,0:T(8,128)(2,1)S(1)}, u32[]{:S(2)}) copy-start(bf16[1792,128]{1,0:T(8,128)(2,1)S(1)} %collective-permute-done.3.first2) | copy-start | bytes 1376260
  112.3 0.8 copy-start.6
  112.3 0.8 copy-start.2
  112.3 1.0 copy-start.3
  113.3 0.8 copy-start.4

commit v7 on v6

--- a/solution.py
+++ b/solution.py
@@ -19,7 +19,7 @@
 CPAD = 384
 HALF = 192
 PACKED = CELLS * 5 // 2
-FIRST = 1792
+FIRST = 1024
 VMEM = 60 * 1024 * 1024
 
 

time: 121 us -> 122 us (level)
  no operation moved by 1% of the time
where the time goes in v7:
time: 122 us; the launch traced here: 121 us
  Pallas kernels  32.6 us (27%)
  starting transfers between devices  31.4 us (26%)
  waiting for transfers between devices  30.3 us (25%)
  blocking collectives  23.6 us (19%)
  local copies, waits for them, and re-layouts  3.06 us (3%)
    all_to_all x1, blocking collectives, body(): line = lax.all_to_all(pieces, ('zh', 'zl'), 0, 0)  23.6 us
    all_to_all x1, waiting for transfers between devices, body(): own = lax.all_to_all(block, ('y', 'x'), 0, 0)  13.7 us
    pallas_call x1, Pallas kernels, body(): call(own_kernel, [struct((FIRST, 128), BF), struct((PACKED - FIRST, 128),...  10.6 us
    all_to_all x1, starting transfers between devices, body(): stats = lax.all_to_all(stats, FRAME, 0, 0)  9.92 us
    pallas_call x1, Pallas kernels, body(): call(act_kernel, [struct(cols, BF)], 'vvvva', 'a', [buffer(KPAD, KPAD), b...  8.42 us
    ppermute x1, waiting for transfers between devices, body(): first0 = lax.ppermute(first1, FRAME, FORWARD)  7.77 us
    all_to_all x1, starting transfers between devices, body(): own = lax.all_to_all(block, ('y', 'x'), 0, 0)  7.03 us
    pallas_call x1, Pallas kernels, body(): call(final_kernel, [struct((CELLS, C), BF)], 'v' * 12)  6.23 us
  transfers between devices with their start and end apart: 7, of which 4 were waited for; matrix products, arithmetic and copies ran while one was open for 0% of the time, Pallas kernels for 10%

profile of v7, /device:TPU:128, one launch (start us, length us, event | category | flops | bytes accessed | tf_op | source)
XLA Modules:
  0.0 121.1 jit_solution(6016739798862619858)
XLA Ops:
  0.0 1.6 %shard_map.136 = bf16[16,24,128]{2,1,0:T(8,128)(2,1)} custom-call(bf16[3,20,30]{2,1,0:T(8,128)(2,1)} %bitcast.4, bf16[10,3,20]{2,1,0:T(4,128)(2,1)} %bitcast.5), custom_call_target="tpu_custom_call" | custom-call | tf_op jit(solution)/shard_map/pallas_call | solution.py:294
  1.6 23.6 %all_to_all.15.pieces = bf16[16,24,128]{2,1,0:T(8,128)(2,1)} all-to-all(bf16[16,24,128]{2,1,0:T(8,128)(2,1)} %shard_map.136), channel_id=1, replica_groups=mesh['y'=4,'zh'=2,'core'=2,'zl'=8,'x'=4] {'zh','zl'}, dimensions={0} | all-to-all | bytes 196608 | tf_op jit(solution)/shard_map/all_to_all | solution.py:295
  25.1 2.3 %shard_map.137 = bf16[16,48,1024]{2,1,0:T(8,128)(2,1)} custom-call(bf16[16,24,128]{2,1,0:T(8,128)(2,1)} %all_to_all.15.pieces), custom_call_target="tpu_custom_call" | custom-call | tf_op jit(solution)/shard_map/pallas_call | solution.py:296
  27.5 7.0 %all-to-all-start.1 = ((bf16[16,48,1024]{2,1,0:T(8,128)(2,1)}), bf16[16,48,1024]{2,1,0:T(8,128)(2,1)S(1)}, u32[]{:S(2)}, u32[]{:S(2)}) async-start(bf16[16,48,1024]{2,1,0:T(8,128)(2,1)} %shard_map.137), calls=%async_computation.1 | async-start | bytes 3145728 | tf_op jit(solution)/shard_map/all_to_all | solution.py:297
  34.5 8.4 %shard_map.138.cols_hbm = bf16[1664,1024]{1,0:T(8,128)(2,1)} custom-call(bf16[1536,320]{1,0:T(8,128)(2,1)} %bitcast.6, f32[320]{0:T(512)} %gain.2, f32[320]{0:T(512)} %shift.2, f32[320,320]{1,0:T(8,128)} %constant.8.clone.same, bf16[1024,1024]{1,0:T(8,128)(2,1)} %constant.9.clone.perm_hbm), custom_call_target="tpu_custom_call" | custom-call | flops 5000000000 | tf_op jit(solution)/shard_map/pallas_call | solution.py:298
  43.0 13.7 %all-to-all-done.1.own_hbm = bf16[16,48,1024]{2,1,0:T(8,128)(2,1)S(1)} async-done(((bf16[16,48,1024]{2,1,0:T(8,128)(2,1)}), bf16[16,48,1024]{2,1,0:T(8,128)(2,1)S(1)}, u32[]{:S(2)}, u32[]{:S(2)}) %all-to-all-start.1) | async-done | bytes 1572896 | tf_op jit(solution)/shard_map/all_to_all | solution.py:297
  56.7 1.9 %collective-permute-start = (bf16[16,48,1024]{2,1,0:T(8,128)(2,1)S(1)}, bf16[16,48,1024]{2,1,0:T(8,128)(2,1)S(1)}, u32[]{:S(2)}, u32[]{:S(2)}) collective-permute-start(bf16[16,48,1024]{2,1,0:T(8,128)(2,1)S(1)} %all-to-all-done.1.own_hbm), channel_id=1, source_target_pairs={{0,32},{32,0},{1,33},{33,1},{2,34},{34,2},{3,35},{35,3},{4,36},{36... | collective-permute-start | bytes 4718600 | tf_op jit(solution)/shard_map/ppermute | solution.py:307
  58.6 3.4 %collective-permute-done.other_hbm = bf16[16,48,1024]{2,1,0:T(8,128)(2,1)S(1)} collective-permute-done((bf16[16,48,1024]{2,1,0:T(8,128)(2,1)S(1)}, bf16[16,48,1024]{2,1,0:T(8,128)(2,1)S(1)}, u32[]{:S(2)}, u32[]{:S(2)}) %collective-permute-start) | collective-permute-done | bytes 1572896 | tf_op jit(solution)/shard_map/ppermute | solution.py:307
  62.0 1.2 copy-done.1
  63.2 10.6 %shard_map.139 = (bf16[1024,128]{1,0:T(8,128)(2,1)}, bf16[2816,128]{1,0:T(8,128)(2,1)}, f32[32,8,128]{2,1,0:T(8,128)}, bf16[320,1024]{1,0:T(8,128)(2,1)}) custom-call(bf16[1664,1024]{1,0:T(8,128)(2,1)} %shard_map.138.cols_hbm, bf16[16,48,1024]{2,1,0:T(8,128)(2,1)} %copy-done, bf16[16,48,1024]{2,1,0:T(8,128)(2,1)} %copy-done.1, f32[1,1,320]{2,1,0:T(1,128)} %emb.1, ...), custom_call_target="tpu_custom_call" | custom-call | tf_op jit(solution)/shard_map/pallas_call | solution.py:309
  73.8 3.8 %collective-permute-start.4 = (bf16[2816,128]{1,0:T(8,128)(2,1)}, bf16[2816,128]{1,0:T(8,128)(2,1)S(1)}, u32[]{:S(2)}, u32[]{:S(2)}) collective-permute-start(bf16[2816,128]{1,0:T(8,128)(2,1)} %get-tuple-element.14.second1), channel_id=1, source_target_pairs={{1,0},{2,1},{3,2},{4,3},{5,4},{6,5},{7,6},{8,7},{9,8},{10,9},{11,1... | collective-permute-start | bytes 2162696 | tf_op jit(solution)/shard_map/ppermute | solution.py:333
  77.6 2.0 %collective-permute-start.2 = (bf16[2816,128]{1,0:T(8,128)(2,1)}, bf16[2816,128]{1,0:T(8,128)(2,1)S(1)}, u32[]{:S(2)}, u32[]{:S(2)}) collective-permute-start(bf16[2816,128]{1,0:T(8,128)(2,1)} %get-tuple-element.14.second1), channel_id=1, source_target_pairs={{0,1},{1,2},{2,3},{3,4},{4,5},{5,6},{6,7},{7,8},{8,9},{9,10},{10,1... | collective-permute-start | bytes 2162696 | tf_op jit(solution)/shard_map/ppermute | solution.py:332
  79.6 9.9 %all-to-all-start.2 = ((f32[32,8,128]{2,1,0:T(8,128)}), f32[32,8,128]{2,1,0:T(8,128)S(1)}, u32[]{:S(2)}, u32[]{:S(2)}) async-start(f32[32,8,128]{2,1,0:T(8,128)} %get-tuple-element.15), calls=%async_computation.2 | async-start | bytes 262144 | tf_op jit(solution)/shard_map/all_to_all | solution.py:331
  89.6 4.6 %collective-permute-start.3 = (bf16[1024,128]{1,0:T(8,128)(2,1)}, bf16[1024,128]{1,0:T(8,128)(2,1)S(1)}, u32[]{:S(2)}, u32[]{:S(2)}) collective-permute-start(bf16[1024,128]{1,0:T(8,128)(2,1)} %get-tuple-element.13.first1), channel_id=1, source_target_pairs={{1,0},{2,1},{3,2},{4,3},{5,4},{6,5},{7,6},{8,7},{9,8},{10,9},{11,1... | collective-permute-start | bytes 786440 | tf_op jit(solution)/shard_map/ppermute | solution.py:330
  94.1 2.1 %collective-permute-start.1 = (bf16[1024,128]{1,0:T(8,128)(2,1)}, bf16[1024,128]{1,0:T(8,128)(2,1)S(1)}, u32[]{:S(2)}, u32[]{:S(2)}) collective-permute-start(bf16[1024,128]{1,0:T(8,128)(2,1)} %get-tuple-element.13.first1), channel_id=1, source_target_pairs={{0,1},{1,2},{2,3},{3,4},{4,5},{5,6},{6,7},{7,8},{8,9},{9,10},{10,1... | collective-permute-start | bytes 786440 | tf_op jit(solution)/shard_map/ppermute | solution.py:329
  96.3 3.5 %shard_map.140.last = bf16[320,1024]{1,0:T(8,128)(2,1)} custom-call(bf16[320,1024]{1,0:T(8,128)(2,1)} %get-tuple-element.16.w, bf16[1024,1024]{1,0:T(8,128)(2,1)} %constant.11.clone.perm), custom_call_target="tpu_custom_call" | custom-call | flops 5000000000 | tf_op jit(solution)/shard_map/pallas_call | solution.py:334
  99.8 5.4 %collective-permute-done.3.first2 = bf16[1024,128]{1,0:T(8,128)(2,1)S(1)} collective-permute-done((bf16[1024,128]{1,0:T(8,128)(2,1)}, bf16[1024,128]{1,0:T(8,128)(2,1)S(1)}, u32[]{:S(2)}, u32[]{:S(2)}) %collective-permute-start.3) | collective-permute-done | bytes 262176 | tf_op jit(solution)/shard_map/ppermute | solution.py:330
  105.2 7.8 %collective-permute-done.1.first0 = bf16[1024,128]{1,0:T(8,128)(2,1)S(1)} collective-permute-done((bf16[1024,128]{1,0:T(8,128)(2,1)}, bf16[1024,128]{1,0:T(8,128)(2,1)S(1)}, u32[]{:S(2)}, u32[]{:S(2)}) %collective-permute-start.1) | collective-permute-done | bytes 262176 | tf_op jit(solution)/shard_map/ppermute | solution.py:329
  113.0 0.0 all-to-all-done.2.stats
  113.0 0.7 copy-done.6
  113.7 0.0 copy-done.4
  113.7 0.3 copy-done.2
  114.0 0.9 copy-done.3
  114.8 6.2 %shard_map.141 = bf16[1536,320]{1,0:T(8,128)(2,1)} custom-call(bf16[1024,128]{1,0:T(8,128)(2,1)} %copy-done.6, bf16[2816,128]{1,0:T(8,128)(2,1)} %copy-done.3, bf16[1024,128]{1,0:T(8,128)(2,1)} %get-tuple-element.13.first1, bf16[2816,128]{1,0:T(8,128)(2,1)} %get-tuple-element.14.second1, bf16[1024,128]{1,0:T(8,128)(2,1)} %copy-done.5, ...), custom_call_target="tpu_custom_call" | custom-call | tf_op jit(solution)/shard_map/pallas_call | solution.py:335
  (11 shorter events, 0.0 us)
Async XLA Ops:
  27.5 29.2 %all-to-all-start.1 = ((bf16[16,48,1024]{2,1,0:T(8,128)(2,1)}), bf16[16,48,1024]{2,1,0:T(8,128)(2,1)S(1)}, u32[]{:S(2)}, u32[]{:S(2)}) async-start(bf16[16,48,1024]{2,1,0:T(8,128)(2,1)} %shard_map.137), calls=%async_computation.1 | async-start | bytes 3145728 | tf_op jit(solution)/shard_map/all_to_all | solution.py:297
  56.7 5.3 %copy-start = (bf16[16,48,1024]{2,1,0:T(8,128)(2,1)}, bf16[16,48,1024]{2,1,0:T(8,128)(2,1)S(1)}, u32[]{:S(2)}) copy-start(bf16[16,48,1024]{2,1,0:T(8,128)(2,1)S(1)} %all-to-all-done.1.own_hbm) | copy-start | bytes 4718596
  56.7 5.3 %collective-permute-start = (bf16[16,48,1024]{2,1,0:T(8,128)(2,1)S(1)}, bf16[16,48,1024]{2,1,0:T(8,128)(2,1)S(1)}, u32[]{:S(2)}, u32[]{:S(2)}) collective-permute-start(bf16[16,48,1024]{2,1,0:T(8,128)(2,1)S(1)} %all-to-all-done.1.own_hbm), channel_id=1, source_target_pairs={{0,32},{32,0},{1,33},{33,1},{2,34},{34,2},{3,35},{35,3},{4,36},{36... | collective-permute-start | bytes 4718600 | tf_op jit(solution)/shard_map/ppermute | solution.py:307
  62.0 1.2 copy-start.1
  73.8 39.2 %collective-permute-start.4 = (bf16[2816,128]{1,0:T(8,128)(2,1)}, bf16[2816,128]{1,0:T(8,128)(2,1)S(1)}, u32[]{:S(2)}, u32[]{:S(2)}) collective-permute-start(bf16[2816,128]{1,0:T(8,128)(2,1)} %get-tuple-element.14.second1), channel_id=1, source_target_pairs={{1,0},{2,1},{3,2},{4,3},{5,4},{6,5},{7,6},{8,7},{9,8},{10,9},{11,1... | collective-permute-start | bytes 2162696 | tf_op jit(solution)/shard_map/ppermute | solution.py:333
  77.6 35.4 %collective-permute-start.2 = (bf16[2816,128]{1,0:T(8,128)(2,1)}, bf16[2816,128]{1,0:T(8,128)(2,1)S(1)}, u32[]{:S(2)}, u32[]{:S(2)}) collective-permute-start(bf16[2816,128]{1,0:T(8,128)(2,1)} %get-tuple-element.14.second1), channel_id=1, source_target_pairs={{0,1},{1,2},{2,3},{3,4},{4,5},{5,6},{6,7},{7,8},{8,9},{9,10},{10,1... | collective-permute-start | bytes 2162696 | tf_op jit(solution)/shard_map/ppermute | solution.py:332
  79.6 33.3 %all-to-all-start.2 = ((f32[32,8,128]{2,1,0:T(8,128)}), f32[32,8,128]{2,1,0:T(8,128)S(1)}, u32[]{:S(2)}, u32[]{:S(2)}) async-start(f32[32,8,128]{2,1,0:T(8,128)} %get-tuple-element.15), calls=%async_computation.2 | async-start | bytes 262144 | tf_op jit(solution)/shard_map/all_to_all | solution.py:331
  89.6 15.6 %collective-permute-start.3 = (bf16[1024,128]{1,0:T(8,128)(2,1)}, bf16[1024,128]{1,0:T(8,128)(2,1)S(1)}, u32[]{:S(2)}, u32[]{:S(2)}) collective-permute-start(bf16[1024,128]{1,0:T(8,128)(2,1)} %get-tuple-element.13.first1), channel_id=1, source_target_pairs={{1,0},{2,1},{3,2},{4,3},{5,4},{6,5},{7,6},{8,7},{9,8},{10,9},{11,1... | collective-permute-start | bytes 786440 | tf_op jit(solution)/shard_map/ppermute | solution.py:330
  94.1 18.8 %collective-permute-start.1 = (bf16[1024,128]{1,0:T(8,128)(2,1)}, bf16[1024,128]{1,0:T(8,128)(2,1)S(1)}, u32[]{:S(2)}, u32[]{:S(2)}) collective-permute-start(bf16[1024,128]{1,0:T(8,128)(2,1)} %get-tuple-element.13.first1), channel_id=1, source_target_pairs={{0,1},{1,2},{2,3},{3,4},{4,5},{5,6},{6,7},{7,8},{8,9},{9,10},{10,1... | collective-permute-start | bytes 786440 | tf_op jit(solution)/shard_map/ppermute | solution.py:329
  105.2 7.8 %copy-start.5 = (bf16[1024,128]{1,0:T(8,128)(2,1)}, bf16[1024,128]{1,0:T(8,128)(2,1)S(1)}, u32[]{:S(2)}) copy-start(bf16[1024,128]{1,0:T(8,128)(2,1)S(1)} %collective-permute-done.3.first2) | copy-start | bytes 786436
  113.0 0.7 copy-start.6
  113.0 0.8 copy-start.4
  113.0 1.0 copy-start.2
  114.0 0.9 copy-start.3
